TPU v7x, 512 devices: a whole 4x4x16 slice. The times are simulated.
512 devices in a mesh: seq: 64 (over x_hi, z, core), tp: 8 (over x_lo, y).
Axes of the slice: x: 4 (x_hi: 2, x_lo: 2; x = x_hi * 2 + x_lo), y: 4, z: 16, core: 2. Of those that a mesh axis runs over, the one named last changes fastest.
Arguments:
- queries: bfloat16 [8192, 8192], P('seq', 'tp'), may hold values from -6 to 6
- keys: bfloat16 [8192, 8192], P('seq', 'tp'), may hold values from -6 to 6
- values: bfloat16 [8192, 8192], P('seq', 'tp'), may hold values from -6 to 6
- short_taps: float32 [3, 3, 8192], P(None, None, 'tp'), may hold values from -3 to 3
- long_filter: float32 [8192, 8192], P(('tp', 'seq')), may hold values from -8 to 8
- out_weight: bfloat16 [8192, 4096], P('seq', 'tp'), may hold values from -0.0625 to 0.0625
- cotangent: bfloat16 [8192, 4096], P('seq', 'tp'), may hold values from -6 to 6
Outputs:
- mixed: bfloat16 [8192, 4096], P('seq', 'tp')
- query_grad: bfloat16 [8192, 8192], P('seq', 'tp')
- key_grad: bfloat16 [8192, 8192], P('seq', 'tp')
- value_grad: bfloat16 [8192, 8192], P('seq', 'tp')
- filter_grad: float32 [8192, 8192], P(('tp', 'seq'))
All inputs are finite; a program needn't handle non-finite values.
Results may differ from a plain program's by a relative error of at most 0.023.
Values may be sent and summed in bfloat16 or wider, within the bound.
No kernel may reach another device: no remote copies, remote signals or barrier semaphores. Data moves between devices by JAX's collectives and lax.ppermute only.
A program may use at most 64 MiB of HBM per device.

v0:
```python
import functools
import math

import jax
import jax.numpy as jnp
import numpy as np
from jax import lax
from jax.experimental import pallas as pl
from jax.experimental.pallas import tpu as pltpu
from jax.sharding import Mesh
from jax.sharding import PartitionSpec as P

BF16 = jnp.bfloat16
F32 = jnp.float32

SEQ = ("xh", "z", "co")
TP = ("xl", "y")
PLANE = ("xh", "y")
COLUMN = ("z", "co")

CHANNELS = 16
BLOCKS = 64
LANES = 128
LENGTH = BLOCKS * LANES


def transform_tables():
    blocks = np.arange(BLOCKS)
    lanes = np.arange(LANES)
    first = 2.0 * np.pi * np.outer(blocks + 0.25, blocks) / BLOCKS
    twist = 2.0 * np.pi * np.outer(blocks + 0.25, lanes) / LENGTH
    second = 2.0 * np.pi * (np.outer(lanes, lanes) % LANES) / LANES
    first_table = np.concatenate([np.cos(first), -np.sin(first)], axis=0)
    cosine, sine = np.cos(second), np.sin(second)
    second_table = np.block([[cosine, -sine], [sine, cosine]])
    return (
        jnp.asarray(first_table, BF16),
        jnp.asarray(first_table.T / LENGTH, BF16),
        jnp.asarray(np.cos(twist), F32),
        jnp.asarray(np.sin(twist), F32),
        jnp.asarray(second_table, BF16),
        jnp.asarray(second_table.T, BF16),
    )


def to_spectrum(grid_ref, turned_ref, first, cos_twist, sin_twist, second):
    for c in range(CHANNELS):
        grid = grid_ref[pl.ds(c, BLOCKS, stride=CHANNELS), :].astype(BF16)
        section = jnp.dot(first, grid, preferred_element_type=F32)
        real, imag = section[:BLOCKS], section[BLOCKS:]
        rows = slice(c * BLOCKS, (c + 1) * BLOCKS)
        turned_ref[rows, :LANES] = (real * cos_twist + imag * sin_twist).astype(BF16)
        turned_ref[rows, LANES:] = (imag * cos_twist - real * sin_twist).astype(BF16)
    return jnp.dot(turned_ref[...], second, preferred_element_type=F32)


def from_spectrum(spectrum, grid_ref, section_ref, first_back, cos_twist, sin_twist, second_back):
    section_ref[...] = jnp.dot(spectrum, second_back, preferred_element_type=F32)
    for c in range(CHANNELS):
        rows = slice(c * BLOCKS, (c + 1) * BLOCKS)
        real, imag = section_ref[rows, :LANES], section_ref[rows, LANES:]
        turned = jnp.concatenate(
            [real * cos_twist - imag * sin_twist, imag * cos_twist + real * sin_twist], axis=0
        ).astype(BF16)
        grid_ref[pl.ds(c, BLOCKS, stride=CHANNELS), :] = jnp.dot(
            first_back, turned, preferred_element_type=F32
        )


def filter_kernel(filter_ref, first, cos_twist, sin_twist, second, spectrum_ref, grid, turned):
    for b in range(BLOCKS):
        grid[b * CHANNELS : (b + 1) * CHANNELS, :] = filter_ref[:, b * LANES : (b + 1) * LANES]
    spectrum_ref[...] = to_spectrum(
        grid, turned, first[...], cos_twist[...], sin_twist[...], second[...]
    )


def forward_kernel(
    product_ref, filter_spectrum, first, first_back, cos_twist, sin_twist, second, second_back,
    long_ref, product_spectrum, grid, turned, section,
):
    grid[...] = product_ref[...].astype(F32).reshape(BLOCKS * CHANNELS, LANES)
    own = to_spectrum(grid, turned, first[...], cos_twist[...], sin_twist[...], second[...])
    product_spectrum[...] = own
    own_re, own_im = own[:, :LANES], own[:, LANES:]
    other_re, other_im = filter_spectrum[:, :LANES], filter_spectrum[:, LANES:]
    turned[:, :LANES] = (own_re * other_re - own_im * other_im).astype(BF16)
    turned[:, LANES:] = (own_re * other_im + own_im * other_re).astype(BF16)
    from_spectrum(
        turned[...], grid, section, first_back[...], cos_twist[...], sin_twist[...], second_back[...]
    )
    long_ref[...] = grid[...].reshape(BLOCKS, CHANNELS, LANES).astype(BF16)


def backward_kernel(
    grad_ref, filter_spectrum, product_spectrum,
    first, first_back, cos_twist, sin_twist, second, second_back,
    back_ref, filter_grad_ref, grid, turned, section,
):
    grid[...] = grad_ref[...].astype(F32).reshape(BLOCKS * CHANNELS, LANES)
    own = to_spectrum(grid, turned, first[...], cos_twist[...], sin_twist[...], second[...])
    own_re, own_im = own[:, :LANES], own[:, LANES:]

    def correlate(other):
        other_re, other_im = other[:, :LANES], other[:, LANES:]
        turned[:, :LANES] = (own_re * other_re + own_im * other_im).astype(BF16)
        turned[:, LANES:] = (own_im * other_re - own_re * other_im).astype(BF16)
        from_spectrum(
            turned[...], grid, section, first_back[...], cos_twist[...], sin_twist[...], second_back[...]
        )

    correlate(filter_spectrum)
    back_ref[...] = grid[...].reshape(BLOCKS, CHANNELS, LANES).astype(BF16)
    correlate(product_spectrum)
    for b in range(BLOCKS):
        filter_grad_ref[:, b * LANES : (b + 1) * LANES] = grid[
            b * CHANNELS : (b + 1) * CHANNELS, :
        ] * (1.0 / math.sqrt(LENGTH))


SPECTRUM = jax.ShapeDtypeStruct((CHANNELS * BLOCKS, 2 * LANES), F32)
SEQUENCES = jax.ShapeDtypeStruct((BLOCKS, CHANNELS, LANES), BF16)
GRID = pltpu.VMEM((BLOCKS * CHANNELS, LANES), F32)
TURNED = pltpu.VMEM((CHANNELS * BLOCKS, 2 * LANES), BF16)
SECTION = pltpu.VMEM((CHANNELS * BLOCKS, 2 * LANES), F32)


def run_kernel(kernel, out_shape, scratch, transforms, *operands):
    transform_flops = 2 * CHANNELS * BLOCKS * LANES * (2 * BLOCKS + 4 * LANES)
    return pl.pallas_call(
        kernel,
        out_shape=out_shape,
        scratch_shapes=scratch,
        compiler_params=pltpu.CompilerParams(vmem_limit_bytes=40 * 2**20),
        cost_estimate=pl.CostEstimate(
            flops=transforms * transform_flops, bytes_accessed=4 * 2**20, transcendentals=0
        ),
    )(*operands)


def shift(value, steps):
    count = 1
    for axis in SEQ:
        count *= lax.axis_size(axis)
    first, last = max(0, -steps), min(count, count - steps)
    return lax.ppermute(value, SEQ, [(i, i + steps) for i in range(first, last)])


def across(value, target):
    pairs = [(2 * a + b, 2 * target(a, b)[0] + target(a, b)[1]) for a in range(2) for b in range(2)]
    return lax.ppermute(value, ("xh", "xl"), pairs)


def per_device(queries, keys, values, short_taps, long_filter, out_weight, cotangent):
    rows, width = queries.shape
    taps = short_taps.shape[1]
    rim = taps - 1
    features = out_weight.shape[1]
    half = lax.axis_index("xl")

    weight = lax.all_gather(
        across(out_weight, lambda a, b: (b, a)), COLUMN, axis=0, tiled=True
    ).reshape(4, width, features)
    near = across(cotangent, lambda a, b: (b, a))
    far = across(cotangent, lambda a, b: (b, 1 - a))
    gradient = jnp.where(half == 0, jnp.stack([near, far]), jnp.stack([far, near]))

    first, first_back, cos_twist, sin_twist, second, second_back = transform_tables()
    filter_spectrum = run_kernel(
        filter_kernel, SPECTRUM, [GRID, TURNED], 1, long_filter, first, cos_twist, sin_twist, second
    )

    stacked = jnp.stack([queries, keys, values])
    before = shift(stacked[:, rows - rim :], 1)
    extended = jnp.concatenate([before, stacked], axis=1).astype(F32)
    filtered = jnp.zeros(stacked.shape, F32)
    for tap in range(taps):
        start = rim - tap
        filtered = filtered + short_taps[:, tap][:, None, :] * extended[:, start : start + rows]
    query_conv, key_conv, value_conv = filtered[0], filtered[1], filtered[2]
    product = (key_conv * value_conv).astype(BF16)

    product_owned = lax.all_to_all(product.T.reshape(BLOCKS, CHANNELS, LANES), SEQ, 0, 0, tiled=True)
    long_owned, product_spectrum = run_kernel(
        forward_kernel, [SEQUENCES, SPECTRUM], [GRID, TURNED, SECTION], 2,
        product_owned, filter_spectrum, first, first_back, cos_twist, sin_twist, second, second_back,
    )
    long_out = lax.all_to_all(long_owned, SEQ, 0, 0, tiled=True).reshape(width, rows).T
    long_float = long_out.astype(F32)
    gated = (query_conv * long_float).astype(BF16)

    partial = jnp.einsum(
        "tmk,ynk->tymn", gradient, weight, preferred_element_type=F32
    ).astype(BF16)
    partial = partial.reshape(8, rows, width)
    gated_grad = jnp.sum(lax.all_to_all(partial, PLANE, 0, 0, tiled=True).astype(F32), axis=0)

    long_grad = (query_conv * gated_grad).astype(BF16)
    query_conv_grad = gated_grad * long_float
    grad_owned = lax.all_to_all(long_grad.T.reshape(BLOCKS, CHANNELS, LANES), SEQ, 0, 0, tiled=True)
    back_owned, filter_grad = run_kernel(
        backward_kernel,
        [SEQUENCES, jax.ShapeDtypeStruct((CHANNELS, LENGTH), F32)],
        [GRID, TURNED, SECTION], 3,
        grad_owned, filter_spectrum, product_spectrum,
        first, first_back, cos_twist, sin_twist, second, second_back,
    )

    gated_all = lax.all_gather(gated, PLANE, axis=0).reshape(2, 4, rows, width)
    share = jnp.einsum("tymn,ynk->tmk", gated_all, weight, preferred_element_type=F32).astype(BF16)
    mine = jnp.where(half == 0, share[0], share[1])
    other = jnp.where(half == 0, share[1], share[0])
    mixed = (
        across(mine, lambda a, b: (b, a)).astype(F32)
        + across(other, lambda a, b: (1 - b, a)).astype(F32)
    ).astype(BF16)

    product_grad = lax.all_to_all(back_owned, SEQ, 0, 0, tiled=True).reshape(width, rows).T
    product_float = product_grad.astype(F32)
    grads = jnp.stack([query_conv_grad, product_float * value_conv, product_float * key_conv])
    after = shift(grads[:, :rim], -1)
    grads = jnp.concatenate([grads, after], axis=1)
    incoming = jnp.zeros(stacked.shape, F32)
    for tap in range(taps):
        incoming = incoming + short_taps[:, tap][:, None, :] * grads[:, tap : tap + rows]
    incoming = incoming.astype(BF16)
    return (mixed, incoming[0], incoming[1], incoming[2], filter_grad)


def solution(mesh):
    fine = Mesh(mesh.devices.reshape(2, 16, 2, 2, 4), ("xh", "z", "co", "xl", "y"))
    token = P(SEQ, TP)
    in_specs = (token, token, token, P(None, None, TP), P(TP + SEQ, None), token, token)
    out_specs = (token, token, token, token, P(TP + SEQ, None))
    return jax.shard_map(
        per_device, mesh=fine, in_specs=in_specs, out_specs=out_specs, check_vma=False
    )
```

profile of v0, /device:TPU:1, one launch (start us, length us, event | category | flops | bytes accessed | tf_op | source)
XLA Modules:
  0.0 335.4 jit_solution(684575707519263882)
XLA Ops:
  7.2 0.0 all-gather.4.cloned.1.call-start
  7.2 1.6 collective-permute-start.1
  8.8 0.7 copy-done.15
  9.4 0.0 all-gather.4.cloned.1.call-update
  9.5 8.9 %collective-permute-start.5 = (bf16[128,512]{1,0:T(8,128)(2,1)}, bf16[128,512]{1,0:T(8,128)(2,1)S(1)}, u32[]{:S(2)}, u32[]{:S(2)}) collective-permute-start(bf16[128,512]{1,0:T(8,128)(2,1)} %param.19), channel_id=1, source_target_pairs={{0,4},{4,260},{256,0},{260,256},{1,5},{5,261},{257,1},{261,257},{2... | collective-permute-start | bytes 393224 | tf_op jit(solution)/shard_map/ppermute | solution.py:151
  18.3 1.6 collective-permute-start.4
  19.9 2.5 collective-permute-done.5
  22.4 72.5 %all-gather.4.cloned.1.call-done = bf16[4096,512]{1,0:T(8,128)(2,1)} async-done(((bf16[128,512]{1,0:T(8,128)(2,1)}), bf16[4096,512]{1,0:T(8,128)(2,1)}) %all-gather.4.cloned.1.call-update) | async-done | bytes 4194320 | tf_op jit(solution)/shard_map/all_gather | solution.py:161
  94.9 4.9 %convolution_convert_fusion = bf16[2,128,4,1024]{3,1,2,0:T(8,128)(2,1)} fusion(bf16[4,1024,512,1]{2,1,0,3:T(8,128)(2,1)} %bitcast.98, bf16[1,128,512]{2,1,0:T(8,128)(2,1)S(1)} %bitcast.108, bf16[1,128,512]{2,1,0:T(8,128)(2,1)S(1)} %bitcast.109, pred[]{:T(512)S(6)} %eq.2), kind=kOutput, calls=%fused_computation.1 | convolution fusion | flops 1075970048 | bytes 6553601 | tf_op jit(solution)/shard_map/tmk,ynk->tymn/dot_general | solution.py:192
  99.8 6.9 %all-to-all-start.2 = ((bf16[8,128,1024]{2,1,0:T(8,128)(2,1)}), bf16[8,128,1024]{2,1,0:T(8,128)(2,1)}, u32[]{:S(2)}, u32[]{:S(2)}) async-start(bf16[8,128,1024]{2,1,0:T(8,128)(2,1)} %bitcast.23), calls=%async_computation.2 | async-start | bytes 4194304 | tf_op jit(solution)/shard_map/all_to_all | solution.py:196
  106.7 3.5 %collective-permute-start = (bf16[3,2,1024]{2,1,0:T(2,128)(2,1)S(1)}, bf16[3,2,1024]{2,1,0:T(2,128)(2,1)S(1)}, u32[]{:S(2)}, u32[]{:S(2)}) collective-permute-start(bf16[3,2,1024]{2,1,0:T(2,128)(2,1)S(1)} %pad_maximum_fusion.2), channel_id=1, source_target_pairs={{0,8},{8,16},{16,24},{24,32},{32,40},{40,48},{48,56},{56,64},{64,7... | collective-permute-start | bytes 36872 | tf_op jit(solution)/shard_map/ppermute | solution.py:146
  110.3 0.7 collective-permute-done
  111.0 0.2 maximum_convert_fusion
  111.2 0.5 fusion.3
  111.7 21.2 %all-to-all-done.2 = bf16[8,128,1024]{2,1,0:T(8,128)(2,1)} async-done(((bf16[8,128,1024]{2,1,0:T(8,128)(2,1)}), bf16[8,128,1024]{2,1,0:T(8,128)(2,1)}, u32[]{:S(2)}, u32[]{:S(2)}) %all-to-all-start.2) | async-done | bytes 2097184 | tf_op jit(solution)/shard_map/all_to_all | solution.py:196
  133.0 2.0 convert_reduce_fusion
  135.0 0.2 fusion.11
  135.2 0.6 copy-done.9
  135.8 0.8 copy.22
  136.6 11.5 %all-to-all-start = ((bf16[64,16,128]{2,1,0:T(8,128)(2,1)}), bf16[64,16,128]{2,1,0:T(8,128)(2,1)S(1)}, u32[]{:S(2)}, u32[]{:S(2)}) async-start(bf16[64,16,128]{2,1,0:T(8,128)(2,1)} %bitcast.7), calls=%async_computation | async-start | bytes 524288 | tf_op jit(solution)/shard_map/all_to_all | solution.py:183
  148.2 0.8 copy.24
  149.0 22.9 %all-to-all-done.product_ref = bf16[64,16,128]{2,1,0:T(8,128)(2,1)S(1)} async-done(((bf16[64,16,128]{2,1,0:T(8,128)(2,1)}), bf16[64,16,128]{2,1,0:T(8,128)(2,1)S(1)}, u32[]{:S(2)}, u32[]{:S(2)}) %all-to-all-start) | async-done | bytes 262176 | tf_op jit(solution)/shard_map/all_to_all | solution.py:183
  171.9 4.2 %all-to-all-start.3 = ((bf16[64,16,128]{2,1,0:T(8,128)(2,1)}), bf16[64,16,128]{2,1,0:T(8,128)(2,1)S(1)}, u32[]{:S(2)}, u32[]{:S(2)}) async-start(bf16[64,16,128]{2,1,0:T(8,128)(2,1)} %bitcast.26), calls=%async_computation.3 | async-start | bytes 524288 | tf_op jit(solution)/shard_map/all_to_all | solution.py:200
  176.2 0.6 shard_map.164.filter_spectrum
  176.7 1.8 shard_map.165
  178.5 21.2 %all-to-all-done.3.grad_ref = bf16[64,16,128]{2,1,0:T(8,128)(2,1)S(1)} async-done(((bf16[64,16,128]{2,1,0:T(8,128)(2,1)}), bf16[64,16,128]{2,1,0:T(8,128)(2,1)S(1)}, u32[]{:S(2)}, u32[]{:S(2)}) %all-to-all-start.3) | async-done | bytes 262176 | tf_op jit(solution)/shard_map/all_to_all | solution.py:200
  199.7 2.5 shard_map.166
  202.2 27.6 %all_to_all.25 = bf16[64,16,128]{2,1,0:T(8,128)(2,1)S(1)} all-to-all(bf16[64,16,128]{2,1,0:T(8,128)(2,1)S(1)} %get-tuple-element.11), channel_id=1, replica_groups=mesh['xh'=2,'z'=16,'co'=2,'xl'=2,'y'=4] {'xh','z','co'}, dimensions={0} | all-to-all | bytes 524288 | tf_op jit(solution)/shard_map/all_to_all | solution.py:218
  229.8 4.2 %all-to-all-start.1 = ((bf16[64,16,128]{2,1,0:T(8,128)(2,1)}), bf16[64,16,128]{2,1,0:T(8,128)(2,1)S(1)}, u32[]{:S(2)}, u32[]{:S(2)}) async-start(bf16[64,16,128]{2,1,0:T(8,128)(2,1)} %get-tuple-element.9), calls=%async_computation.1 | async-start | bytes 524288 | tf_op jit(solution)/shard_map/all_to_all | solution.py:188
  234.0 0.0 all-gather.6.cloned.1.call-start
  234.0 0.1 bitcast_convert_fusion
  234.1 1.0 copy.25
  235.1 22.5 %all-to-all-done.1 = bf16[64,16,128]{2,1,0:T(8,128)(2,1)S(1)} async-done(((bf16[64,16,128]{2,1,0:T(8,128)(2,1)}), bf16[64,16,128]{2,1,0:T(8,128)(2,1)S(1)}, u32[]{:S(2)}, u32[]{:S(2)}) %all-to-all-start.1) | async-done | bytes 262176 | tf_op jit(solution)/shard_map/all_to_all | solution.py:188
  257.6 0.1 bitcast_convert_fusion.1
  257.6 1.0 copy.23
  258.7 2.3 fusion.6
  261.0 0.2 pad_maximum_fusion.1
  261.2 1.9 collective-permute-start.6
  263.2 3.2 collective-permute-done.6
  266.4 0.2 pad_maximum_fusion
  266.6 0.5 fusion.1
  267.1 51.0 %all-gather.6.cloned.1.call-done = bf16[1024,1024]{1,0:T(8,128)(2,1)} async-done(((bf16[128,1024]{1,0:T(8,128)(2,1)}), bf16[1024,1024]{1,0:T(8,128)(2,1)}) %all-gather.6.cloned.1.call-update) | async-done | bytes 2097168 | tf_op jit(solution)/shard_map/all_gather | solution.py:209
  318.1 4.1 %fusion.5 = bf16[2,128,512]{2,1,0:T(8,128)(2,1)S(1)} fusion(bf16[2,4,128,1024]{3,2,1,0:T(8,128)(2,1)} %bitcast.110, bf16[4,1024,512,1]{2,1,0,3:T(8,128)(2,1)} %bitcast.99), kind=kOutput, calls=%fused_computation.15 | convolution fusion | flops 1073872896 | bytes 6553600 | tf_op jit(solution)/shard_map/tymn,ynk->tmk/dot_general | solution.py:210
  322.2 2.2 collective-permute-start.3
  324.4 0.7 collective-permute-start.2
  325.1 0.9 slice_bitcast_fusion.3
  325.9 2.0 collective-permute-done.3
  327.9 0.7 add_convert_fusion
  (42 shorter events, 0.2 us)
Async XLA Ops:
  7.2 87.7 %all-gather.4.cloned.1.call-start = ((), (), s32[]{:S(2)}) async-start(), calls=%async_computation.5 | async-start | bytes 4325376 | tf_op jit(solution)/shard_map/all_gather | solution.py:161
  7.2 1.6 collective-permute-start.1
  8.8 0.7 copy-start.15
  9.5 12.9 %collective-permute-start.5 = (bf16[128,512]{1,0:T(8,128)(2,1)}, bf16[128,512]{1,0:T(8,128)(2,1)S(1)}, u32[]{:S(2)}, u32[]{:S(2)}) collective-permute-start(bf16[128,512]{1,0:T(8,128)(2,1)} %param.19), channel_id=1, source_target_pairs={{0,4},{4,260},{256,0},{260,256},{1,5},{5,261},{257,1},{261,257},{2... | collective-permute-start | bytes 393224 | tf_op jit(solution)/shard_map/ppermute | solution.py:151
  18.3 4.1 %collective-permute-start.4 = (bf16[128,512]{1,0:T(8,128)(2,1)}, bf16[128,512]{1,0:T(8,128)(2,1)S(1)}, u32[]{:S(2)}, u32[]{:S(2)}) collective-permute-start(bf16[128,512]{1,0:T(8,128)(2,1)} %param.19), channel_id=1, source_target_pairs={{0,0},{4,256},{256,4},{260,260},{1,1},{5,257},{257,5},{261,261},{2... | collective-permute-start | bytes 393224 | tf_op jit(solution)/shard_map/ppermute | solution.py:151
  99.8 6.9 %copy-start.10 = (bf16[128,1024]{1,0:T(8,128)(2,1)S(1)}, bf16[128,1024]{1,0:T(8,128)(2,1)}, u32[]{:S(2)}) copy-start(bf16[128,1024]{1,0:T(8,128)(2,1)} %param.15) | copy-start | bytes 786436
  99.8 6.9 %copy-start.11 = (bf16[128,1024]{1,0:T(8,128)(2,1)S(1)}, bf16[128,1024]{1,0:T(8,128)(2,1)}, u32[]{:S(2)}) copy-start(bf16[128,1024]{1,0:T(8,128)(2,1)} %param.14) | copy-start | bytes 786436
  99.8 6.9 %copy-start.12 = (bf16[128,1024]{1,0:T(8,128)(2,1)S(1)}, bf16[128,1024]{1,0:T(8,128)(2,1)}, u32[]{:S(2)}) copy-start(bf16[128,1024]{1,0:T(8,128)(2,1)} %param.13) | copy-start | bytes 786436
  99.8 10.4 %copy-start.16 = (f32[3,3,1024]{2,1,0:T(4,128)S(1)}, f32[3,3,1024]{2,1,0:T(4,128)}, u32[]{:S(2)}) copy-start(f32[3,3,1024]{2,1,0:T(4,128)} %param.16) | copy-start | bytes 110596
  99.8 33.2 %all-to-all-start.2 = ((bf16[8,128,1024]{2,1,0:T(8,128)(2,1)}), bf16[8,128,1024]{2,1,0:T(8,128)(2,1)}, u32[]{:S(2)}, u32[]{:S(2)}) async-start(bf16[8,128,1024]{2,1,0:T(8,128)(2,1)} %bitcast.23), calls=%async_computation.2 | async-start | bytes 4194304 | tf_op jit(solution)/shard_map/all_to_all | solution.py:196
  106.7 4.3 %collective-permute-start = (bf16[3,2,1024]{2,1,0:T(2,128)(2,1)S(1)}, bf16[3,2,1024]{2,1,0:T(2,128)(2,1)S(1)}, u32[]{:S(2)}, u32[]{:S(2)}) collective-permute-start(bf16[3,2,1024]{2,1,0:T(2,128)(2,1)S(1)} %pad_maximum_fusion.2), channel_id=1, source_target_pairs={{0,8},{8,16},{16,24},{24,32},{32,40},{40,48},{48,56},{56,64},{64,7... | collective-permute-start | bytes 36872 | tf_op jit(solution)/shard_map/ppermute | solution.py:146
  110.3 1.5 copy-start.13
  111.7 23.3 %copy-start.7 = (f32[3,128,1024]{2,1,0:T(8,128)}, f32[3,128,1024]{2,1,0:T(8,128)S(1)}, u32[]{:S(2)}) copy-start(f32[3,128,1024]{2,1,0:T(8,128)S(1)} %fusion.3) | copy-start | bytes 4718596
  135.0 0.8 copy-start.9
  135.8 40.3 %copy-start = (bf16[256,256]{1,0:T(8,128)(2,1)S(1)}, bf16[256,256]{1,0:T(8,128)(2,1)}, u32[]{:S(2)}) copy-start(bf16[256,256]{1,0:T(8,128)(2,1)} %constant.26.clone.second) | copy-start | bytes 393220
  135.8 40.4 %copy-start.1 = (f32[16,8192]{1,0:T(8,128)S(1)}, f32[16,8192]{1,0:T(8,128)}, u32[]{:S(2)}) copy-start(f32[16,8192]{1,0:T(8,128)} %filter_ref.1) | copy-start | bytes 1572868
  135.8 40.4 %copy-start.3 = (bf16[128,64]{1,0:T(8,128)(2,1)S(1)}, bf16[128,64]{1,0:T(8,128)(2,1)}, u32[]{:S(2)}) copy-start(bf16[128,64]{1,0:T(8,128)(2,1)} %constant.22.clone.first) | copy-start | bytes 49156
  135.8 40.4 %copy-start.4 = (f32[64,128]{1,0:T(8,128)S(1)}, f32[64,128]{1,0:T(8,128)}, u32[]{:S(2)}) copy-start(f32[64,128]{1,0:T(8,128)} %constant.24.clone.cos_twist) | copy-start | bytes 98308
  135.8 40.4 %copy-start.5 = (f32[64,128]{1,0:T(8,128)S(1)}, f32[64,128]{1,0:T(8,128)}, u32[]{:S(2)}) copy-start(f32[64,128]{1,0:T(8,128)} %constant.25.clone.sin_twist) | copy-start | bytes 98308
  136.6 40.1 %copy-start.2 = (bf16[256,256]{1,0:T(8,128)(2,1)S(1)}, bf16[256,256]{1,0:T(8,128)(2,1)}, u32[]{:S(2)}) copy-start(bf16[256,256]{1,0:T(8,128)(2,1)} %constant.27.clone.second_back) | copy-start | bytes 393220
  136.6 40.1 %copy-start.6 = (bf16[64,128]{1,0:T(8,128)(2,1)S(1)}, bf16[64,128]{1,0:T(8,128)(2,1)}, u32[]{:S(2)}) copy-start(bf16[64,128]{1,0:T(8,128)(2,1)} %constant.23.clone.first_back) | copy-start | bytes 49156
  136.6 35.3 %all-to-all-start = ((bf16[64,16,128]{2,1,0:T(8,128)(2,1)}), bf16[64,16,128]{2,1,0:T(8,128)(2,1)S(1)}, u32[]{:S(2)}, u32[]{:S(2)}) async-start(bf16[64,16,128]{2,1,0:T(8,128)(2,1)} %bitcast.7), calls=%async_computation | async-start | bytes 524288 | tf_op jit(solution)/shard_map/all_to_all | solution.py:183
  171.9 27.8 %all-to-all-start.3 = ((bf16[64,16,128]{2,1,0:T(8,128)(2,1)}), bf16[64,16,128]{2,1,0:T(8,128)(2,1)S(1)}, u32[]{:S(2)}, u32[]{:S(2)}) async-start(bf16[64,16,128]{2,1,0:T(8,128)(2,1)} %bitcast.26), calls=%async_computation.3 | async-start | bytes 524288 | tf_op jit(solution)/shard_map/all_to_all | solution.py:200
  229.8 27.8 %all-to-all-start.1 = ((bf16[64,16,128]{2,1,0:T(8,128)(2,1)}), bf16[64,16,128]{2,1,0:T(8,128)(2,1)S(1)}, u32[]{:S(2)}, u32[]{:S(2)}) async-start(bf16[64,16,128]{2,1,0:T(8,128)(2,1)} %get-tuple-element.9), calls=%async_computation.1 | async-start | bytes 524288 | tf_op jit(solution)/shard_map/all_to_all | solution.py:188
  234.0 24.7 %copy-start.8 = (f32[3,128,1024]{2,1,0:T(8,128)S(1)}, f32[3,128,1024]{2,1,0:T(8,128)}, u32[]{:S(2)}) copy-start(f32[3,128,1024]{2,1,0:T(8,128)} %copy-done.7) | copy-start | bytes 4718596
  234.0 84.1 %all-gather.6.cloned.1.call-start = ((), (), s32[]{:S(2)}) async-start(), calls=%async_computation.6 | async-start | bytes 2359296 | tf_op jit(solution)/shard_map/all_gather | solution.py:209
  261.2 5.4 %copy-start.14 = (f32[3,1,1024]{2,0,1:T(4,128)S(1)}, f32[3,1,1024]{2,0,1:T(4,128)}, u32[]{:S(2)}) copy-start(f32[3,1,1024]{2,0,1:T(4,128)} %copy-done.13) | copy-start | bytes 36868
  261.2 5.1 %collective-permute-start.6 = (f32[3,2,1024]{2,1,0:T(2,128)S(1)}, f32[3,2,1024]{2,1,0:T(2,128)S(1)}, u32[]{:S(2)}, u32[]{:S(2)}) collective-permute-start(f32[3,2,1024]{2,1,0:T(2,128)S(1)} %slice.85), channel_id=1, source_target_pairs={{8,0},{16,8},{24,16},{32,24},{40,32},{48,40},{56,48},{64,56},{72,6... | collective-permute-start | bytes 73736 | tf_op jit(solution)/shard_map/ppermute | solution.py:146
  322.2 5.7 %collective-permute-start.3 = (bf16[128,512]{1,0:T(8,128)(2,1)S(1)}, bf16[128,512]{1,0:T(8,128)(2,1)S(1)}, u32[]{:S(2)}, u32[]{:S(2)}) collective-permute-start(bf16[128,512]{1,0:T(8,128)(2,1)S(1)} %get-tuple-element.23), channel_id=1, source_target_pairs={{0,256},{4,0},{256,260},{260,4},{1,257},{5,1},{257,261},{261,5},{2... | collective-permute-start | bytes 393224 | tf_op jit(solution)/shard_map/ppermute | solution.py:151
  324.4 3.5 %collective-permute-start.2 = (bf16[128,512]{1,0:T(8,128)(2,1)S(1)}, bf16[128,512]{1,0:T(8,128)(2,1)S(1)}, u32[]{:S(2)}, u32[]{:S(2)}) collective-permute-start(bf16[128,512]{1,0:T(8,128)(2,1)S(1)} %get-tuple-element.22), channel_id=1, source_target_pairs={{0,0},{4,256},{256,4},{260,260},{1,1},{5,257},{257,5},{261,261},{2... | collective-permute-start | bytes 393224 | tf_op jit(solution)/shard_map/ppermute | solution.py:151
Sparse Core Ops, SparseCore 0:
  10.7 84.1 all-gather.3
  261.1 56.8 all-gather.5
where the time goes:
time: 340 us; the launch traced here: 335 us
  waiting for transfers between devices  220 us (65%)
  starting transfers between devices  47.1 us (14%)
  blocking collectives  27.6 us (8%)
  between operations  14.4 us (4%)
  matrix products  8.95 us (3%)
  other arithmetic  6.93 us (2%)
  local copies, waits for them, and re-layouts  5.99 us (2%)
  Pallas kernels  4.81 us (1%)
    all_gather x1, waiting for transfers between devices, per_device(): lax.all_gather(across(out_weight, lambda a, b: (b, a)), COLUMN, axis=0, t...  72.5 us
    all_gather x1, waiting for transfers between devices, per_device(): gated_all = lax.all_gather(gated, PLANE, axis=0).reshape(2, 4, rows, width)  51 us
    all_to_all x1, blocking collectives, per_device(): lax.all_to_all(back_owned, SEQ, 0, 0, tiled=True).reshape(width, rows)  27.6 us
    all_to_all x1, waiting for transfers between devices, per_device(): lax.all_to_all(product.T.reshape(BLOCKS, CHANNELS, LANES), SEQ, 0, 0, til...  22.9 us
    all_to_all x1, waiting for transfers between devices, per_device(): lax.all_to_all(long_owned, SEQ, 0, 0, tiled=True).reshape(width, rows)  22.5 us
    all_to_all x1, waiting for transfers between devices, per_device(): lax.all_to_all(partial, PLANE, 0, 0, tiled=True).astype(F32)  21.2 us
    all_to_all x1, waiting for transfers between devices, per_device(): lax.all_to_all(long_grad.T.reshape(BLOCKS, CHANNELS, LANES), SEQ, 0, 0, t...  21.2 us
    ppermute x5, starting transfers between devices, across(): return lax.ppermute(value, ('xh', 'xl'), pairs)  14.8 us
  transfers between devices with their start and end apart: 13, of which 10 were waited for; matrix products, arithmetic and copies ran while one was open for 1% of the time, Pallas kernels for 1%

commit v1 on v0

--- a/solution.py
+++ b/solution.py
@@ -93,7 +93,7 @@
 
 
 def backward_kernel(
-    grad_ref, filter_spectrum, product_spectrum,
+    grad_ref, filter_spectrum, product_spectrum, _,
     first, first_back, cos_twist, sin_twist, second, second_back,
     back_ref, filter_grad_ref, grid, turned, section,
 ):
@@ -125,17 +125,53 @@
 SECTION = pltpu.VMEM((CHANNELS * BLOCKS, 2 * LANES), F32)
 
 
-def run_kernel(kernel, out_shape, scratch, transforms, *operands):
+def run_kernel(kernel, out_shape, scratch, transforms, *operands, unread=()):
+    in_specs = [
+        pl.BlockSpec(memory_space=pl.ANY if i in unread else pltpu.VMEM) for i in range(len(operands))
+    ]
     transform_flops = 2 * CHANNELS * BLOCKS * LANES * (2 * BLOCKS + 4 * LANES)
     return pl.pallas_call(
         kernel,
         out_shape=out_shape,
+        in_specs=in_specs,
         scratch_shapes=scratch,
         compiler_params=pltpu.CompilerParams(vmem_limit_bytes=40 * 2**20),
         cost_estimate=pl.CostEstimate(
             flops=transforms * transform_flops, bytes_accessed=4 * 2**20, transcendentals=0
         ),
     )(*operands)
+
+
+def partial_kernel(gradient_ref, weight_ref, _, out_ref):
+    rows = gradient_ref.shape[0] * gradient_ref.shape[1]
+    product = lax.dot_general(
+        gradient_ref[...].reshape(rows, -1), weight_ref[0], (((1,), (1,)), ((), ())),
+        preferred_element_type=F32,
+    )
+    out_ref[...] = product.astype(BF16).reshape(out_ref.shape)
+
+
+def partial_product(gradient, weight, after):
+    halves, rows, features = gradient.shape
+    groups, width, _ = weight.shape
+    step = width // 2
+    return pl.pallas_call(
+        partial_kernel,
+        grid=(groups, width // step),
+        in_specs=[
+            pl.BlockSpec((halves, rows, features), lambda y, n: (0, 0, 0)),
+            pl.BlockSpec((1, step, features), lambda y, n: (y, n, 0)),
+            pl.BlockSpec(memory_space=pl.ANY),
+        ],
+        out_specs=pl.BlockSpec((halves, 1, rows, step), lambda y, n: (0, y, 0, n)),
+        out_shape=jax.ShapeDtypeStruct((halves, groups, rows, width), BF16),
+        compiler_params=pltpu.CompilerParams(vmem_limit_bytes=24 * 2**20),
+        cost_estimate=pl.CostEstimate(
+            flops=2 * halves * rows * groups * width * features,
+            bytes_accessed=8 * 2**20,
+            transcendentals=0,
+        ),
+    )(gradient, weight, after)
 
 
 def shift(value, steps):
@@ -189,10 +225,8 @@
     long_float = long_out.astype(F32)
     gated = (query_conv * long_float).astype(BF16)
 
-    partial = jnp.einsum(
-        "tmk,ynk->tymn", gradient, weight, preferred_element_type=F32
-    ).astype(BF16)
-    partial = partial.reshape(8, rows, width)
+    partial = partial_product(gradient, weight, gated).reshape(8, rows, width)
+    gated_all = lax.all_gather(gated, PLANE, axis=0)
     gated_grad = jnp.sum(lax.all_to_all(partial, PLANE, 0, 0, tiled=True).astype(F32), axis=0)
 
     long_grad = (query_conv * gated_grad).astype(BF16)
@@ -202,11 +236,11 @@
         backward_kernel,
         [SEQUENCES, jax.ShapeDtypeStruct((CHANNELS, LENGTH), F32)],
         [GRID, TURNED, SECTION], 3,
-        grad_owned, filter_spectrum, product_spectrum,
-        first, first_back, cos_twist, sin_twist, second, second_back,
-    )
-
-    gated_all = lax.all_gather(gated, PLANE, axis=0).reshape(2, 4, rows, width)
+        grad_owned, filter_spectrum, product_spectrum, gated_all,
+        first, first_back, cos_twist, sin_twist, second, second_back, unread=(3,),
+    )
+
+    gated_all = gated_all.reshape(2, 4, rows, width)
     share = jnp.einsum("tymn,ynk->tmk", gated_all, weight, preferred_element_type=F32).astype(BF16)
     mine = jnp.where(half == 0, share[0], share[1])
     other = jnp.where(half == 0, share[1], share[0])

time: 340 us -> 253 us (0.74)
  waiting for transfers between devices: 220 us -> 88.1 us
  starting transfers between devices: 47.1 us -> 75.5 us
  local copies, waits for them, and re-layouts: 5.99 us -> 19.4 us
  blocking collectives: 27.6 us -> 34.4 us
  matrix products: 8.95 us -> 3.43 us
    all_gather x1, waiting for transfers between devices: 72.5 us -> 0.02 us  [per_device(): lax.all_gather(across(out_weight, lambda a, b: (b, a)), COLUMN, axis=0, t...]
    all_gather x1, waiting for transfers between devices: 51 us -> 23.3 us  [per_device(): gated_all = lax.all_gather(gated, PLANE, axis=0)]
    all_to_all x1, waiting for transfers between devices: 21.2 us -> 0.42 us  [per_device(): lax.all_to_all(long_grad.T.reshape(BLOCKS, CHANNELS, LANES), SEQ, 0, 0, t...]
    unnamed x36 -> x64, local copies, waits for them, and re-layouts: 1.34 us -> 14.4 us
    all_to_all x1, starting transfers between devices: 11.5 us -> 22.8 us  [per_device(): lax.all_to_all(product.T.reshape(BLOCKS, CHANNELS, LANES), SEQ, 0, 0, til...]
    all_to_all x1, starting transfers between devices: 4.19 us -> 12.5 us  [per_device(): lax.all_to_all(long_grad.T.reshape(BLOCKS, CHANNELS, LANES), SEQ, 0, 0, t...]
    all_to_all x1, waiting for transfers between devices: 21.2 us -> 13.3 us  [per_device(): lax.all_to_all(back_owned, SEQ, 0, 0, tiled=True).reshape(width, rows)]
    all_to_all x1, blocking collectives: 27.6 us -> 34.4 us  [per_device(): lax.all_to_all(partial, PLANE, 0, 0, tiled=True).astype(F32)]
  transfers between devices with their start and end apart: 13 -> 13, of which waited for: 10 -> 7; matrix products, arithmetic and copies ran while one was open for 1% -> 6% of each run, Pallas kernels for 1% -> 2%
where the time goes in v1:
time: 253 us; the launch traced here: 251 us
  waiting for transfers between devices  88.1 us (35%)
  starting transfers between devices  75.5 us (30%)
  blocking collectives  34.4 us (14%)
  local copies, waits for them, and re-layouts  19.4 us (8%)
  between operations  14.5 us (6%)
  other arithmetic  8.36 us (3%)
  Pallas kernels  7.62 us (3%)
  matrix products  3.43 us (1%)
    all_to_all x1, blocking collectives, per_device(): lax.all_to_all(partial, PLANE, 0, 0, tiled=True).astype(F32)  34.4 us
    all_to_all x1, waiting for transfers between devices, per_device(): lax.all_to_all(product.T.reshape(BLOCKS, CHANNELS, LANES), SEQ, 0, 0, til...  25.5 us
    all_gather x1, waiting for transfers between devices, per_device(): gated_all = lax.all_gather(gated, PLANE, axis=0)  23.3 us
    all_to_all x1, starting transfers between devices, per_device(): lax.all_to_all(product.T.reshape(BLOCKS, CHANNELS, LANES), SEQ, 0, 0, til...  22.8 us
    all_to_all x1, waiting for transfers between devices, per_device(): lax.all_to_all(long_owned, SEQ, 0, 0, tiled=True).reshape(width, rows)  20 us
    ppermute x5, starting transfers between devices, across(): return lax.ppermute(value, ('xh', 'xl'), pairs)  15 us
    unnamed x64, local copies, waits for them, and re-layouts  14.4 us
    all_to_all x1, starting transfers between devices, per_device(): lax.all_to_all(back_owned, SEQ, 0, 0, tiled=True).reshape(width, rows)  13.7 us
  transfers between devices with their start and end apart: 13, of which 7 were waited for; matrix products, arithmetic and copies ran while one was open for 6% of the time, Pallas kernels for 2%

profile of v1, /device:TPU:1, one launch (start us, length us, event | category | flops | bytes accessed | tf_op | source)
XLA Modules:
  0.0 251.3 jit_solution(17602449720596228282)
XLA Ops:
  7.2 1.6 collective-permute-start.1
  8.8 0.7 copy-done.30
  9.5 0.8 pad_maximum_fusion.2
  10.2 4.9 %collective-permute-start = (bf16[3,2,1024]{2,1,0:T(2,128)(2,1)S(1)}, bf16[3,2,1024]{2,1,0:T(2,128)(2,1)S(1)}, u32[]{:S(2)}, u32[]{:S(2)}) collective-permute-start(bf16[3,2,1024]{2,1,0:T(2,128)(2,1)S(1)} %pad_maximum_fusion.2), channel_id=1, source_target_pairs={{0,8},{8,16},{16,24},{24,32},{32,40},{40,48},{48,56},{56,64},{64,7... | collective-permute-start | bytes 36872 | tf_op jit(solution)/shard_map/ppermute | solution.py:182
  15.2 0.9 fusion.12
  16.2 2.9 %collective-permute-done = bf16[3,2,1024]{2,1,0:T(2,128)(2,1)S(1)} collective-permute-done((bf16[3,2,1024]{2,1,0:T(2,128)(2,1)S(1)}, bf16[3,2,1024]{2,1,0:T(2,128)(2,1)S(1)}, u32[]{:S(2)}, u32[]{:S(2)}) %collective-permute-start) | collective-permute-done | bytes 12320 | tf_op jit(solution)/shard_map/ppermute | solution.py:182
  19.1 1.3 maximum_convert_fusion
  20.9 1.2 copy-done.18
  22.2 0.8 copy.22
  23.1 22.8 %all-to-all-start = ((bf16[64,16,128]{2,1,0:T(8,128)(2,1)}), bf16[64,16,128]{2,1,0:T(8,128)(2,1)S(1)}, u32[]{:S(2)}, u32[]{:S(2)}) async-start(bf16[64,16,128]{2,1,0:T(8,128)(2,1)} %bitcast.7), calls=%async_computation | async-start | bytes 524288 | tf_op jit(solution)/shard_map/all_to_all | solution.py:219
  46.5 25.5 %all-to-all-done.product_ref = bf16[64,16,128]{2,1,0:T(8,128)(2,1)S(1)} async-done(((bf16[64,16,128]{2,1,0:T(8,128)(2,1)}), bf16[64,16,128]{2,1,0:T(8,128)(2,1)S(1)}, u32[]{:S(2)}, u32[]{:S(2)}) %all-to-all-start) | async-done | bytes 262176 | tf_op jit(solution)/shard_map/all_to_all | solution.py:219
  72.0 1.8 shard_map.165
  73.8 1.1 copy-done.5
  74.9 4.6 %all-to-all-start.1 = ((bf16[64,16,128]{2,1,0:T(8,128)(2,1)}), bf16[64,16,128]{2,1,0:T(8,128)(2,1)S(1)}, u32[]{:S(2)}, u32[]{:S(2)}) async-start(bf16[64,16,128]{2,1,0:T(8,128)(2,1)} %get-tuple-element.9), calls=%async_computation.1 | async-start | bytes 524288 | tf_op jit(solution)/shard_map/all_to_all | solution.py:224
  79.5 1.6 collective-permute-start.4
  81.1 4.9 %collective-permute-start.5 = (bf16[128,512]{1,0:T(8,128)(2,1)}, bf16[128,512]{1,0:T(8,128)(2,1)S(1)}, u32[]{:S(2)}, u32[]{:S(2)}) collective-permute-start(bf16[128,512]{1,0:T(8,128)(2,1)} %param.19), channel_id=1, source_target_pairs={{0,4},{4,260},{256,0},{260,256},{1,5},{5,261},{257,1},{261,257},{2... | collective-permute-start | bytes 393224 | tf_op jit(solution)/shard_map/ppermute | solution.py:187
  86.0 20.0 %all-to-all-done.1 = bf16[64,16,128]{2,1,0:T(8,128)(2,1)S(1)} async-done(((bf16[64,16,128]{2,1,0:T(8,128)(2,1)}), bf16[64,16,128]{2,1,0:T(8,128)(2,1)S(1)}, u32[]{:S(2)}, u32[]{:S(2)}) %all-to-all-start.1) | async-done | bytes 262176 | tf_op jit(solution)/shard_map/all_to_all | solution.py:224
  106.1 0.8 bitcast_convert_fusion.1
  106.9 1.2 copy.23
  108.2 0.8 fusion.8._
  109.0 0.6 copy-done.28
  109.7 1.1 maximum_select_fusion.gradient_ref
  110.8 2.2 copy-done
  113.0 0.9 copy-done.1
  114.0 2.8 %shard_map.166 = bf16[2,4,128,1024]{3,2,1,0:T(8,128)(2,1)S(1)} custom-call(bf16[2,128,512]{2,1,0:T(8,128)(2,1)S(1)} %maximum_select_fusion.gradient_ref, bf16[4,1024,512]{2,1,0:T(8,128)(2,1)S(1)} %bitcast.93, bf16[128,1024]{1,0:T(8,128)(2,1)S(1)} %copy-done.1), custom_call_target="tpu_custom_call" | custom-call | flops 1073741824 | bytes 8388608 | tf_op jit(solution)/shard_map/pallas_call | solution.py:158
  116.8 34.4 %all_to_all.25 = bf16[8,128,1024]{2,1,0:T(8,128)(2,1)S(1)} all-to-all(bf16[8,128,1024]{2,1,0:T(8,128)(2,1)S(1)} %bitcast.91), channel_id=1, replica_groups=mesh['xh'=2,'z'=16,'co'=2,'xl'=2,'y'=4] {'xh','y'}, dimensions={0} | all-to-all | bytes 4194304 | tf_op jit(solution)/shard_map/all_to_all | solution.py:230
  151.6 0.9 fusion.9
  152.5 0.8 copy.24
  153.3 12.5 %all-to-all-start.3 = ((bf16[64,16,128]{2,1,0:T(8,128)(2,1)}), bf16[64,16,128]{2,1,0:T(8,128)(2,1)S(1)}, u32[]{:S(2)}, u32[]{:S(2)}) async-start(bf16[64,16,128]{2,1,0:T(8,128)(2,1)} %bitcast.22), calls=%async_computation.3 | async-start | bytes 524288 | tf_op jit(solution)/shard_map/all_to_all | solution.py:234
  165.9 23.3 %all-gather.6.cloned.1.call-done = bf16[1024,1024]{1,0:T(8,128)(2,1)} async-done(((bf16[128,1024]{1,0:T(8,128)(2,1)}), bf16[1024,1024]{1,0:T(8,128)(2,1)}) %all-gather.6.cloned.1.call-update) | async-done | bytes 2097168 | tf_op jit(solution)/shard_map/all_gather | solution.py:229
  189.7 1.6 copy-done.2
  191.2 1.2 copy-done.6
  192.5 0.9 copy-done.9
  193.4 0.8 copy-done.11
  194.1 0.8 copy-done.13
  194.9 0.8 copy-done.15
  195.7 2.5 shard_map.167
  198.1 0.7 copy-done.16
  198.8 13.7 %all-to-all-start.4 = ((bf16[64,16,128]{2,1,0:T(8,128)(2,1)}), bf16[64,16,128]{2,1,0:T(8,128)(2,1)S(1)}, u32[]{:S(2)}, u32[]{:S(2)}) async-start(bf16[64,16,128]{2,1,0:T(8,128)(2,1)} %copy-done.16), calls=%async_computation.4 | async-start | bytes 524288 | tf_op jit(solution)/shard_map/all_to_all | solution.py:252
  212.5 3.4 %fusion.5 = bf16[2,128,512]{2,1,0:T(8,128)(2,1)S(1)} fusion(bf16[2,4,128,1024]{3,2,1,0:T(8,128)(2,1)S(1)} %bitcast.95, bf16[4,1024,512,1]{2,1,0,3:T(8,128)(2,1)} %bitcast.92), kind=kOutput, calls=%fused_computation.14 | convolution fusion | flops 1073872896 | bytes 6553600 | tf_op jit(solution)/shard_map/tymn,ynk->tmk/dot_general | solution.py:244
  216.0 0.8 collective-permute-start.2
  216.8 6.1 %collective-permute-start.3 = (bf16[128,512]{1,0:T(8,128)(2,1)S(1)}, bf16[128,512]{1,0:T(8,128)(2,1)S(1)}, u32[]{:S(2)}, u32[]{:S(2)}) collective-permute-start(bf16[128,512]{1,0:T(8,128)(2,1)S(1)} %get-tuple-element.21), channel_id=1, source_target_pairs={{0,256},{4,0},{256,260},{260,4},{1,257},{5,1},{257,261},{261,5},{2... | collective-permute-start | bytes 393224 | tf_op jit(solution)/shard_map/ppermute | solution.py:187
  223.0 13.3 %all-to-all-done.4 = bf16[64,16,128]{2,1,0:T(8,128)(2,1)S(1)} async-done(((bf16[64,16,128]{2,1,0:T(8,128)(2,1)}), bf16[64,16,128]{2,1,0:T(8,128)(2,1)S(1)}, u32[]{:S(2)}, u32[]{:S(2)}) %all-to-all-start.4) | async-done | bytes 262176 | tf_op jit(solution)/shard_map/all_to_all | solution.py:252
  236.7 0.9 copy-done.21
  237.8 1.9 collective-permute-start.6
  239.7 0.7 add_convert_fusion
  240.4 2.5 collective-permute-done.6
  243.6 0.9 slice_bitcast_fusion.3
  (73 shorter events, 3.4 us)
Async XLA Ops:
  7.2 103.7 %all-gather.4.cloned.1.call-start = ((), (), s32[]{:S(2)}) async-start(), calls=%async_computation.5 | async-start | bytes 4325376 | tf_op jit(solution)/shard_map/all_gather | solution.py:197
  7.2 1.6 collective-permute-start.1
  8.8 0.7 copy-start.30
  10.2 8.8 %collective-permute-start = (bf16[3,2,1024]{2,1,0:T(2,128)(2,1)S(1)}, bf16[3,2,1024]{2,1,0:T(2,128)(2,1)S(1)}, u32[]{:S(2)}, u32[]{:S(2)}) collective-permute-start(bf16[3,2,1024]{2,1,0:T(2,128)(2,1)S(1)} %pad_maximum_fusion.2), channel_id=1, source_target_pairs={{0,8},{8,16},{16,24},{24,32},{32,40},{40,48},{48,56},{56,64},{64,7... | collective-permute-start | bytes 36872 | tf_op jit(solution)/shard_map/ppermute | solution.py:182
  16.1 4.7 %copy-start.22 = (f32[3,1024]{1,0:T(4,128)}, f32[3,1024]{1,0:T(4,128)S(1)}, u32[]{:S(2)}) copy-start(f32[3,1024]{1,0:T(4,128)S(1)} %get-tuple-element.25) | copy-start | bytes 36868
  16.2 4.7 %copy-start.24 = (f32[3,1024]{1,0:T(4,128)}, f32[3,1024]{1,0:T(4,128)S(1)}, u32[]{:S(2)}) copy-start(f32[3,1024]{1,0:T(4,128)S(1)} %get-tuple-element.26) | copy-start | bytes 36868
  16.2 4.7 %copy-start.26 = (f32[3,1,1024]{2,0,1:T(4,128)}, f32[3,1,1024]{2,0,1:T(4,128)S(1)}, u32[]{:S(2)}) copy-start(f32[3,1,1024]{2,0,1:T(4,128)S(1)} %copy.33) | copy-start | bytes 36868
  20.9 1.2 copy-start.18
  22.1 23.7 %copy-start.4 = (bf16[256,256]{1,0:T(8,128)(2,1)S(1)}, bf16[256,256]{1,0:T(8,128)(2,1)}, u32[]{:S(2)}) copy-start(bf16[256,256]{1,0:T(8,128)(2,1)} %constant.26.clone.second) | copy-start | bytes 393220
  22.1 23.8 %copy-start.7 = (f32[16,8192]{1,0:T(8,128)S(1)}, f32[16,8192]{1,0:T(8,128)}, u32[]{:S(2)}) copy-start(f32[16,8192]{1,0:T(8,128)} %filter_ref.1) | copy-start | bytes 1572868
  22.1 23.8 %copy-start.10 = (bf16[128,64]{1,0:T(8,128)(2,1)S(1)}, bf16[128,64]{1,0:T(8,128)(2,1)}, u32[]{:S(2)}) copy-start(bf16[128,64]{1,0:T(8,128)(2,1)} %constant.22.clone.first) | copy-start | bytes 49156
  22.1 23.8 %copy-start.12 = (f32[64,128]{1,0:T(8,128)S(1)}, f32[64,128]{1,0:T(8,128)}, u32[]{:S(2)}) copy-start(f32[64,128]{1,0:T(8,128)} %constant.24.clone.cos_twist) | copy-start | bytes 98308
  22.1 23.8 %copy-start.14 = (f32[64,128]{1,0:T(8,128)S(1)}, f32[64,128]{1,0:T(8,128)}, u32[]{:S(2)}) copy-start(f32[64,128]{1,0:T(8,128)} %constant.25.clone.sin_twist) | copy-start | bytes 98308
  22.2 49.8 %copy-start.8 = (bf16[256,256]{1,0:T(8,128)(2,1)S(1)}, bf16[256,256]{1,0:T(8,128)(2,1)}, u32[]{:S(2)}) copy-start(bf16[256,256]{1,0:T(8,128)(2,1)} %constant.27.clone.second_back) | copy-start | bytes 393220
  22.2 49.8 %copy-start.17 = (bf16[64,128]{1,0:T(8,128)(2,1)S(1)}, bf16[64,128]{1,0:T(8,128)(2,1)}, u32[]{:S(2)}) copy-start(bf16[64,128]{1,0:T(8,128)(2,1)} %constant.23.clone.first_back) | copy-start | bytes 49156
  23.1 48.9 %all-to-all-start = ((bf16[64,16,128]{2,1,0:T(8,128)(2,1)}), bf16[64,16,128]{2,1,0:T(8,128)(2,1)S(1)}, u32[]{:S(2)}, u32[]{:S(2)}) async-start(bf16[64,16,128]{2,1,0:T(8,128)(2,1)} %bitcast.7), calls=%async_computation | async-start | bytes 524288 | tf_op jit(solution)/shard_map/all_to_all | solution.py:219
  73.8 1.1 copy-start.5
  74.9 33.3 %copy-start.19 = (f32[3,128,1024]{2,1,0:T(8,128)S(1)}, f32[3,128,1024]{2,1,0:T(8,128)}, u32[]{:S(2)}) copy-start(f32[3,128,1024]{2,1,0:T(8,128)} %copy-done.18) | copy-start | bytes 4718596
  74.9 31.2 %all-to-all-start.1 = ((bf16[64,16,128]{2,1,0:T(8,128)(2,1)}), bf16[64,16,128]{2,1,0:T(8,128)(2,1)S(1)}, u32[]{:S(2)}, u32[]{:S(2)}) async-start(bf16[64,16,128]{2,1,0:T(8,128)(2,1)} %get-tuple-element.9), calls=%async_computation.1 | async-start | bytes 524288 | tf_op jit(solution)/shard_map/all_to_all | solution.py:224
  79.5 109.8 %all-gather.6.cloned.1.call-start = ((), (), s32[]{:S(2)}) async-start(), calls=%async_computation.6 | async-start | bytes 2359296 | tf_op jit(solution)/shard_map/all_gather | solution.py:229
  79.5 29.4 %collective-permute-start.4 = (bf16[128,512]{1,0:T(8,128)(2,1)}, bf16[128,512]{1,0:T(8,128)(2,1)S(1)}, u32[]{:S(2)}, u32[]{:S(2)}) collective-permute-start(bf16[128,512]{1,0:T(8,128)(2,1)} %param.19), channel_id=1, source_target_pairs={{0,0},{4,256},{256,4},{260,260},{1,1},{5,257},{257,5},{261,261},{2... | collective-permute-start | bytes 393224 | tf_op jit(solution)/shard_map/ppermute | solution.py:187
  81.1 27.9 %collective-permute-start.5 = (bf16[128,512]{1,0:T(8,128)(2,1)}, bf16[128,512]{1,0:T(8,128)(2,1)S(1)}, u32[]{:S(2)}, u32[]{:S(2)}) collective-permute-start(bf16[128,512]{1,0:T(8,128)(2,1)} %param.19), channel_id=1, source_target_pairs={{0,4},{4,260},{256,0},{260,256},{1,5},{5,261},{257,1},{261,257},{2... | collective-permute-start | bytes 393224 | tf_op jit(solution)/shard_map/ppermute | solution.py:187
  109.0 0.7 copy-start.28
  109.0 0.7 copy-start.29
  110.8 2.2 copy-start
  113.0 0.9 copy-start.1
  153.3 36.3 %all-to-all-start.3 = ((bf16[64,16,128]{2,1,0:T(8,128)(2,1)}), bf16[64,16,128]{2,1,0:T(8,128)(2,1)S(1)}, u32[]{:S(2)}, u32[]{:S(2)}) async-start(bf16[64,16,128]{2,1,0:T(8,128)(2,1)} %bitcast.22), calls=%async_computation.3 | async-start | bytes 524288 | tf_op jit(solution)/shard_map/all_to_all | solution.py:234
  189.7 1.6 copy-start.2
  191.2 1.2 copy-start.6
  192.5 0.9 copy-start.9
  193.4 0.8 copy-start.11
  194.1 0.8 copy-start.13
  194.9 0.8 copy-start.15
  195.7 16.9 %copy-start.3 = (bf16[1024,1024]{1,0:T(8,128)(2,1)S(1)}, bf16[1024,1024]{1,0:T(8,128)(2,1)}, u32[]{:S(2)}) copy-start(bf16[1024,1024]{1,0:T(8,128)(2,1)} %all-gather.6.cloned.1.call-done) | copy-start | bytes 6291460
  198.1 0.7 copy-start.16
  198.8 37.4 %all-to-all-start.4 = ((bf16[64,16,128]{2,1,0:T(8,128)(2,1)}), bf16[64,16,128]{2,1,0:T(8,128)(2,1)S(1)}, u32[]{:S(2)}, u32[]{:S(2)}) async-start(bf16[64,16,128]{2,1,0:T(8,128)(2,1)} %copy-done.16), calls=%async_computation.4 | async-start | bytes 524288 | tf_op jit(solution)/shard_map/all_to_all | solution.py:252
  216.0 20.6 %copy-start.20 = (f32[3,128,1024]{2,1,0:T(8,128)S(1)}, f32[3,128,1024]{2,1,0:T(8,128)}, u32[]{:S(2)}) copy-start(f32[3,128,1024]{2,1,0:T(8,128)} %copy-done.18) | copy-start | bytes 4718596
  216.0 23.7 %collective-permute-start.2 = (bf16[128,512]{1,0:T(8,128)(2,1)S(1)}, bf16[128,512]{1,0:T(8,128)(2,1)S(1)}, u32[]{:S(2)}, u32[]{:S(2)}) collective-permute-start(bf16[128,512]{1,0:T(8,128)(2,1)S(1)} %get-tuple-element.20), channel_id=1, source_target_pairs={{0,0},{4,256},{256,4},{260,260},{1,1},{5,257},{257,5},{261,261},{2... | collective-permute-start | bytes 393224 | tf_op jit(solution)/shard_map/ppermute | solution.py:187
  216.8 22.9 %collective-permute-start.3 = (bf16[128,512]{1,0:T(8,128)(2,1)S(1)}, bf16[128,512]{1,0:T(8,128)(2,1)S(1)}, u32[]{:S(2)}, u32[]{:S(2)}) collective-permute-start(bf16[128,512]{1,0:T(8,128)(2,1)S(1)} %get-tuple-element.21), channel_id=1, source_target_pairs={{0,256},{4,0},{256,260},{260,4},{1,257},{5,1},{257,261},{261,5},{2... | collective-permute-start | bytes 393224 | tf_op jit(solution)/shard_map/ppermute | solution.py:187
  236.5 1.0 copy-start.21
  237.8 5.1 %collective-permute-start.6 = (f32[3,2,1024]{2,1,0:T(2,128)S(1)}, f32[3,2,1024]{2,1,0:T(2,128)S(1)}, u32[]{:S(2)}, u32[]{:S(2)}) collective-permute-start(f32[3,2,1024]{2,1,0:T(2,128)S(1)} %slice.85), channel_id=1, source_target_pairs={{8,0},{16,8},{24,16},{32,24},{40,32},{48,40},{56,48},{64,56},{72,6... | collective-permute-start | bytes 73736 | tf_op jit(solution)/shard_map/ppermute | solution.py:182
  240.4 2.6 %copy-start.23 = (f32[3,1024]{1,0:T(4,128)S(1)}, f32[3,1024]{1,0:T(4,128)}, u32[]{:S(2)}) copy-start(f32[3,1024]{1,0:T(4,128)} %copy-done.22) | copy-start | bytes 36868
  240.4 2.7 %copy-start.25 = (f32[3,1024]{1,0:T(4,128)S(1)}, f32[3,1024]{1,0:T(4,128)}, u32[]{:S(2)}) copy-start(f32[3,1024]{1,0:T(4,128)} %copy-done.24) | copy-start | bytes 36868
  240.4 2.7 %copy-start.27 = (f32[3,1,1024]{2,0,1:T(4,128)S(1)}, f32[3,1,1024]{2,0,1:T(4,128)}, u32[]{:S(2)}) copy-start(f32[3,1,1024]{2,0,1:T(4,128)} %copy-done.26) | copy-start | bytes 36868
Sparse Core Ops, SparseCore 0:
  10.7 98.4 all-gather.3
  113.0 76.2 all-gather.5

commit v2 on v0

v2 whole, which is shorter than its diff:
```python
import math

import jax
import jax.numpy as jnp
import numpy as np
from jax import lax
from jax.experimental import pallas as pl
from jax.experimental.pallas import tpu as pltpu
from jax.sharding import Mesh
from jax.sharding import PartitionSpec as P

BF16 = jnp.bfloat16
F32 = jnp.float32

SEQ = ("xh", "z", "co")
TP = ("xl", "y")
ROW = ("xh", "xl")
PLANE = ("xh", "y")
COLUMN = ("z", "co")

CHANNELS = 16
BLOCKS = 64
LANES = 128
LENGTH = BLOCKS * LANES


def transform_tables():
    blocks = np.arange(BLOCKS)
    lanes = np.arange(LANES)
    first = 2.0 * np.pi * np.outer(blocks + 0.25, blocks) / BLOCKS
    twist = 2.0 * np.pi * np.outer(blocks + 0.25, lanes) / LENGTH
    second = 2.0 * np.pi * (np.outer(lanes, lanes) % LANES) / LANES
    first_table = np.concatenate([np.cos(first), -np.sin(first)], axis=0)
    cosine, sine = np.cos(second), np.sin(second)
    second_table = np.block([[cosine, -sine], [sine, cosine]])
    steps = np.zeros((2 * LANES, 5 * LANES))
    steps[:, : 2 * LANES] = second_table
    steps[:, 2 * LANES : 4 * LANES] = second_table.T
    steps[: 2 * BLOCKS, 4 * LANES : 4 * LANES + BLOCKS] = first_table
    steps[2 * BLOCKS : 3 * BLOCKS, 4 * LANES : 4 * LANES + 2 * BLOCKS] = first_table.T / LENGTH
    turns = np.concatenate([np.cos(twist), np.sin(twist)], axis=1)
    return jnp.asarray(steps, BF16), jnp.asarray(turns, F32)


def to_spectrum(grid_ref, turned_ref, steps, turns):
    first = steps[: 2 * BLOCKS, 4 * LANES : 4 * LANES + BLOCKS]
    cos_twist, sin_twist = turns[:, :LANES], turns[:, LANES:]
    for c in range(CHANNELS):
        grid = grid_ref[pl.ds(c, BLOCKS, stride=CHANNELS), :].astype(BF16)
        section = jnp.dot(first, grid, preferred_element_type=F32)
        real, imag = section[:BLOCKS], section[BLOCKS:]
        rows = slice(c * BLOCKS, (c + 1) * BLOCKS)
        turned_ref[rows, :LANES] = (real * cos_twist + imag * sin_twist).astype(BF16)
        turned_ref[rows, LANES:] = (imag * cos_twist - real * sin_twist).astype(BF16)
    return jnp.dot(turned_ref[...], steps[:, : 2 * LANES], preferred_element_type=F32)


def from_spectrum(spectrum, grid_ref, section_ref, steps, turns):
    first_back = steps[2 * BLOCKS : 3 * BLOCKS, 4 * LANES : 4 * LANES + 2 * BLOCKS]
    cos_twist, sin_twist = turns[:, :LANES], turns[:, LANES:]
    section_ref[...] = jnp.dot(
        spectrum, steps[:, 2 * LANES : 4 * LANES], preferred_element_type=F32
    )
    for c in range(CHANNELS):
        rows = slice(c * BLOCKS, (c + 1) * BLOCKS)
        real, imag = section_ref[rows, :LANES], section_ref[rows, LANES:]
        turned = jnp.concatenate(
            [real * cos_twist - imag * sin_twist, imag * cos_twist + real * sin_twist], axis=0
        ).astype(BF16)
        grid_ref[pl.ds(c, BLOCKS, stride=CHANNELS), :] = jnp.dot(
            first_back, turned, preferred_element_type=F32
        )


def filter_kernel(filter_ref, steps, turns, spectrum_ref, grid, turned):
    for b in range(BLOCKS):
        grid[b * CHANNELS : (b + 1) * CHANNELS, :] = filter_ref[:, b * LANES : (b + 1) * LANES]
    spectrum_ref[...] = to_spectrum(grid, turned, steps, turns)


def forward_kernel(
    product_ref, filter_spectrum, steps, turns, long_ref, product_spectrum, grid, turned, section
):
    grid[...] = product_ref[...].astype(F32).reshape(BLOCKS * CHANNELS, LANES)
    own = to_spectrum(grid, turned, steps, turns)
    product_spectrum[...] = own
    own_re, own_im = own[:, :LANES], own[:, LANES:]
    other_re, other_im = filter_spectrum[:, :LANES], filter_spectrum[:, LANES:]
    turned[:, :LANES] = (own_re * other_re - own_im * other_im).astype(BF16)
    turned[:, LANES:] = (own_re * other_im + own_im * other_re).astype(BF16)
    from_spectrum(turned[...], grid, section, steps, turns)
    long_ref[...] = grid[...].reshape(BLOCKS, CHANNELS, LANES).astype(BF16)


def backward_kernel(
    grad_ref, filter_spectrum, product_spectrum, _, steps, turns,
    back_ref, filter_grad_ref, grid, turned, section,
):
    grid[...] = grad_ref[...].astype(F32).reshape(BLOCKS * CHANNELS, LANES)
    own = to_spectrum(grid, turned, steps, turns)
    own_re, own_im = own[:, :LANES], own[:, LANES:]

    def correlate(other):
        other_re, other_im = other[:, :LANES], other[:, LANES:]
        turned[:, :LANES] = (own_re * other_re + own_im * other_im).astype(BF16)
        turned[:, LANES:] = (own_im * other_re - own_re * other_im).astype(BF16)
        from_spectrum(turned[...], grid, section, steps, turns)

    correlate(filter_spectrum)
    back_ref[...] = grid[...].reshape(BLOCKS, CHANNELS, LANES).astype(BF16)
    correlate(product_spectrum)
    for b in range(BLOCKS):
        filter_grad_ref[:, b * LANES : (b + 1) * LANES] = grid[
            b * CHANNELS : (b + 1) * CHANNELS, :
        ] * (1.0 / math.sqrt(LENGTH))


SPECTRUM = jax.ShapeDtypeStruct((CHANNELS * BLOCKS, 2 * LANES), F32)
SEQUENCES = jax.ShapeDtypeStruct((BLOCKS, CHANNELS, LANES), BF16)
GRID = pltpu.VMEM((BLOCKS * CHANNELS, LANES), F32)
TURNED = pltpu.VMEM((CHANNELS * BLOCKS, 2 * LANES), BF16)
SECTION = pltpu.VMEM((CHANNELS * BLOCKS, 2 * LANES), F32)


def run_kernel(kernel, out_shape, scratch, transforms, *operands, unread=()):
    in_specs = [
        pl.BlockSpec(memory_space=pl.ANY if i in unread else pltpu.VMEM) for i in range(len(operands))
    ]
    transform_flops = 2 * CHANNELS * BLOCKS * LANES * (2 * BLOCKS + 4 * LANES)
    return pl.pallas_call(
        kernel,
        out_shape=out_shape,
        in_specs=in_specs,
        scratch_shapes=scratch,
        compiler_params=pltpu.CompilerParams(vmem_limit_bytes=20 * 2**20),
        cost_estimate=pl.CostEstimate(
            flops=transforms * transform_flops, bytes_accessed=4 * 2**20, transcendentals=0
        ),
    )(*operands)


def run_blocks(kernel, steps, ins, outs, moved, flops=10**6, scratch=()):
    def spec(block, axis):
        if block is None:
            return pl.BlockSpec(memory_space=pl.ANY)
        return pl.BlockSpec(block, lambda i: tuple(i if d == axis else 0 for d in range(len(block))))

    return pl.pallas_call(
        kernel,
        grid=(steps,),
        in_specs=[spec(block, axis) for _, block, axis in ins],
        out_specs=[spec(block, axis) for _, _, block, axis in outs],
        out_shape=[jax.ShapeDtypeStruct(shape, dtype) for shape, dtype, _, _ in outs],
        scratch_shapes=list(scratch),
        compiler_params=pltpu.CompilerParams(vmem_limit_bytes=20 * 2**20),
        cost_estimate=pl.CostEstimate(flops=flops, bytes_accessed=moved, transcendentals=0),
    )(*[array for array, _, _ in ins])


def row_numbers(value):
    return lax.broadcasted_iota(jnp.int32, value.shape, 0)


def causal(value, before, taps):
    number = row_numbers(value)
    one = jnp.where(number == 0, before[1:2], pltpu.roll(value, 1, 0))
    two = jnp.where(number == 0, before[0:1], pltpu.roll(value, 2, 0))
    two = jnp.where(number == 1, before[1:2], two)
    return taps[0:1] * value + taps[1:2] * one + taps[2:3] * two


def adjoint(value, after, taps):
    rows = value.shape[0]
    number = row_numbers(value)
    one = jnp.where(number == rows - 1, after[0:1], pltpu.roll(value, rows - 1, 0))
    two = jnp.where(number == rows - 1, after[1:2], pltpu.roll(value, rows - 2, 0))
    two = jnp.where(number == rows - 2, after[0:1], two)
    return taps[0:1] * value + taps[1:2] * one + taps[2:3] * two


def filter_inputs(q_ref, k_ref, v_ref, before_ref, taps_ref, qc_ref, kc_ref, vc_ref, product_ref):
    sources = (q_ref, k_ref, v_ref)
    qc, kc, vc = (
        causal(sources[i][...].astype(F32), before_ref[i].astype(F32), taps_ref[i]) for i in range(3)
    )
    qc_ref[...], kc_ref[...], vc_ref[...] = qc, kc, vc
    product_ref[...] = (kc * vc).T.astype(BF16)


def gate(long_ref, qc_ref, out_ref, gated_ref):
    long = long_ref[...].astype(F32).T
    out_ref[...] = long
    gated = (qc_ref[...] * long).astype(BF16)
    gated_ref[0] = gated[:, :LANES]
    gated_ref[1] = gated[:, LANES:]


def partial_kernel(gradient_ref, weight_ref, _, out_ref):
    halves, groups, rows, features = gradient_ref.shape
    width = weight_ref.shape[0] * weight_ref.shape[2]
    total = jnp.zeros((halves * rows, width), F32)
    for f in range(groups):
        total += lax.dot_general(
            gradient_ref[:, f].reshape(halves * rows, features),
            weight_ref[:, f].reshape(width, features),
            (((1,), (1,)), ((), ())),
            preferred_element_type=F32,
        )
    out_ref[...] = total.astype(BF16).reshape(out_ref.shape)


def long_gradient(parts_ref, qc_ref, long_ref, grad_ref, qg_ref):
    parts = parts_ref[...].astype(F32)
    gated_grad = jnp.concatenate(
        [(parts[r] + parts[r + 1]) + (parts[r + 2] + parts[r + 3]) for r in (0, 4)], axis=1
    )
    grad_ref[...] = (qc_ref[...] * gated_grad).T.astype(BF16)
    qg_ref[...] = gated_grad * long_ref[...]


def mix_kernel(gated_ref, weight_ref, out_ref, total):
    halves, rows, width = gated_ref.shape[1:]
    groups, features = weight_ref.shape[1], weight_ref.shape[3]
    step = pl.program_id(0)

    @pl.when(step == 0)
    def _():
        total[...] = jnp.zeros_like(total)

    gated = gated_ref[...].reshape(halves * rows, width)
    for f in range(groups):
        total[f] += jnp.dot(
            gated, weight_ref[:, f].reshape(width, features), preferred_element_type=F32
        )

    @pl.when(step == pl.num_programs(0) - 1)
    def _():
        out_ref[...] = total[...].astype(BF16).reshape(out_ref.shape)


def query_adjoint(qg_ref, after_ref, taps_ref, out_ref):
    out_ref[...] = adjoint(qg_ref[...], after_ref[...], taps_ref[0]).astype(BF16)


def key_value_adjoint(
    back_ref, kc_ref, vc_ref, after_ref, next_ref, taps_ref, key_ref, value_ref
):
    back = back_ref[...].astype(F32).T
    after = after_ref[...].astype(F32)
    key_ref[...] = adjoint(back * vc_ref[...], after * next_ref[1], taps_ref[1]).astype(BF16)
    value_ref[...] = adjoint(back * kc_ref[...], after * next_ref[0], taps_ref[2]).astype(BF16)


def shift(value, steps):
    count = 1
    for axis in SEQ:
        count *= lax.axis_size(axis)
    first, last = max(0, -steps), min(count, count - steps)
    return lax.ppermute(value, SEQ, [(i, i + steps) for i in range(first, last)])


def across(value, dx, dl):
    if not (dx or dl):
        return value
    return lax.ppermute(value, ROW, [(i, i ^ (2 * dx + dl)) for i in range(4)])


def per_device(queries, keys, values, short_taps, long_filter, out_weight, cotangent):
    rows, width = queries.shape
    features = out_weight.shape[1]
    own_xh, own_xl = lax.axis_index("xh"), lax.axis_index("xl")
    kinds, chunk = 4, width // 4

    turned = lax.ppermute(
        out_weight,
        ("xh", "co", "xl"),
        [(4 * a + 2 * c + b, 4 * c + 2 * b + a) for a in range(2) for c in range(2) for b in range(2)],
    )
    weight = lax.all_gather(turned, COLUMN, axis=0).reshape(16, 2, rows, features)

    before = shift(jnp.stack([x[rows - 2 :] for x in (queries, keys, values)]), 1)
    steps, turns = transform_tables()
    filter_spectrum = run_kernel(filter_kernel, SPECTRUM, [GRID, TURNED], 1, long_filter, steps, turns)

    tokens = (rows, chunk)
    channels = (chunk, rows)
    taps_block = (3, 3, chunk)
    plane = ((rows, width), F32, tokens, 1)
    query_conv, key_conv, value_conv, product = run_blocks(
        filter_inputs, kinds,
        [(queries, tokens, 1), (keys, tokens, 1), (values, tokens, 1),
         (before, (3, 2, chunk), 2), (short_taps, taps_block, 2)],
        [plane, plane, plane, ((width, rows), BF16, channels, 0)], 3 * 2**20,
    )

    product_owned = lax.all_to_all(product.reshape(BLOCKS, CHANNELS, LANES), SEQ, 0, 0, tiled=True)
    long_owned, product_spectrum = run_kernel(
        forward_kernel, [SEQUENCES, SPECTRUM], [GRID, TURNED, SECTION], 2,
        product_owned, filter_spectrum, steps, turns,
    )
    blocks = [[across(cotangent, dx, dl) for dl in range(2)] for dx in range(2)]
    gradient = jnp.stack([jnp.stack(line) for line in blocks])
    gradient = jnp.where(own_xh == 0, gradient, gradient[::-1])
    gradient = jnp.where(own_xl == 0, gradient, gradient[:, ::-1])

    long_raw = lax.all_to_all(long_owned, SEQ, 0, 0, tiled=True).reshape(width, rows)
    long_out, gated = run_blocks(
        gate, kinds,
        [(long_raw, channels, 0), (query_conv, tokens, 1)],
        [plane, ((2, rows, width // 2), BF16, (2, rows, LANES), 2)], 2 * 2**20,
    )

    quarter = (4, 2, rows, features)
    (partial,) = run_blocks(
        partial_kernel, kinds,
        [(gradient, gradient.shape, None), (weight, quarter, 0), (gated, None, None)],
        [((2, 4, rows, width // 2), BF16, (2, 1, rows, width // 2), 1)], 6 * 2**20, 2**30,
    )
    parts = lax.all_to_all(partial.reshape(8, rows, width // 2), PLANE, 0, 0, tiled=True)
    long_grad, query_conv_grad = run_blocks(
        long_gradient, kinds,
        [(parts, (8, rows, LANES), 2), (query_conv, tokens, 1), (long_out, tokens, 1)],
        [((width, rows), BF16, channels, 0), plane], 3 * 2**20,
    )
    grad_owned = lax.all_to_all(long_grad.reshape(BLOCKS, CHANNELS, LANES), SEQ, 0, 0, tiled=True)

    keep = jnp.where(own_xh == 0, gated[0], gated[1])
    send = jnp.where(own_xh == 0, gated[1], gated[0])
    gated_all = lax.all_gather(jnp.stack([keep, across(send, 1, 0)]), "y", axis=0)

    back_owned, filter_grad = run_kernel(
        backward_kernel,
        [SEQUENCES, jax.ShapeDtypeStruct((CHANNELS, LENGTH), F32)],
        [GRID, TURNED, SECTION], 3,
        grad_owned, filter_spectrum, product_spectrum, gated_all, steps, turns, unread=(3,),
    )

    (share,) = run_blocks(
        mix_kernel, kinds,
        [(gated_all, (1, 2, rows, width // 2), 0), (weight, quarter, 0)],
        [((2, 2, rows, features), BF16, (2, 2, rows, features), None)], 6 * 2**20, 2**30,
        [pltpu.VMEM((2, 2 * rows, features), F32)],
    )
    share = jnp.where(own_xl == 0, share, share[::-1])
    mixed = share[0, 0].astype(F32)
    for dx, dl in ((0, 1), (1, 0), (1, 1)):
        mixed = mixed + across(share[dl, dx], dx, dl).astype(F32)
    mixed = mixed.astype(BF16)

    rim = (2, chunk)
    (query_grad,) = run_blocks(
        query_adjoint, kinds,
        [(query_conv_grad, tokens, 1), (shift(query_conv_grad[:2], -1), rim, 1), (short_taps, taps_block, 2)],
        [((rows, width), BF16, tokens, 1)], 2**20,
    )
    following = shift(jnp.stack([key_conv[:2], value_conv[:2]]), -1)

    back_raw = lax.all_to_all(back_owned, SEQ, 0, 0, tiled=True).reshape(width, rows)
    after = shift(back_raw[:, :2].T, -1)
    key_grad, value_grad = run_blocks(
        key_value_adjoint, kinds,
        [(back_raw, channels, 0), (key_conv, tokens, 1), (value_conv, tokens, 1),
         (after, rim, 1), (following, (2, 2, chunk), 2), (short_taps, taps_block, 2)],
        [((rows, width), BF16, tokens, 1)] * 2, 3 * 2**20,
    )
    return (mixed, query_grad, key_grad, value_grad, filter_grad)


def solution(mesh):
    fine = Mesh(mesh.devices.reshape(2, 16, 2, 2, 4), ("xh", "z", "co", "xl", "y"))
    token = P(SEQ, TP)
    in_specs = (token, token, token, P(None, None, TP), P(TP + SEQ, None), token, token)
    out_specs = (token, token, token, token, P(TP + SEQ, None))
    return jax.shard_map(
        per_device, mesh=fine, in_specs=in_specs, out_specs=out_specs, check_vma=False
    )
```

time: 340 us -> 228 us (0.67)
  waiting for transfers between devices: 220 us -> 81.9 us
  starting transfers between devices: 47.1 us -> 86.6 us
  blocking collectives: 27.6 us -> 0 us
  local copies, waits for them, and re-layouts: 5.99 us -> 22.9 us
  Pallas kernels: 4.81 us -> 17.6 us
  matrix products: 8.95 us -> 0 us
  other arithmetic: 6.93 us -> 1.89 us
    all_gather x2, waiting for transfers between devices: 123 us -> 12.2 us  [the longest x1 12.2 us: per_device(): lax.all_gather(jnp.stack([keep, across(send, 1, 0)]), 'y', axis=0)]
    all_to_all x1 -> x0, blocking collectives: 27.6 us -> none  [per_device(): lax.all_to_all(back_owned, SEQ, 0, 0, tiled=True).reshape(width, rows)]
    all_to_all x3 -> x4, waiting for transfers between devices: 65.3 us -> 37.9 us  [the longest x1 22.4 us: per_device(): lax.all_to_all(product.reshape(BLOCKS, CHANNELS, LANES), SEQ, 0, 0, tiled...]
    all_to_all x3 -> x4, starting transfers between devices: 22.6 us -> 43.8 us  [the longest x1 22.5 us: per_device(): lax.all_to_all(product.reshape(BLOCKS, CHANNELS, LANES), SEQ, 0, 0, tiled...]
    unnamed x36 -> x57, local copies, waits for them, and re-layouts: 1.34 us -> 20.7 us
    ppermute x5 -> x8, waiting for transfers between devices: 4.48 us -> 20 us  [the longest x7 17.8 us: across(): return lax.ppermute(value, ROW, [(i, i ^ 2 * dx + dl) for i in range(4)])]
    ppermute x5 -> x8, starting transfers between devices: 14.8 us -> 29.2 us  [the longest x7 23.2 us: across(): return lax.ppermute(value, ROW, [(i, i ^ 2 * dx + dl) for i in range(4)])]
    pallas_call x3 -> x10, Pallas kernels: 4.81 us -> 17.6 us  [the longest x7 12.8 us: run_blocks(): pl.pallas_call(kernel, grid=(steps,), in_specs=[spec(block, axis) for _,...]
  transfers between devices with their start and end apart: 13 -> 19, of which waited for: 10 -> 11; matrix products, arithmetic and copies ran while one was open for 1% -> 2% of each run, Pallas kernels for 1% -> 5%
where the time goes in v2:
time: 228 us; the launch traced here: 227 us
  starting transfers between devices  86.6 us (38%)
  waiting for transfers between devices  81.9 us (36%)
  local copies, waits for them, and re-layouts  22.9 us (10%)
  Pallas kernels  17.6 us (8%)
  between operations  15.9 us (7%)
    ppermute x7, starting transfers between devices, across(): return lax.ppermute(value, ROW, [(i, i ^ 2 * dx + dl) for i in range(4)])  23.2 us
    all_to_all x1, starting transfers between devices, per_device(): lax.all_to_all(product.reshape(BLOCKS, CHANNELS, LANES), SEQ, 0, 0, tiled...  22.5 us
    all_to_all x1, waiting for transfers between devices, per_device(): lax.all_to_all(product.reshape(BLOCKS, CHANNELS, LANES), SEQ, 0, 0, tiled...  22.4 us
    unnamed x57, local copies, waits for them, and re-layouts  20.7 us
    ppermute x7, waiting for transfers between devices, across(): return lax.ppermute(value, ROW, [(i, i ^ 2 * dx + dl) for i in range(4)])  17.8 us
    pallas_call x7, Pallas kernels, run_blocks(): pl.pallas_call(kernel, grid=(steps,), in_specs=[spec(block, axis) for _,...  12.8 us
    all_gather x1, waiting for transfers between devices, per_device(): lax.all_gather(jnp.stack([keep, across(send, 1, 0)]), 'y', axis=0)  12.2 us
    all_to_all x1, waiting for transfers between devices, per_device(): lax.all_to_all(long_grad.reshape(BLOCKS, CHANNELS, LANES), SEQ, 0, 0, til...  11.6 us
  transfers between devices with their start and end apart: 19, of which 11 were waited for; matrix products, arithmetic and copies ran while one was open for 2% of the time, Pallas kernels for 5%

profile of v2, /device:TPU:1, one launch (start us, length us, event | category | flops | bytes accessed | tf_op | source)
XLA Modules:
  0.0 226.8 jit_solution(4492969822647493205)
XLA Ops:
  8.1 6.0 %collective-permute-start.2 = (bf16[128,512]{1,0:T(8,128)(2,1)}, bf16[128,512]{1,0:T(8,128)(2,1)S(1)}, u32[]{:S(2)}, u32[]{:S(2)}) collective-permute-start(bf16[128,512]{1,0:T(8,128)(2,1)} %param.14), channel_id=1, source_target_pairs={{0,0},{4,8},{8,256},{12,264},{256,4},{260,12},{264,260},{268,268},... | collective-permute-start | bytes 393224 | tf_op jit(solution)/shard_map/ppermute | solution.py:274
  14.1 2.2 collective-permute-done.2
  18.5 1.9 collective-permute-start
  20.5 1.1 collective-permute-done.before_ref
  22.4 0.9 copy-done.23
  23.4 0.9 copy-done.24
  24.3 0.9 copy-done.25
  25.3 2.1 shard_map.128
  27.4 0.8 copy-done.12
  28.2 0.9 copy-done.14
  29.1 22.5 %all-to-all-start = ((bf16[64,16,128]{2,1,0:T(8,128)(2,1)}), bf16[64,16,128]{2,1,0:T(8,128)(2,1)S(1)}, u32[]{:S(2)}, u32[]{:S(2)}) async-start(bf16[64,16,128]{2,1,0:T(8,128)(2,1)} %bitcast.3), calls=%async_computation | async-start | bytes 524288 | tf_op jit(solution)/shard_map/all_to_all | solution.py:296
  51.6 1.0 copy-done.4
  53.4 1.0 copy-done.18
  55.0 22.4 %all-to-all-done.product_ref = bf16[64,16,128]{2,1,0:T(8,128)(2,1)S(1)} async-done(((bf16[64,16,128]{2,1,0:T(8,128)(2,1)}), bf16[64,16,128]{2,1,0:T(8,128)(2,1)S(1)}, u32[]{:S(2)}, u32[]{:S(2)}) %all-to-all-start) | async-done | bytes 262176 | tf_op jit(solution)/shard_map/all_to_all | solution.py:296
  77.4 1.0 copy-done.5
  79.2 1.8 shard_map.130
  81.0 1.0 copy-done.7
  82.0 4.6 %all-to-all-start.1 = ((bf16[64,16,128]{2,1,0:T(8,128)(2,1)}), bf16[64,16,128]{2,1,0:T(8,128)(2,1)S(1)}, u32[]{:S(2)}, u32[]{:S(2)}) async-start(bf16[64,16,128]{2,1,0:T(8,128)(2,1)} %get-tuple-element.20), calls=%async_computation.1 | async-start | bytes 524288 | tf_op jit(solution)/shard_map/all_to_all | solution.py:306
  86.6 4.9 %collective-permute-start.7 = (bf16[128,512]{1,0:T(8,128)(2,1)S(1)}, bf16[128,512]{1,0:T(8,128)(2,1)S(1)}, u32[]{:S(2)}, u32[]{:S(2)}) collective-permute-start(bf16[128,512]{1,0:T(8,128)(2,1)S(1)} %copy-done.27), channel_id=1, source_target_pairs={{0,256},{4,260},{256,0},{260,4},{1,257},{5,261},{257,1},{261,5},{2... | collective-permute-start | bytes 393224 | tf_op jit(solution)/shard_map/ppermute | solution.py:265
  91.5 1.9 collective-permute-start.8
  93.4 1.9 collective-permute-start.6
  95.4 4.6 %collective-permute-done.8 = bf16[128,512]{1,0:T(8,128)(2,1)S(1)} collective-permute-done((bf16[128,512]{1,0:T(8,128)(2,1)S(1)}, bf16[128,512]{1,0:T(8,128)(2,1)S(1)}, u32[]{:S(2)}, u32[]{:S(2)}) %collective-permute-start.8) | collective-permute-done | bytes 131104 | tf_op jit(solution)/shard_map/ppermute | solution.py:265
  100.9 9.9 %all-to-all-done.1 = bf16[64,16,128]{2,1,0:T(8,128)(2,1)S(1)} async-done(((bf16[64,16,128]{2,1,0:T(8,128)(2,1)}), bf16[64,16,128]{2,1,0:T(8,128)(2,1)S(1)}, u32[]{:S(2)}, u32[]{:S(2)}) %all-to-all-start.1) | async-done | bytes 262176 | tf_op jit(solution)/shard_map/all_to_all | solution.py:306
  111.4 2.4 %copy-done = bf16[4096,512]{1,0:T(8,128)(2,1)S(1)} copy-done((bf16[4096,512]{1,0:T(8,128)(2,1)S(1)}, bf16[4096,512]{1,0:T(8,128)(2,1)}, u32[]{:S(2)}) %copy-start) | copy-done | bytes 4194328
  113.8 2.9 %shard_map.133 = bf16[2,4,128,512]{3,2,1,0:T(8,128)(2,1)} custom-call(bf16[2,2,128,512]{3,2,1,0:T(8,128)(2,1)S(1)} %reverse_select_fusion.gradient_ref, bf16[16,2,128,512]{3,2,1,0:T(8,128)(2,1)S(1)} %bitcast.41, bf16[2,128,512]{2,1,0:T(8,128)(2,1)S(1)} %get-tuple-element.22._), custom_call_target="tpu_custom_call" | custom-call | flops 1073741824 | bytes 6291456 | tf_op jit(solution)/shard_map/pallas_call | solution.py:148
  116.7 4.7 %all-to-all-start.2 = ((bf16[8,128,512]{2,1,0:T(8,128)(2,1)}), bf16[8,128,512]{2,1,0:T(8,128)(2,1)S(1)}, u32[]{:S(2)}, u32[]{:S(2)}) async-start(bf16[8,128,512]{2,1,0:T(8,128)(2,1)} %bitcast.19), calls=%async_computation.2 | async-start | bytes 2097152 | tf_op jit(solution)/shard_map/all_to_all | solution.py:319
  121.5 4.8 %collective-permute-start.1 = (bf16[128,512]{1,0:T(8,128)(2,1)S(1)}, bf16[128,512]{1,0:T(8,128)(2,1)S(1)}, u32[]{:S(2)}, u32[]{:S(2)}) collective-permute-start(bf16[128,512]{1,0:T(8,128)(2,1)S(1)} %get-tuple-element.37), channel_id=1, source_target_pairs={{0,256},{4,260},{256,0},{260,4},{1,257},{5,261},{257,1},{261,5},{2... | collective-permute-start | bytes 393224 | tf_op jit(solution)/shard_map/ppermute | solution.py:265
  126.3 12.6 %collective-permute-done.1 = bf16[128,512]{1,0:T(8,128)(2,1)S(1)} collective-permute-done((bf16[128,512]{1,0:T(8,128)(2,1)S(1)}, bf16[128,512]{1,0:T(8,128)(2,1)S(1)}, u32[]{:S(2)}, u32[]{:S(2)}) %collective-permute-start.1) | collective-permute-done | bytes 131104 | tf_op jit(solution)/shard_map/ppermute | solution.py:265
  139.6 1.0 copy-done.20
  140.7 1.8 shard_map.134
  143.3 10.4 %all-to-all-start.3 = ((bf16[64,16,128]{2,1,0:T(8,128)(2,1)}), bf16[64,16,128]{2,1,0:T(8,128)(2,1)S(1)}, u32[]{:S(2)}, u32[]{:S(2)}) async-start(bf16[64,16,128]{2,1,0:T(8,128)(2,1)} %bitcast.20), calls=%async_computation.3 | async-start | bytes 524288 | tf_op jit(solution)/shard_map/all_to_all | solution.py:325
  153.7 12.2 %all-gather.5.cloned.1.call-done = bf16[8,128,512]{2,1,0:T(8,128)(2,1)} async-done(((bf16[2,128,512]{2,1,0:T(8,128)(2,1)}), bf16[8,128,512]{2,1,0:T(8,128)(2,1)}) %all-gather.5.cloned.1.call-update) | async-done | bytes 1048592 | tf_op jit(solution)/shard_map/all_gather | solution.py:329
  165.8 11.6 %all-to-all-done.3.grad_ref = bf16[64,16,128]{2,1,0:T(8,128)(2,1)S(1)} async-done(((bf16[64,16,128]{2,1,0:T(8,128)(2,1)}), bf16[64,16,128]{2,1,0:T(8,128)(2,1)S(1)}, u32[]{:S(2)}, u32[]{:S(2)}) %all-to-all-start.3) | async-done | bytes 262176 | tf_op jit(solution)/shard_map/all_to_all | solution.py:325
  177.4 1.2 copy-done.2
  178.7 1.2 copy-done.8
  179.9 2.5 %shard_map.136 = (bf16[64,16,128]{2,1,0:T(8,128)(2,1)}, f32[16,8192]{1,0:T(8,128)}) custom-call(bf16[64,16,128]{2,1,0:T(8,128)(2,1)S(1)} %all-to-all-done.3.grad_ref, f32[1024,256]{1,0:T(8,128)S(1)} %shard_map.129.filter_spectrum, f32[1024,256]{1,0:T(8,128)S(1)} %copy-done.8, bf16[4,2,128,512]{3,2,1,0:T(8,128)(2,1)S(1)} %bitcast.43, ...), custom_call_target="tpu_custom_call" | custom-call | flops 503316480 | bytes 4194304 | tf_op jit(solution)/shard_map/pallas_call | solution.py:130
  182.4 6.3 %all-to-all-start.4 = ((bf16[64,16,128]{2,1,0:T(8,128)(2,1)}), bf16[64,16,128]{2,1,0:T(8,128)(2,1)S(1)}, u32[]{:S(2)}, u32[]{:S(2)}) async-start(bf16[64,16,128]{2,1,0:T(8,128)(2,1)} %get-tuple-element.27), calls=%async_computation.4 | async-start | bytes 524288 | tf_op jit(solution)/shard_map/all_to_all | solution.py:358
  188.7 2.2 copy-done.1
  190.9 1.9 shard_map.132
  192.9 2.2 collective-permute-start.3
  195.1 5.5 %collective-permute-start.4 = (bf16[128,512]{1,0:T(8,128)(2,1)S(1)}, bf16[128,512]{1,0:T(8,128)(2,1)S(1)}, u32[]{:S(2)}, u32[]{:S(2)}) collective-permute-start(bf16[128,512]{1,0:T(8,128)(2,1)S(1)} %get-tuple-element.35), channel_id=1, source_target_pairs={{0,256},{4,260},{256,0},{260,4},{1,257},{5,261},{257,1},{261,5},{2... | collective-permute-start | bytes 393224 | tf_op jit(solution)/shard_map/ppermute | solution.py:265
  200.6 1.9 collective-permute-start.5
  202.6 3.2 %collective-permute-start.11 = (f32[2,2,1024]{2,1,0:T(2,128)S(1)}, f32[2,2,1024]{2,1,0:T(2,128)S(1)}, u32[]{:S(2)}, u32[]{:S(2)}) collective-permute-start(f32[2,2,1024]{2,1,0:T(2,128)S(1)} %pad_maximum_fusion.2), channel_id=1, source_target_pairs={{8,0},{16,8},{24,16},{32,24},{40,32},{48,40},{56,48},{64,56},{72,6... | collective-permute-start | bytes 49160 | tf_op jit(solution)/shard_map/ppermute | solution.py:259
  206.5 1.9 collective-permute-start.9
  208.4 3.9 %all-to-all-done.4 = bf16[64,16,128]{2,1,0:T(8,128)(2,1)S(1)} async-done(((bf16[64,16,128]{2,1,0:T(8,128)(2,1)}), bf16[64,16,128]{2,1,0:T(8,128)(2,1)S(1)}, u32[]{:S(2)}, u32[]{:S(2)}) %all-to-all-start.4) | async-done | bytes 262176 | tf_op jit(solution)/shard_map/all_to_all | solution.py:358
  212.5 1.9 collective-permute-start.10
  215.2 1.5 shard_map.135
  217.4 1.9 shard_map.137
  (76 shorter events, 11.0 us)
Async XLA Ops:
  8.0 78.6 %copy-start.27 = (bf16[128,512]{1,0:T(8,128)(2,1)S(1)}, bf16[128,512]{1,0:T(8,128)(2,1)}, u32[]{:S(2)}) copy-start(bf16[128,512]{1,0:T(8,128)(2,1)} %param.15) | copy-start | bytes 393220
  8.0 103.4 %all-gather.7.cloned.1.call-start = ((), (), s32[]{:S(2)}) async-start(), calls=%async_computation.6 | async-start | bytes 4325376 | tf_op jit(solution)/shard_map/all_gather | solution.py:279
  8.1 8.3 %collective-permute-start.2 = (bf16[128,512]{1,0:T(8,128)(2,1)}, bf16[128,512]{1,0:T(8,128)(2,1)S(1)}, u32[]{:S(2)}, u32[]{:S(2)}) collective-permute-start(bf16[128,512]{1,0:T(8,128)(2,1)} %param.14), channel_id=1, source_target_pairs={{0,0},{4,8},{8,256},{12,264},{256,4},{260,12},{264,260},{268,268},... | collective-permute-start | bytes 393224 | tf_op jit(solution)/shard_map/ppermute | solution.py:274
  16.3 0.7 copy-start.26
  18.5 3.1 %collective-permute-start = (bf16[3,2,1024]{2,1,0:T(2,128)(2,1)S(1)}, bf16[3,2,1024]{2,1,0:T(2,128)(2,1)S(1)}, u32[]{:S(2)}, u32[]{:S(2)}) collective-permute-start(bf16[3,2,1024]{2,1,0:T(2,128)(2,1)S(1)} %pad_maximum_fusion.3), channel_id=1, source_target_pairs={{0,8},{8,16},{16,24},{24,32},{32,40},{40,48},{48,56},{56,64},{64,7... | collective-permute-start | bytes 36872 | tf_op jit(solution)/shard_map/ppermute | solution.py:259
  21.6 0.8 copy-start.21
  22.4 0.9 copy-start.23
  23.4 0.9 copy-start.24
  24.3 0.9 copy-start.25
  27.4 0.8 copy-start.12
  28.2 0.9 copy-start.14
  29.1 48.3 %all-to-all-start = ((bf16[64,16,128]{2,1,0:T(8,128)(2,1)}), bf16[64,16,128]{2,1,0:T(8,128)(2,1)S(1)}, u32[]{:S(2)}, u32[]{:S(2)}) async-start(bf16[64,16,128]{2,1,0:T(8,128)(2,1)} %bitcast.3), calls=%async_computation | async-start | bytes 524288 | tf_op jit(solution)/shard_map/all_to_all | solution.py:296
  51.6 1.0 copy-start.4
  52.6 0.8 copy-start.9
  53.4 1.0 copy-start.18
  77.4 1.0 copy-start.5
  78.4 0.8 copy-start.10
  81.0 1.0 copy-start.7
  82.0 28.8 %all-to-all-start.1 = ((bf16[64,16,128]{2,1,0:T(8,128)(2,1)}), bf16[64,16,128]{2,1,0:T(8,128)(2,1)S(1)}, u32[]{:S(2)}, u32[]{:S(2)}) async-start(bf16[64,16,128]{2,1,0:T(8,128)(2,1)} %get-tuple-element.20), calls=%async_computation.1 | async-start | bytes 524288 | tf_op jit(solution)/shard_map/all_to_all | solution.py:306
  86.6 8.8 %collective-permute-start.7 = (bf16[128,512]{1,0:T(8,128)(2,1)S(1)}, bf16[128,512]{1,0:T(8,128)(2,1)S(1)}, u32[]{:S(2)}, u32[]{:S(2)}) collective-permute-start(bf16[128,512]{1,0:T(8,128)(2,1)S(1)} %copy-done.27), channel_id=1, source_target_pairs={{0,256},{4,260},{256,0},{260,4},{1,257},{5,261},{257,1},{261,5},{2... | collective-permute-start | bytes 393224 | tf_op jit(solution)/shard_map/ppermute | solution.py:265
  91.5 8.4 %collective-permute-start.8 = (bf16[128,512]{1,0:T(8,128)(2,1)S(1)}, bf16[128,512]{1,0:T(8,128)(2,1)S(1)}, u32[]{:S(2)}, u32[]{:S(2)}) collective-permute-start(bf16[128,512]{1,0:T(8,128)(2,1)S(1)} %copy-done.27), channel_id=1, source_target_pairs={{0,260},{4,256},{256,4},{260,0},{1,261},{5,257},{257,5},{261,1},{2... | collective-permute-start | bytes 393224 | tf_op jit(solution)/shard_map/ppermute | solution.py:265
  93.4 7.2 %collective-permute-start.6 = (bf16[128,512]{1,0:T(8,128)(2,1)S(1)}, bf16[128,512]{1,0:T(8,128)(2,1)S(1)}, u32[]{:S(2)}, u32[]{:S(2)}) collective-permute-start(bf16[128,512]{1,0:T(8,128)(2,1)S(1)} %copy-done.27), channel_id=1, source_target_pairs={{0,4},{4,0},{256,260},{260,256},{1,5},{5,1},{257,261},{261,257},{2... | collective-permute-start | bytes 393224 | tf_op jit(solution)/shard_map/ppermute | solution.py:265
  111.4 5.3 %copy-start.19 = (f32[128,1024]{1,0:T(8,128)}, f32[128,1024]{1,0:T(8,128)S(1)}, u32[]{:S(2)}) copy-start(f32[128,1024]{1,0:T(8,128)S(1)} %get-tuple-element.23.long_ref) | copy-start | bytes 1572868
  111.4 2.4 %copy-start = (bf16[4096,512]{1,0:T(8,128)(2,1)S(1)}, bf16[4096,512]{1,0:T(8,128)(2,1)}, u32[]{:S(2)}) copy-start(bf16[4096,512]{1,0:T(8,128)(2,1)} %all-gather.7.cloned.1.call-done) | copy-start | bytes 12582916
  116.7 60.8 %copy-start.6 = (bf16[256,640]{1,0:T(8,128)(2,1)S(1)}, bf16[256,640]{1,0:T(8,128)(2,1)}, u32[]{:S(2)}) copy-start(bf16[256,640]{1,0:T(8,128)(2,1)} %constant.16.clone.steps) | copy-start | bytes 983044
  116.7 60.8 %copy-start.11 = (f32[64,256]{1,0:T(8,128)S(1)}, f32[64,256]{1,0:T(8,128)}, u32[]{:S(2)}) copy-start(f32[64,256]{1,0:T(8,128)} %constant.17.clone.turns) | copy-start | bytes 196612
  116.7 22.9 %all-to-all-start.2 = ((bf16[8,128,512]{2,1,0:T(8,128)(2,1)}), bf16[8,128,512]{2,1,0:T(8,128)(2,1)S(1)}, u32[]{:S(2)}, u32[]{:S(2)}) async-start(bf16[8,128,512]{2,1,0:T(8,128)(2,1)} %bitcast.19), calls=%async_computation.2 | async-start | bytes 2097152 | tf_op jit(solution)/shard_map/all_to_all | solution.py:319
  121.4 44.4 %all-gather.5.cloned.1.call-start = ((), (), s32[]{:S(2)}) async-start(), calls=%async_computation.5 | async-start | bytes 1310720 | tf_op jit(solution)/shard_map/all_gather | solution.py:329
  121.5 17.4 %collective-permute-start.1 = (bf16[128,512]{1,0:T(8,128)(2,1)S(1)}, bf16[128,512]{1,0:T(8,128)(2,1)S(1)}, u32[]{:S(2)}, u32[]{:S(2)}) collective-permute-start(bf16[128,512]{1,0:T(8,128)(2,1)S(1)} %get-tuple-element.37), channel_id=1, source_target_pairs={{0,256},{4,260},{256,0},{260,4},{1,257},{5,261},{257,1},{261,5},{2... | collective-permute-start | bytes 393224 | tf_op jit(solution)/shard_map/ppermute | solution.py:265
  139.6 1.0 copy-start.20
  142.5 0.8 copy-start.16
  143.3 45.4 %copy-start.15 = (f32[128,1024]{1,0:T(8,128)S(1)}, f32[128,1024]{1,0:T(8,128)}, u32[]{:S(2)}) copy-start(f32[128,1024]{1,0:T(8,128)} %copy-done.14) | copy-start | bytes 1572868
  143.3 34.1 %all-to-all-start.3 = ((bf16[64,16,128]{2,1,0:T(8,128)(2,1)}), bf16[64,16,128]{2,1,0:T(8,128)(2,1)S(1)}, u32[]{:S(2)}, u32[]{:S(2)}) async-start(bf16[64,16,128]{2,1,0:T(8,128)(2,1)} %bitcast.20), calls=%async_computation.3 | async-start | bytes 524288 | tf_op jit(solution)/shard_map/all_to_all | solution.py:325
  177.4 1.2 copy-start.2
  178.6 1.2 copy-start.8
  179.9 8.8 %copy-start.3 = (bf16[8,128,512]{2,1,0:T(8,128)(2,1)S(1)}, bf16[8,128,512]{2,1,0:T(8,128)(2,1)}, u32[]{:S(2)}) copy-start(bf16[8,128,512]{2,1,0:T(8,128)(2,1)} %all-gather.5.cloned.1.call-done) | copy-start | bytes 3145732
  182.3 20.2 %copy-start.13 = (f32[128,1024]{1,0:T(8,128)S(1)}, f32[128,1024]{1,0:T(8,128)}, u32[]{:S(2)}) copy-start(f32[128,1024]{1,0:T(8,128)} %copy-done.12) | copy-start | bytes 1572868
  182.4 30.0 %all-to-all-start.4 = ((bf16[64,16,128]{2,1,0:T(8,128)(2,1)}), bf16[64,16,128]{2,1,0:T(8,128)(2,1)S(1)}, u32[]{:S(2)}, u32[]{:S(2)}) async-start(bf16[64,16,128]{2,1,0:T(8,128)(2,1)} %get-tuple-element.27), calls=%async_computation.4 | async-start | bytes 524288 | tf_op jit(solution)/shard_map/all_to_all | solution.py:358
  188.7 2.2 copy-start.1
  190.9 24.3 %copy-start.17 = (f32[128,1024]{1,0:T(8,128)S(1)}, f32[128,1024]{1,0:T(8,128)}, u32[]{:S(2)}) copy-start(f32[128,1024]{1,0:T(8,128)} %copy-done.16) | copy-start | bytes 1572868
  190.9 24.3 %copy-start.22 = (f32[3,3,1024]{2,1,0:T(4,128)S(1)}, f32[3,3,1024]{2,1,0:T(4,128)}, u32[]{:S(2)}) copy-start(f32[3,3,1024]{2,1,0:T(4,128)} %taps_ref.5) | copy-start | bytes 110596
  192.9 19.6 %collective-permute-start.3 = (bf16[128,512]{1,0:T(8,128)(2,1)S(1)}, bf16[128,512]{1,0:T(8,128)(2,1)S(1)}, u32[]{:S(2)}, u32[]{:S(2)}) collective-permute-start(bf16[128,512]{1,0:T(8,128)(2,1)S(1)} %get-tuple-element.33), channel_id=1, source_target_pairs={{0,4},{4,0},{256,260},{260,256},{1,5},{5,1},{257,261},{261,257},{2... | collective-permute-start | bytes 393224 | tf_op jit(solution)/shard_map/ppermute | solution.py:265
  195.1 19.3 %collective-permute-start.4 = (bf16[128,512]{1,0:T(8,128)(2,1)S(1)}, bf16[128,512]{1,0:T(8,128)(2,1)S(1)}, u32[]{:S(2)}, u32[]{:S(2)}) collective-permute-start(bf16[128,512]{1,0:T(8,128)(2,1)S(1)} %get-tuple-element.35), channel_id=1, source_target_pairs={{0,256},{4,260},{256,0},{260,4},{1,257},{5,261},{257,1},{261,5},{2... | collective-permute-start | bytes 393224 | tf_op jit(solution)/shard_map/ppermute | solution.py:265
  200.6 13.8 %collective-permute-start.5 = (bf16[128,512]{1,0:T(8,128)(2,1)S(1)}, bf16[128,512]{1,0:T(8,128)(2,1)S(1)}, u32[]{:S(2)}, u32[]{:S(2)}) collective-permute-start(bf16[128,512]{1,0:T(8,128)(2,1)S(1)} %get-tuple-element.34), channel_id=1, source_target_pairs={{0,260},{4,256},{256,4},{260,0},{1,261},{5,257},{257,5},{261,1},{2... | collective-permute-start | bytes 393224 | tf_op jit(solution)/shard_map/ppermute | solution.py:265
  202.6 14.1 %collective-permute-start.11 = (f32[2,2,1024]{2,1,0:T(2,128)S(1)}, f32[2,2,1024]{2,1,0:T(2,128)S(1)}, u32[]{:S(2)}, u32[]{:S(2)}) collective-permute-start(f32[2,2,1024]{2,1,0:T(2,128)S(1)} %pad_maximum_fusion.2), channel_id=1, source_target_pairs={{8,0},{16,8},{24,16},{32,24},{40,32},{48,40},{56,48},{64,56},{72,6... | collective-permute-start | bytes 49160 | tf_op jit(solution)/shard_map/ppermute | solution.py:259
  206.5 8.7 %collective-permute-start.9 = (f32[2,1024]{1,0:T(2,128)S(1)}, f32[2,1024]{1,0:T(2,128)S(1)}, u32[]{:S(2)}, u32[]{:S(2)}) collective-permute-start(f32[2,1024]{1,0:T(2,128)S(1)} %slice.50), channel_id=1, source_target_pairs={{8,0},{16,8},{24,16},{32,24},{40,32},{48,40},{56,48},{64,56},{72,6... | collective-permute-start | bytes 24584 | tf_op jit(solution)/shard_map/ppermute | solution.py:259
  212.5 4.9 %collective-permute-start.10 = (bf16[2,1024]{1,0:T(2,128)(2,1)S(1)}, bf16[2,1024]{1,0:T(2,128)(2,1)S(1)}, u32[]{:S(2)}, u32[]{:S(2)}) collective-permute-start(bf16[2,1024]{1,0:T(2,128)(2,1)S(1)} %bitcast.53), channel_id=1, source_target_pairs={{8,0},{16,8},{24,16},{32,24},{40,32},{48,40},{56,48},{64,56},{72,6... | collective-permute-start | bytes 12296 | tf_op jit(solution)/shard_map/ppermute | solution.py:259
Sparse Core Ops, SparseCore 0:
  17.1 93.6 all-gather.6
Sparse Core Ops, SparseCore 1:
  139.7 26.1 all-gather.4

commit v3 on v2

--- a/solution.py
+++ b/solution.py
@@ -12,16 +12,19 @@
 BF16 = jnp.bfloat16
 F32 = jnp.float32
 
-SEQ = ("xh", "z", "co")
-TP = ("xl", "y")
-ROW = ("xh", "xl")
-PLANE = ("xh", "y")
-COLUMN = ("z", "co")
+AXES = {"xh": 2, "zy": 4, "zh": 2, "zb": 2, "co": 2, "xl": 2, "yh": 2, "yl": 2}
+SEQ = ("xh", "zy", "zh", "zb", "co")
+TP = ("xl", "yh", "yl")
+PLANE = ("xh", "yh", "yl")
+COLUMN = ("zy", "zh", "zb", "co")
 
 CHANNELS = 16
 BLOCKS = 64
 LANES = 128
 LENGTH = BLOCKS * LANES
+
+VMEM_LIMIT = 20 * 2**20
+WHOLE_VMEM = 60 * 2**20
 
 
 def transform_tables():
@@ -93,7 +96,7 @@
 
 
 def backward_kernel(
-    grad_ref, filter_spectrum, product_spectrum, _, steps, turns,
+    grad_ref, filter_spectrum, product_spectrum, steps, turns,
     back_ref, filter_grad_ref, grid, turned, section,
 ):
     grid[...] = grad_ref[...].astype(F32).reshape(BLOCKS * CHANNELS, LANES)
@@ -132,18 +135,21 @@
         out_shape=out_shape,
         in_specs=in_specs,
         scratch_shapes=scratch,
-        compiler_params=pltpu.CompilerParams(vmem_limit_bytes=20 * 2**20),
+        compiler_params=pltpu.CompilerParams(vmem_limit_bytes=VMEM_LIMIT),
         cost_estimate=pl.CostEstimate(
             flops=transforms * transform_flops, bytes_accessed=4 * 2**20, transcendentals=0
         ),
     )(*operands)
 
 
-def run_blocks(kernel, steps, ins, outs, moved, flops=10**6, scratch=()):
+def run_blocks(kernel, steps, ins, outs, moved, flops=10**6, scratch=(), limit=VMEM_LIMIT):
     def spec(block, axis):
         if block is None:
-            return pl.BlockSpec(memory_space=pl.ANY)
-        return pl.BlockSpec(block, lambda i: tuple(i if d == axis else 0 for d in range(len(block))))
+            return pl.BlockSpec(memory_space=axis or pl.ANY)
+        fixed = (0,) * len(block)
+        if isinstance(block[0], tuple):
+            block, fixed = block[0], (0,) * (len(block[0]) - 3) + (block[1][1],) + (0, 0)
+        return pl.BlockSpec(block, lambda i: tuple(i if d == axis else fixed[d] for d in range(len(block))))
 
     return pl.pallas_call(
         kernel,
@@ -152,7 +158,7 @@
         out_specs=[spec(block, axis) for _, _, block, axis in outs],
         out_shape=[jax.ShapeDtypeStruct(shape, dtype) for shape, dtype, _, _ in outs],
         scratch_shapes=list(scratch),
-        compiler_params=pltpu.CompilerParams(vmem_limit_bytes=20 * 2**20),
+        compiler_params=pltpu.CompilerParams(vmem_limit_bytes=limit),
         cost_estimate=pl.CostEstimate(flops=flops, bytes_accessed=moved, transcendentals=0),
     )(*[array for array, _, _ in ins])
 
@@ -191,36 +197,42 @@
     long = long_ref[...].astype(F32).T
     out_ref[...] = long
     gated = (qc_ref[...] * long).astype(BF16)
-    gated_ref[0] = gated[:, :LANES]
-    gated_ref[1] = gated[:, LANES:]
-
-
-def partial_kernel(gradient_ref, weight_ref, _, out_ref):
-    halves, groups, rows, features = gradient_ref.shape
-    width = weight_ref.shape[0] * weight_ref.shape[2]
-    total = jnp.zeros((halves * rows, width), F32)
-    for f in range(groups):
-        total += lax.dot_general(
-            gradient_ref[:, f].reshape(halves * rows, features),
-            weight_ref[:, f].reshape(width, features),
-            (((1,), (1,)), ((), ())),
-            preferred_element_type=F32,
-        )
-    out_ref[...] = total.astype(BF16).reshape(out_ref.shape)
+    for zb in range(2):
+        for co in range(2):
+            start = (2 * zb + co) * LANES
+            gated_ref[co, zb] = gated[:, start : start + LANES]
+
+
+def partial_kernel(place_ref, gradient_ref, weight_ref, gated_ref, out_ref):
+    xh, xl, yl = place_ref[0], place_ref[1], place_ref[3]
+    rows, features = gradient_ref.shape[3:]
+    width = out_ref.shape[4]
+    total = jnp.zeros((2 * rows, width), F32)
+    for e in range(2):
+        for f in range(2):
+            total += lax.dot_general(
+                gradient_ref[e ^ yl, f ^ xl].reshape(2 * rows, features),
+                weight_ref[0, :, e, f].reshape(width, features),
+                (((1,), (1,)), ((), ())),
+                preferred_element_type=F32,
+            )
+    for t in range(2):
+        out_ref[t ^ xh, 0, 0] = total[t * rows : (t + 1) * rows].astype(BF16)
+        out_ref[t, 0, 1] = gated_ref[t, pl.program_id(0) % 2]
 
 
 def long_gradient(parts_ref, qc_ref, long_ref, grad_ref, qg_ref):
-    parts = parts_ref[...].astype(F32)
+    parts = parts_ref[...].astype(F32).reshape(8, *qg_ref.shape[:1], LANES)
     gated_grad = jnp.concatenate(
-        [(parts[r] + parts[r + 1]) + (parts[r + 2] + parts[r + 3]) for r in (0, 4)], axis=1
+        [parts[4 * r + e] + parts[4 * r + 2 + e] for e in range(2) for r in range(2)], axis=1
     )
     grad_ref[...] = (qc_ref[...] * gated_grad).T.astype(BF16)
     qg_ref[...] = gated_grad * long_ref[...]
 
 
 def mix_kernel(gated_ref, weight_ref, out_ref, total):
-    halves, rows, width = gated_ref.shape[1:]
-    groups, features = weight_ref.shape[1], weight_ref.shape[3]
+    halves, _, _, rows, width = gated_ref.shape
+    features = weight_ref.shape[5]
     step = pl.program_id(0)
 
     @pl.when(step == 0)
@@ -228,14 +240,18 @@
         total[...] = jnp.zeros_like(total)
 
     gated = gated_ref[...].reshape(halves * rows, width)
-    for f in range(groups):
-        total[f] += jnp.dot(
-            gated, weight_ref[:, f].reshape(width, features), preferred_element_type=F32
-        )
+    for e in range(2):
+        for f in range(2):
+            total[2 * e + f] += jnp.dot(
+                gated, weight_ref[0, :, e, f].reshape(width, features), preferred_element_type=F32
+            )
 
     @pl.when(step == pl.num_programs(0) - 1)
     def _():
-        out_ref[...] = total[...].astype(BF16).reshape(out_ref.shape)
+        for e in range(2):
+            for f in range(2):
+                for t in range(2):
+                    out_ref[t, f, e] = total[2 * e + f, t * rows : (t + 1) * rows].astype(BF16)
 
 
 def query_adjoint(qg_ref, after_ref, taps_ref, out_ref):
@@ -259,26 +275,37 @@
     return lax.ppermute(value, SEQ, [(i, i + steps) for i in range(first, last)])
 
 
+def partner(value, axis):
+    return lax.ppermute(value, axis, [(0, 1), (1, 0)])
+
+
 def across(value, dx, dl):
     if not (dx or dl):
         return value
-    return lax.ppermute(value, ROW, [(i, i ^ (2 * dx + dl)) for i in range(4)])
+    return lax.ppermute(value, ("xh", "xl"), [(i, i ^ (2 * dx + dl)) for i in range(4)])
+
+
+def turn(value):
+    pairs = []
+    for i in range(32):
+        a, s, c, b, e = ((i >> k) & 1 for k in (4, 3, 2, 1, 0))
+        pairs.append((i, 16 * c + 8 * e + 4 * b + 2 * a + s))
+    return lax.ppermute(value, ("xh", "zb", "co", "xl", "yl"), pairs)
 
 
 def per_device(queries, keys, values, short_taps, long_filter, out_weight, cotangent):
     rows, width = queries.shape
     features = out_weight.shape[1]
-    own_xh, own_xl = lax.axis_index("xh"), lax.axis_index("xl")
+    place = jnp.stack([lax.axis_index(axis) for axis in ("xh", "xl", "yh", "yl")])
+    place = (place.astype(jnp.int32), None, pltpu.SMEM)
     kinds, chunk = 4, width // 4
 
-    turned = lax.ppermute(
-        out_weight,
-        ("xh", "co", "xl"),
-        [(4 * a + 2 * c + b, 4 * c + 2 * b + a) for a in range(2) for c in range(2) for b in range(2)],
-    )
-    weight = lax.all_gather(turned, COLUMN, axis=0).reshape(16, 2, rows, features)
-
-    before = shift(jnp.stack([x[rows - 2 :] for x in (queries, keys, values)]), 1)
+    rims = jnp.stack([x[rows - 2 :] for x in (queries, keys, values)])
+    rims, out_weight = lax.optimization_barrier((rims, out_weight))
+    before, turned = lax.optimization_barrier((shift(rims, 1), turn(out_weight)))
+    weight = lax.all_gather(turned, COLUMN, axis=0).reshape(4, 2, 2, 2, rows, features)
+    weight = pltpu.with_memory_space_constraint(weight, pltpu.HBM)
+
     steps, turns = transform_tables()
     filter_spectrum = run_kernel(filter_kernel, SPECTRUM, [GRID, TURNED], 1, long_filter, steps, turns)
 
@@ -290,7 +317,7 @@
         filter_inputs, kinds,
         [(queries, tokens, 1), (keys, tokens, 1), (values, tokens, 1),
          (before, (3, 2, chunk), 2), (short_taps, taps_block, 2)],
-        [plane, plane, plane, ((width, rows), BF16, channels, 0)], 3 * 2**20,
+        [plane, plane, plane, ((width, rows), BF16, channels, 0)], 3 * 2**20, limit=WHOLE_VMEM,
     )
 
     product_owned = lax.all_to_all(product.reshape(BLOCKS, CHANNELS, LANES), SEQ, 0, 0, tiled=True)
@@ -298,54 +325,49 @@
         forward_kernel, [SEQUENCES, SPECTRUM], [GRID, TURNED, SECTION], 2,
         product_owned, filter_spectrum, steps, turns,
     )
-    blocks = [[across(cotangent, dx, dl) for dl in range(2)] for dx in range(2)]
-    gradient = jnp.stack([jnp.stack(line) for line in blocks])
-    gradient = jnp.where(own_xh == 0, gradient, gradient[::-1])
-    gradient = jnp.where(own_xl == 0, gradient, gradient[:, ::-1])
+    gradient = jnp.stack([jnp.stack([across(cotangent, dx, dl) for dx in range(2)]) for dl in range(2)])
+    gradient = jnp.stack([gradient, partner(gradient, "yl")])
 
     long_raw = lax.all_to_all(long_owned, SEQ, 0, 0, tiled=True).reshape(width, rows)
+    wide, tall = (rows, width // 2), (width // 2, rows)
+
     long_out, gated = run_blocks(
-        gate, kinds,
-        [(long_raw, channels, 0), (query_conv, tokens, 1)],
-        [plane, ((2, rows, width // 2), BF16, (2, rows, LANES), 2)], 2 * 2**20,
-    )
-
-    quarter = (4, 2, rows, features)
-    (partial,) = run_blocks(
+        gate, 2,
+        [(long_raw, tall, 0), (query_conv, wide, 1)],
+        [((rows, width), F32, wide, 1), ((2, 2, rows, chunk), BF16, (2, 2, rows, LANES), 3)], 2 * 2**20,
+    )
+
+    quarter = (1, 2, 2, 2, rows, features)
+    (outgoing,) = run_blocks(
         partial_kernel, kinds,
-        [(gradient, gradient.shape, None), (weight, quarter, 0), (gated, None, None)],
-        [((2, 4, rows, width // 2), BF16, (2, 1, rows, width // 2), 1)], 6 * 2**20, 2**30,
-    )
-    parts = lax.all_to_all(partial.reshape(8, rows, width // 2), PLANE, 0, 0, tiled=True)
+        [place, (gradient, gradient.shape, None), (weight, quarter, 0), (gated, gated.shape, None)],
+        [((2, 4, 2, rows, chunk), BF16, (2, 1, 2, rows, chunk), 1)], 6 * 2**20, 2**30,
+    )
+    arrived = lax.all_to_all(outgoing.reshape(8, 2, rows, chunk), PLANE, 0, 0, tiled=True)
     long_grad, query_conv_grad = run_blocks(
-        long_gradient, kinds,
-        [(parts, (8, rows, LANES), 2), (query_conv, tokens, 1), (long_out, tokens, 1)],
-        [((width, rows), BF16, channels, 0), plane], 3 * 2**20,
+        long_gradient, 2,
+        [(arrived, (8, 1, rows, LANES), 3), (query_conv, wide, 1), (long_out, wide, 1)],
+        [((width, rows), BF16, tall, 0), ((rows, width), F32, wide, 1)], 3 * 2**20,
     )
     grad_owned = lax.all_to_all(long_grad.reshape(BLOCKS, CHANNELS, LANES), SEQ, 0, 0, tiled=True)
-
-    keep = jnp.where(own_xh == 0, gated[0], gated[1])
-    send = jnp.where(own_xh == 0, gated[1], gated[0])
-    gated_all = lax.all_gather(jnp.stack([keep, across(send, 1, 0)]), "y", axis=0)
 
     back_owned, filter_grad = run_kernel(
         backward_kernel,
         [SEQUENCES, jax.ShapeDtypeStruct((CHANNELS, LENGTH), F32)],
         [GRID, TURNED, SECTION], 3,
-        grad_owned, filter_spectrum, product_spectrum, gated_all, steps, turns, unread=(3,),
-    )
-
+        grad_owned, filter_spectrum, product_spectrum, steps, turns,
+    )
+
+    mixing = arrived.reshape(2, 4, 2, rows, chunk)
     (share,) = run_blocks(
         mix_kernel, kinds,
-        [(gated_all, (1, 2, rows, width // 2), 0), (weight, quarter, 0)],
-        [((2, 2, rows, features), BF16, (2, 2, rows, features), None)], 6 * 2**20, 2**30,
-        [pltpu.VMEM((2, 2 * rows, features), F32)],
-    )
-    share = jnp.where(own_xl == 0, share, share[::-1])
-    mixed = share[0, 0].astype(F32)
-    for dx, dl in ((0, 1), (1, 0), (1, 1)):
-        mixed = mixed + across(share[dl, dx], dx, dl).astype(F32)
-    mixed = mixed.astype(BF16)
+        [(mixing, ((2, 1, 1, rows, chunk), (0, 1)), 1), (weight, quarter, 0)],
+        [((2, 2, 2, rows, features), BF16, (2, 2, 2, rows, features), None)], 6 * 2**20, 2**30,
+        [pltpu.VMEM((4, 2 * rows, features), F32)],
+    )
+    mixed = lax.psum_scatter(
+        share.reshape(8 * rows, features), ("xh", "xl", "yl"), scatter_dimension=0, tiled=True
+    )
 
     rim = (2, chunk)
     (query_grad,) = run_blocks(
@@ -356,7 +378,8 @@
     following = shift(jnp.stack([key_conv[:2], value_conv[:2]]), -1)
 
     back_raw = lax.all_to_all(back_owned, SEQ, 0, 0, tiled=True).reshape(width, rows)
-    after = shift(back_raw[:, :2].T, -1)
+    head, query_grad = lax.optimization_barrier((back_raw[:, :2].T, query_grad))
+    after = shift(head, -1)
     key_grad, value_grad = run_blocks(
         key_value_adjoint, kinds,
         [(back_raw, channels, 0), (key_conv, tokens, 1), (value_conv, tokens, 1),
@@ -367,7 +390,7 @@
 
 
 def solution(mesh):
-    fine = Mesh(mesh.devices.reshape(2, 16, 2, 2, 4), ("xh", "z", "co", "xl", "y"))
+    fine = Mesh(mesh.devices.reshape(tuple(AXES.values())), tuple(AXES))
     token = P(SEQ, TP)
     in_specs = (token, token, token, P(None, None, TP), P(TP + SEQ, None), token, token)
     out_specs = (token, token, token, token, P(TP + SEQ, None))

time: 228 us -> 225 us (0.987)
  starting transfers between devices: 86.6 us -> 66.2 us
  blocking collectives: 0 us -> 20.1 us
  local copies, waits for them, and re-layouts: 22.9 us -> 14.4 us
  Pallas kernels: 17.6 us -> 22.9 us
    all_to_all x0 -> x1, blocking collectives: none -> 20.1 us  [per_device(): lax.all_to_all(outgoing.reshape(8, 2, rows, chunk), PLANE, 0, 0, tiled=True)]
    ppermute x4, waiting for transfers between devices: 1.91 us -> 13.1 us  [shift(): lax.ppermute(value, SEQ, [(i, i + steps) for i in range(first, last)])]
    ppermute x8 -> x5, starting transfers between devices: 29.2 us -> 18.8 us  [the longest x3 9.19 us: across(): lax.ppermute(value, ('xh', 'xl'), [(i, i ^ 2 * dx + dl) for i in range(4)])]
    all_to_all x1, waiting for transfers between devices: 22.4 us -> 13.8 us  [per_device(): lax.all_to_all(product.reshape(BLOCKS, CHANNELS, LANES), SEQ, 0, 0, tiled...]
    unnamed x57 -> x45, local copies, waits for them, and re-layouts: 20.7 us -> 12.2 us
    ppermute x8 -> x5, waiting for transfers between devices: 20 us -> 11.9 us  [the longest x1 11.9 us: partner(): return lax.ppermute(value, axis, [(0, 1), (1, 0)])]
    all_to_all x1, waiting for transfers between devices: 11.6 us -> 18.5 us  [per_device(): lax.all_to_all(long_grad.reshape(BLOCKS, CHANNELS, LANES), SEQ, 0, 0, til...]
    all_to_all x1 -> x0, starting transfers between devices: 4.73 us -> none  [per_device(): lax.all_to_all(partial.reshape(8, rows, width // 2), PLANE, 0, 0, tiled=T...]
  transfers between devices with their start and end apart: 19 -> 15, of which waited for: 11 -> 9; matrix products, arithmetic and copies ran while one was open for 2% -> 1% of each run, Pallas kernels for 5% -> 8%
where the time goes in v3:
time: 225 us; the launch traced here: 223 us
  waiting for transfers between devices  84.1 us (37%)
  starting transfers between devices  66.2 us (29%)
  Pallas kernels  22.9 us (10%)
  blocking collectives  20.1 us (9%)
  local copies, waits for them, and re-layouts  14.4 us (6%)
  between operations  14.4 us (6%)
    all_to_all x1, blocking collectives, per_device(): lax.all_to_all(outgoing.reshape(8, 2, rows, chunk), PLANE, 0, 0, tiled=True)  20.1 us
    all_to_all x1, starting transfers between devices, per_device(): lax.all_to_all(product.reshape(BLOCKS, CHANNELS, LANES), SEQ, 0, 0, tiled...  19.6 us
    all_to_all x1, waiting for transfers between devices, per_device(): lax.all_to_all(long_grad.reshape(BLOCKS, CHANNELS, LANES), SEQ, 0, 0, til...  18.5 us
    pallas_call x7, Pallas kernels, run_blocks(): pl.pallas_call(kernel, grid=(steps,), in_specs=[spec(block, axis) for _,...  17.1 us
    all_to_all x1, waiting for transfers between devices, per_device(): lax.all_to_all(product.reshape(BLOCKS, CHANNELS, LANES), SEQ, 0, 0, tiled...  13.8 us
    ppermute x4, waiting for transfers between devices, shift(): lax.ppermute(value, SEQ, [(i, i + steps) for i in range(first, last)])  13.1 us
    unnamed x45, local copies, waits for them, and re-layouts  12.2 us
    ppermute x1, waiting for transfers between devices, partner(): return lax.ppermute(value, axis, [(0, 1), (1, 0)])  11.9 us
  transfers between devices with their start and end apart: 15, of which 9 were waited for; matrix products, arithmetic and copies ran while one was open for 1% of the time, Pallas kernels for 8%

profile of v3, /device:TPU:1, one launch (start us, length us, event | category | flops | bytes accessed | tf_op | source)
XLA Modules:
  0.0 223.4 jit_solution(586845973755631648)
XLA Ops:
  7.2 0.8 slice_bitcast_fusion.4
  8.0 0.7 slice_bitcast_fusion.2
  8.8 6.0 %collective-permute-start.5 = (bf16[128,512]{1,0:T(8,128)(2,1)}, bf16[128,512]{1,0:T(8,128)(2,1)S(1)}, u32[]{:S(2)}, u32[]{:S(2)}) collective-permute-start(bf16[128,512]{1,0:T(8,128)(2,1)} %param.14), channel_id=1, source_target_pairs={{0,0},{1,16},{4,8},{5,24},{8,256},{9,272},{12,264},{13,280},{16,1}... | collective-permute-start | bytes 393224 | tf_op jit(solution)/shard_map/ppermute | solution.py:293
  14.8 1.9 collective-permute-start.4
  16.7 2.4 %collective-permute-done.4.before_ref = bf16[3,2,1024]{2,1,0:T(2,128)(2,1)S(1)} collective-permute-done((bf16[3,2,1024]{2,1,0:T(2,128)(2,1)S(1)}, bf16[3,2,1024]{2,1,0:T(2,128)(2,1)S(1)}, u32[]{:S(2)}, u32[]{:S(2)}) %collective-permute-start.4) | collective-permute-done | bytes 12320 | tf_op jit(solution)/shard_map/ppermute | solution.py:275
  19.1 0.7 copy-done.19
  19.8 3.7 %shard_map.128 = (f32[128,1024]{1,0:T(8,128)}, f32[128,1024]{1,0:T(8,128)}, f32[128,1024]{1,0:T(8,128)}, bf16[1024,128]{1,0:T(8,128)(2,1)}) custom-call(bf16[128,1024]{1,0:T(8,128)(2,1)} %q_ref.1, bf16[128,1024]{1,0:T(8,128)(2,1)} %k_ref.1, bf16[128,1024]{1,0:T(8,128)(2,1)} %v_ref.1, bf16[3,2,1024]{2,1,0:T(2,128)(2,1)} %copy-done.21, f32[3,3,1024]{2,1,0:T(4,128)} %taps_ref.5), custom_call_target="tpu_custom_call" | custom-call | flops 1000000 | bytes 3145728 | tf_op jit(solution)/shard_map/pallas_call | solution.py:154
  23.5 19.6 %all-to-all-start = ((bf16[64,16,128]{2,1,0:T(8,128)(2,1)}), bf16[64,16,128]{2,1,0:T(8,128)(2,1)S(1)}, u32[]{:S(2)}, u32[]{:S(2)}) async-start(bf16[64,16,128]{2,1,0:T(8,128)(2,1)} %bitcast.43), calls=%async_computation | async-start | bytes 524288 | tf_op jit(solution)/shard_map/all_to_all | solution.py:323
  43.1 1.9 collective-permute-start.1
  45.0 5.2 %collective-permute-start.2 = (bf16[128,512]{1,0:T(8,128)(2,1)}, bf16[128,512]{1,0:T(8,128)(2,1)S(1)}, u32[]{:S(2)}, u32[]{:S(2)}) collective-permute-start(bf16[128,512]{1,0:T(8,128)(2,1)} %param.15), channel_id=1, source_target_pairs={{0,260},{4,256},{256,4},{260,0},{1,261},{5,257},{257,5},{261,1},{2... | collective-permute-start | bytes 393224 | tf_op jit(solution)/shard_map/ppermute | solution.py:285
  50.2 2.1 collective-permute-start
  52.3 1.0 copy-done
  53.3 0.8 copy-done.6
  54.1 1.0 copy-done.12
  55.7 13.8 %all-to-all-done.product_ref = bf16[64,16,128]{2,1,0:T(8,128)(2,1)S(1)} async-done(((bf16[64,16,128]{2,1,0:T(8,128)(2,1)}), bf16[64,16,128]{2,1,0:T(8,128)(2,1)S(1)}, u32[]{:S(2)}, u32[]{:S(2)}) %all-to-all-start) | async-done | bytes 262176 | tf_op jit(solution)/shard_map/all_to_all | solution.py:323
  69.6 1.0 copy-done.1
  70.5 1.8 shard_map.130
  72.3 1.0 copy-done.4
  73.3 4.2 %all-to-all-start.1 = ((bf16[64,16,128]{2,1,0:T(8,128)(2,1)}), bf16[64,16,128]{2,1,0:T(8,128)(2,1)S(1)}, u32[]{:S(2)}, u32[]{:S(2)}) async-start(bf16[64,16,128]{2,1,0:T(8,128)(2,1)} %get-tuple-element.30), calls=%async_computation.1 | async-start | bytes 524288 | tf_op jit(solution)/shard_map/all_to_all | solution.py:331
  77.7 3.5 %collective-permute-start.3 = (bf16[2,2,128,512]{3,2,1,0:T(8,128)(2,1)S(1)}, bf16[2,2,128,512]{3,2,1,0:T(8,128)(2,1)}, u32[]{:S(2)}, u32[]{:S(2)}) collective-permute-start(bf16[2,2,128,512]{3,2,1,0:T(8,128)(2,1)S(1)} %get-tuple-element.46), channel_id=1, source_target_pairs={{0,1},{1,0},{2,3},{3,2},{4,5},{5,4},{6,7},{7,6},{8,9},{9,8},{10,11... | collective-permute-start | bytes 1572872 | tf_op jit(solution)/shard_map/ppermute | solution.py:279
  81.3 11.9 %collective-permute-done.3 = bf16[2,2,128,512]{3,2,1,0:T(8,128)(2,1)} collective-permute-done((bf16[2,2,128,512]{3,2,1,0:T(8,128)(2,1)S(1)}, bf16[2,2,128,512]{3,2,1,0:T(8,128)(2,1)}, u32[]{:S(2)}, u32[]{:S(2)}) %collective-permute-start.3) | collective-permute-done | bytes 524320 | tf_op jit(solution)/shard_map/ppermute | solution.py:279
  93.2 1.1 pad_maximum_fusion.gradient_ref
  94.3 9.4 %all-to-all-done.1 = bf16[64,16,128]{2,1,0:T(8,128)(2,1)S(1)} async-done(((bf16[64,16,128]{2,1,0:T(8,128)(2,1)}), bf16[64,16,128]{2,1,0:T(8,128)(2,1)S(1)}, u32[]{:S(2)}, u32[]{:S(2)}) %all-to-all-start.1) | async-done | bytes 262176 | tf_op jit(solution)/shard_map/all_to_all | solution.py:331
  104.2 0.7 copy-done.17
  104.9 9.8 %all-gather.3.cloned.1.call-done = bf16[4096,512]{1,0:T(8,128)(2,1)} async-done(((bf16[128,512]{1,0:T(8,128)(2,1)}), bf16[4096,512]{1,0:T(8,128)(2,1)}) %all-gather.3.cloned.1.call-update) | async-done | bytes 4194320 | tf_op jit(solution)/shard_map/all_gather | solution.py:306
  114.6 0.9 copy-done.18
  115.6 4.1 %shard_map.132 = bf16[2,4,2,128,256]{4,3,2,1,0:T(8,128)(2,1)S(1)} custom-call(s32[4]{0:T(128)S(1)} %pad_add_fusion.place_ref, bf16[2,2,2,128,512]{4,3,2,1,0:T(8,128)(2,1)S(1)} %pad_maximum_fusion.gradient_ref, bf16[4,2,2,2,128,512]{5,4,3,2,1,0:T(8,128)(2,1)} %bitcast.41, bf16[2,2,128,256]{3,2,1,0:T(8,128)(2,1)S(1)} %copy-done.18), custom_call_target="tpu_custom_call" | custom-call | flops 1073741824 | bytes 6291456 | tf_op jit(solution)/shard_map/pallas_call | solution.py:154
  119.7 20.1 %all_to_all.25.parts_ref = bf16[8,2,128,256]{3,2,1,0:T(8,128)(2,1)S(1)} all-to-all(bf16[8,2,128,256]{3,2,1,0:T(8,128)(2,1)S(1)} %bitcast.36), channel_id=1, replica_groups=mesh['xh'=2,'zy'=4,'zh'=2,'zb'=2,'co'=2,'xl'=2,'yh'=2,'yl'=2] {'xh','yh'..., dimensions={0} | all-to-all | bytes 2097152 | tf_op jit(solution)/shard_map/all_to_all | solution.py:346
  140.2 0.8 copy-done.10
  141.1 0.7 copy-done.16
  141.8 11.4 %all-to-all-start.3 = ((bf16[64,16,128]{2,1,0:T(8,128)(2,1)}), bf16[64,16,128]{2,1,0:T(8,128)(2,1)}, u32[]{:S(2)}, u32[]{:S(2)}) async-start(bf16[64,16,128]{2,1,0:T(8,128)(2,1)} %bitcast.40), calls=%async_computation.4 | async-start | bytes 524288 | tf_op jit(solution)/shard_map/all_to_all | solution.py:352
  153.2 5.1 %shard_map.133 = bf16[2,2,2,128,512]{4,3,2,1,0:T(8,128)(2,1)} custom-call(bf16[2,4,2,128,256]{4,3,2,1,0:T(8,128)(2,1)S(1)} %bitcast.35, bf16[4,2,2,2,128,512]{5,4,3,2,1,0:T(8,128)(2,1)} %bitcast.42), custom_call_target="tpu_custom_call" | custom-call | flops 1073741824 | bytes 6291456 | tf_op jit(solution)/shard_map/pallas_call | solution.py:154
  158.4 18.5 %all-to-all-done.3.grad_ref = bf16[64,16,128]{2,1,0:T(8,128)(2,1)} async-done(((bf16[64,16,128]{2,1,0:T(8,128)(2,1)}), bf16[64,16,128]{2,1,0:T(8,128)(2,1)}, u32[]{:S(2)}, u32[]{:S(2)}) %all-to-all-start.3) | async-done | bytes 262176 | tf_op jit(solution)/shard_map/all_to_all | solution.py:352
  176.8 3.4 %shard_map.135 = (bf16[64,16,128]{2,1,0:T(8,128)(2,1)S(1)}, f32[16,8192]{1,0:T(8,128)}) custom-call(bf16[64,16,128]{2,1,0:T(8,128)(2,1)} %all-to-all-done.3.grad_ref, f32[1024,256]{1,0:T(8,128)S(1)} %shard_map.129.filter_spectrum, f32[1024,256]{1,0:T(8,128)S(1)} %copy-done.5, bf16[256,640]{1,0:T(8,128)(2,1)S(1)} %copy-done.2, f32[64,256]{1,0:T(8,128)S(1)} %copy-done.7), custom_call_target="tpu_custom_call" | custom-call | flops 503316480 | bytes 4194304 | tf_op jit(solution)/shard_map/pallas_call | solution.py:133
  180.3 0.7 copy-done.15
  181.0 4.2 %all-to-all-start.4 = ((bf16[64,16,128]{2,1,0:T(8,128)(2,1)}), bf16[64,16,128]{2,1,0:T(8,128)(2,1)S(1)}, u32[]{:S(2)}, u32[]{:S(2)}) async-start(bf16[64,16,128]{2,1,0:T(8,128)(2,1)} %copy-done.15), calls=%async_computation.5 | async-start | bytes 524288 | tf_op jit(solution)/shard_map/all_to_all | solution.py:380
  185.2 2.2 collective-permute-start.8
  187.5 0.8 slice.25
  188.2 1.9 collective-permute-start.6
  190.1 7.7 %collective-permute-done.6.after_ref = f32[2,1024]{1,0:T(2,128)S(1)} collective-permute-done((f32[2,1024]{1,0:T(2,128)S(1)}, f32[2,1024]{1,0:T(2,128)S(1)}, u32[]{:S(2)}, u32[]{:S(2)}) %collective-permute-start.6) | collective-permute-done | bytes 8224 | tf_op jit(solution)/shard_map/ppermute | solution.py:275
  197.8 1.0 copy-done.11
  198.9 0.8 copy-done.13
  199.7 1.5 shard_map.136
  201.1 7.6 %all-to-all-done.4 = bf16[64,16,128]{2,1,0:T(8,128)(2,1)S(1)} async-done(((bf16[64,16,128]{2,1,0:T(8,128)(2,1)}), bf16[64,16,128]{2,1,0:T(8,128)(2,1)S(1)}, u32[]{:S(2)}, u32[]{:S(2)}) %all-to-all-start.4) | async-done | bytes 262176 | tf_op jit(solution)/shard_map/all_to_all | solution.py:380
  208.9 1.9 collective-permute-start.7
  210.9 3.0 %collective-permute-done.7.after_ref = bf16[2,1024]{1,0:T(2,128)(2,1)S(1)} collective-permute-done((bf16[2,1024]{1,0:T(2,128)(2,1)S(1)}, bf16[2,1024]{1,0:T(2,128)(2,1)S(1)}, u32[]{:S(2)}, u32[]{:S(2)}) %collective-permute-start.7) | collective-permute-done | bytes 4128 | tf_op jit(solution)/shard_map/ppermute | solution.py:275
  213.8 0.8 copy-done.14
  214.6 1.9 shard_map.137
  (52 shorter events, 2.0 us)
Async XLA Ops:
  7.2 70.4 %copy-start.20 = (bf16[128,512]{1,0:T(8,128)(2,1)S(1)}, bf16[128,512]{1,0:T(8,128)(2,1)}, u32[]{:S(2)}) copy-start(bf16[128,512]{1,0:T(8,128)(2,1)} %param.15) | copy-start | bytes 393220
  7.2 107.5 %all-gather.3.cloned.1.call-start = ((), (), s32[]{:S(2)}) async-start(), calls=%async_computation.7 | async-start | bytes 4325376 | tf_op jit(solution)/shard_map/all_gather | solution.py:306
  8.8 10.4 %collective-permute-start.5 = (bf16[128,512]{1,0:T(8,128)(2,1)}, bf16[128,512]{1,0:T(8,128)(2,1)S(1)}, u32[]{:S(2)}, u32[]{:S(2)}) collective-permute-start(bf16[128,512]{1,0:T(8,128)(2,1)} %param.14), channel_id=1, source_target_pairs={{0,0},{1,16},{4,8},{5,24},{8,256},{9,272},{12,264},{13,280},{16,1}... | collective-permute-start | bytes 393224 | tf_op jit(solution)/shard_map/ppermute | solution.py:293
  14.8 4.3 %collective-permute-start.4 = (bf16[3,2,1024]{2,1,0:T(2,128)(2,1)S(1)}, bf16[3,2,1024]{2,1,0:T(2,128)(2,1)S(1)}, u32[]{:S(2)}, u32[]{:S(2)}) collective-permute-start(bf16[3,2,1024]{2,1,0:T(2,128)(2,1)S(1)} %pad_maximum_fusion.3), channel_id=1, source_target_pairs={{0,8},{8,16},{16,24},{24,32},{32,40},{40,48},{48,56},{56,64},{64,7... | collective-permute-start | bytes 36872 | tf_op jit(solution)/shard_map/ppermute | solution.py:275
  19.1 0.7 copy-start.21
  19.1 0.7 copy-start.19
  23.5 80.2 %copy-start.3 = (f32[128,1024]{1,0:T(8,128)S(1)}, f32[128,1024]{1,0:T(8,128)}, u32[]{:S(2)}) copy-start(f32[128,1024]{1,0:T(8,128)} %get-tuple-element.31.qc_ref) | copy-start | bytes 1572868
  23.5 46.0 %all-to-all-start = ((bf16[64,16,128]{2,1,0:T(8,128)(2,1)}), bf16[64,16,128]{2,1,0:T(8,128)(2,1)S(1)}, u32[]{:S(2)}, u32[]{:S(2)}) async-start(bf16[64,16,128]{2,1,0:T(8,128)(2,1)} %bitcast.43), calls=%async_computation | async-start | bytes 524288 | tf_op jit(solution)/shard_map/all_to_all | solution.py:323
  43.1 34.4 %collective-permute-start.1 = (bf16[128,512]{1,0:T(8,128)(2,1)}, bf16[128,512]{1,0:T(8,128)(2,1)S(1)}, u32[]{:S(2)}, u32[]{:S(2)}) collective-permute-start(bf16[128,512]{1,0:T(8,128)(2,1)} %param.15), channel_id=1, source_target_pairs={{0,4},{4,0},{256,260},{260,256},{1,5},{5,1},{257,261},{261,257},{2... | collective-permute-start | bytes 393224 | tf_op jit(solution)/shard_map/ppermute | solution.py:285
  45.0 32.5 %collective-permute-start.2 = (bf16[128,512]{1,0:T(8,128)(2,1)}, bf16[128,512]{1,0:T(8,128)(2,1)S(1)}, u32[]{:S(2)}, u32[]{:S(2)}) collective-permute-start(bf16[128,512]{1,0:T(8,128)(2,1)} %param.15), channel_id=1, source_target_pairs={{0,260},{4,256},{256,4},{260,0},{1,261},{5,257},{257,5},{261,1},{2... | collective-permute-start | bytes 393224 | tf_op jit(solution)/shard_map/ppermute | solution.py:285
  50.2 27.3 %collective-permute-start = (bf16[128,512]{1,0:T(8,128)(2,1)}, bf16[128,512]{1,0:T(8,128)(2,1)S(1)}, u32[]{:S(2)}, u32[]{:S(2)}) collective-permute-start(bf16[128,512]{1,0:T(8,128)(2,1)} %param.15), channel_id=1, source_target_pairs={{0,256},{4,260},{256,0},{260,4},{1,257},{5,261},{257,1},{261,5},{2... | collective-permute-start | bytes 393224 | tf_op jit(solution)/shard_map/ppermute | solution.py:285
  52.3 1.0 copy-start
  53.3 0.8 copy-start.6
  54.1 1.0 copy-start.12
  69.6 1.0 copy-start.1
  72.3 1.0 copy-start.4
  73.3 30.5 %all-to-all-start.1 = ((bf16[64,16,128]{2,1,0:T(8,128)(2,1)}), bf16[64,16,128]{2,1,0:T(8,128)(2,1)S(1)}, u32[]{:S(2)}, u32[]{:S(2)}) async-start(bf16[64,16,128]{2,1,0:T(8,128)(2,1)} %get-tuple-element.30), calls=%async_computation.1 | async-start | bytes 524288 | tf_op jit(solution)/shard_map/all_to_all | solution.py:331
  77.7 15.5 %collective-permute-start.3 = (bf16[2,2,128,512]{3,2,1,0:T(8,128)(2,1)S(1)}, bf16[2,2,128,512]{3,2,1,0:T(8,128)(2,1)}, u32[]{:S(2)}, u32[]{:S(2)}) collective-permute-start(bf16[2,2,128,512]{3,2,1,0:T(8,128)(2,1)S(1)} %get-tuple-element.46), channel_id=1, source_target_pairs={{0,1},{1,0},{2,3},{3,2},{4,5},{5,4},{6,7},{7,6},{8,9},{9,8},{10,11... | collective-permute-start | bytes 1572872 | tf_op jit(solution)/shard_map/ppermute | solution.py:279
  104.2 0.7 copy-start.17
  114.6 0.9 copy-start.18
  140.2 0.8 copy-start.10
  141.1 0.7 copy-start.16
  141.8 35.1 %copy-start.2 = (bf16[256,640]{1,0:T(8,128)(2,1)S(1)}, bf16[256,640]{1,0:T(8,128)(2,1)}, u32[]{:S(2)}) copy-start(bf16[256,640]{1,0:T(8,128)(2,1)} %constant.18.clone.steps) | copy-start | bytes 983044
  141.8 35.1 %copy-start.5 = (f32[1024,256]{1,0:T(8,128)S(1)}, f32[1024,256]{1,0:T(8,128)}, u32[]{:S(2)}) copy-start(f32[1024,256]{1,0:T(8,128)} %copy-done.4) | copy-start | bytes 3145732
  141.8 35.1 %copy-start.7 = (f32[64,256]{1,0:T(8,128)S(1)}, f32[64,256]{1,0:T(8,128)}, u32[]{:S(2)}) copy-start(f32[64,256]{1,0:T(8,128)} %constant.19.clone.turns) | copy-start | bytes 196612
  141.8 35.1 %all-to-all-start.3 = ((bf16[64,16,128]{2,1,0:T(8,128)(2,1)}), bf16[64,16,128]{2,1,0:T(8,128)(2,1)}, u32[]{:S(2)}, u32[]{:S(2)}) async-start(bf16[64,16,128]{2,1,0:T(8,128)(2,1)} %bitcast.40), calls=%async_computation.4 | async-start | bytes 524288 | tf_op jit(solution)/shard_map/all_to_all | solution.py:352
  153.2 63.4 %reduce-scatter.2.cloned.1.call-start = ((), (), s32[]{:S(2)}) async-start(), calls=%async_computation.6 | async-start | bytes 1179648 | tf_op jit(solution)/shard_map/reduce_scatter | solution.py:368
  158.4 26.8 %copy-start.9 = (f32[128,1024]{1,0:T(8,128)S(1)}, f32[128,1024]{1,0:T(8,128)}, u32[]{:S(2)}) copy-start(f32[128,1024]{1,0:T(8,128)} %get-tuple-element.40.vc_ref) | copy-start | bytes 1572868
  158.4 26.8 %copy-start.8 = (f32[128,1024]{1,0:T(8,128)S(1)}, f32[128,1024]{1,0:T(8,128)}, u32[]{:S(2)}) copy-start(f32[128,1024]{1,0:T(8,128)} %get-tuple-element.39.kc_ref) | copy-start | bytes 1572868
  180.3 0.7 copy-start.15
  181.0 27.8 %all-to-all-start.4 = ((bf16[64,16,128]{2,1,0:T(8,128)(2,1)}), bf16[64,16,128]{2,1,0:T(8,128)(2,1)S(1)}, u32[]{:S(2)}, u32[]{:S(2)}) async-start(bf16[64,16,128]{2,1,0:T(8,128)(2,1)} %copy-done.15), calls=%async_computation.5 | async-start | bytes 524288 | tf_op jit(solution)/shard_map/all_to_all | solution.py:380
  185.2 25.6 %collective-permute-start.8 = (f32[2,2,1024]{2,1,0:T(2,128)S(1)}, f32[2,2,1024]{2,1,0:T(2,128)S(1)}, u32[]{:S(2)}, u32[]{:S(2)}) collective-permute-start(f32[2,2,1024]{2,1,0:T(2,128)S(1)} %pad_maximum_fusion.2), channel_id=1, source_target_pairs={{8,0},{16,8},{24,16},{32,24},{40,32},{48,40},{56,48},{64,56},{72,6... | collective-permute-start | bytes 49160 | tf_op jit(solution)/shard_map/ppermute | solution.py:275
  188.2 9.6 %collective-permute-start.6 = (f32[2,1024]{1,0:T(2,128)S(1)}, f32[2,1024]{1,0:T(2,128)S(1)}, u32[]{:S(2)}, u32[]{:S(2)}) collective-permute-start(f32[2,1024]{1,0:T(2,128)S(1)} %slice.25), channel_id=1, source_target_pairs={{8,0},{16,8},{24,16},{32,24},{40,32},{48,40},{56,48},{64,56},{72,6... | collective-permute-start | bytes 24584 | tf_op jit(solution)/shard_map/ppermute | solution.py:275
  197.8 1.0 copy-start.11
  198.9 0.8 copy-start.13
  208.9 4.9 %collective-permute-start.7 = (bf16[2,1024]{1,0:T(2,128)(2,1)S(1)}, bf16[2,1024]{1,0:T(2,128)(2,1)S(1)}, u32[]{:S(2)}, u32[]{:S(2)}) collective-permute-start(bf16[2,1024]{1,0:T(2,128)(2,1)S(1)} %bitcast.48), channel_id=1, source_target_pairs={{8,0},{16,8},{24,16},{32,24},{40,32},{48,40},{56,48},{64,56},{72,6... | collective-permute-start | bytes 12296 | tf_op jit(solution)/shard_map/ppermute | solution.py:275
  213.8 0.8 copy-start.14
Sparse Core Ops, SparseCore 0:
  20.0 94.6 all-gather.2
  158.5 42.2 reduce-scatter.1

commit v4 on v3

--- a/solution.py
+++ b/solution.py
@@ -23,6 +23,7 @@
 LANES = 128
 LENGTH = BLOCKS * LANES
 
+RIM = 16
 VMEM_LIMIT = 20 * 2**20
 WHOLE_VMEM = 60 * 2**20
 
@@ -78,7 +79,7 @@
 def filter_kernel(filter_ref, steps, turns, spectrum_ref, grid, turned):
     for b in range(BLOCKS):
         grid[b * CHANNELS : (b + 1) * CHANNELS, :] = filter_ref[:, b * LANES : (b + 1) * LANES]
-    spectrum_ref[...] = to_spectrum(grid, turned, steps, turns)
+    spectrum_ref[...] = to_spectrum(grid, turned, steps, turns).astype(BF16)
 
 
 def forward_kernel(
@@ -86,9 +87,10 @@
 ):
     grid[...] = product_ref[...].astype(F32).reshape(BLOCKS * CHANNELS, LANES)
     own = to_spectrum(grid, turned, steps, turns)
-    product_spectrum[...] = own
+    product_spectrum[...] = own.astype(BF16)
     own_re, own_im = own[:, :LANES], own[:, LANES:]
-    other_re, other_im = filter_spectrum[:, :LANES], filter_spectrum[:, LANES:]
+    other = filter_spectrum[...].astype(F32)
+    other_re, other_im = other[:, :LANES], other[:, LANES:]
     turned[:, :LANES] = (own_re * other_re - own_im * other_im).astype(BF16)
     turned[:, LANES:] = (own_re * other_im + own_im * other_re).astype(BF16)
     from_spectrum(turned[...], grid, section, steps, turns)
@@ -104,7 +106,7 @@
     own_re, own_im = own[:, :LANES], own[:, LANES:]
 
     def correlate(other):
-        other_re, other_im = other[:, :LANES], other[:, LANES:]
+        other_re, other_im = other[:, :LANES].astype(F32), other[:, LANES:].astype(F32)
         turned[:, :LANES] = (own_re * other_re + own_im * other_im).astype(BF16)
         turned[:, LANES:] = (own_im * other_re - own_re * other_im).astype(BF16)
         from_spectrum(turned[...], grid, section, steps, turns)
@@ -118,7 +120,7 @@
         ] * (1.0 / math.sqrt(LENGTH))
 
 
-SPECTRUM = jax.ShapeDtypeStruct((CHANNELS * BLOCKS, 2 * LANES), F32)
+SPECTRUM = jax.ShapeDtypeStruct((CHANNELS * BLOCKS, 2 * LANES), BF16)
 SEQUENCES = jax.ShapeDtypeStruct((BLOCKS, CHANNELS, LANES), BF16)
 GRID = pltpu.VMEM((BLOCKS * CHANNELS, LANES), F32)
 TURNED = pltpu.VMEM((CHANNELS * BLOCKS, 2 * LANES), BF16)
@@ -142,13 +144,13 @@
     )(*operands)
 
 
-def run_blocks(kernel, steps, ins, outs, moved, flops=10**6, scratch=(), limit=VMEM_LIMIT):
+def run_blocks(kernel, steps, ins, outs, moved, flops=10**6, scratch=(), limit=VMEM_LIMIT, pinned=False, alias=()):
     def spec(block, axis):
         if block is None:
             return pl.BlockSpec(memory_space=axis or pl.ANY)
         fixed = (0,) * len(block)
         if isinstance(block[0], tuple):
-            block, fixed = block[0], (0,) * (len(block[0]) - 3) + (block[1][1],) + (0, 0)
+            block, fixed = block
         return pl.BlockSpec(block, lambda i: tuple(i if d == axis else fixed[d] for d in range(len(block))))
 
     return pl.pallas_call(
@@ -156,7 +158,10 @@
         grid=(steps,),
         in_specs=[spec(block, axis) for _, block, axis in ins],
         out_specs=[spec(block, axis) for _, _, block, axis in outs],
-        out_shape=[jax.ShapeDtypeStruct(shape, dtype) for shape, dtype, _, _ in outs],
+        out_shape=[
+            (pltpu.HBM if pinned else jax.ShapeDtypeStruct)(shape, dtype) for shape, dtype, _, _ in outs
+        ],
+        input_output_aliases=dict(alias),
         scratch_shapes=list(scratch),
         compiler_params=pltpu.CompilerParams(vmem_limit_bytes=limit),
         cost_estimate=pl.CostEstimate(flops=flops, bytes_accessed=moved, transcendentals=0),
@@ -184,55 +189,67 @@
     return taps[0:1] * value + taps[1:2] * one + taps[2:3] * two
 
 
-def filter_inputs(q_ref, k_ref, v_ref, before_ref, taps_ref, qc_ref, kc_ref, vc_ref, product_ref):
-    sources = (q_ref, k_ref, v_ref)
-    qc, kc, vc = (
-        causal(sources[i][...].astype(F32), before_ref[i].astype(F32), taps_ref[i]) for i in range(3)
-    )
-    qc_ref[...], kc_ref[...], vc_ref[...] = qc, kc, vc
+def filter_product(k_ref, v_ref, before_ref, taps_ref, product_ref):
+    kc = causal(k_ref[...].astype(F32), before_ref[1].astype(F32), taps_ref[1])
+    vc = causal(v_ref[...].astype(F32), before_ref[2].astype(F32), taps_ref[2])
     product_ref[...] = (kc * vc).T.astype(BF16)
 
 
-def gate(long_ref, qc_ref, out_ref, gated_ref):
-    long = long_ref[...].astype(F32).T
-    out_ref[...] = long
-    gated = (qc_ref[...] * long).astype(BF16)
-    for zb in range(2):
-        for co in range(2):
-            start = (2 * zb + co) * LANES
-            gated_ref[co, zb] = gated[:, start : start + LANES]
-
-
-def partial_kernel(place_ref, gradient_ref, weight_ref, gated_ref, out_ref):
+def filter_inputs(
+    q_ref, k_ref, v_ref, before_ref, taps_ref, _, qc_ref, kc_ref, vc_ref, turned_ref
+):
+    sources, results = (q_ref, k_ref, v_ref), (qc_ref, kc_ref, vc_ref)
+    for i in range(3):
+        results[i][...] = causal(sources[i][...].astype(F32), before_ref[i].astype(F32), taps_ref[i])
+    turned_ref[...] = qc_ref[...].T
+
+
+def gate(long_ref, qc_ref, gated_ref):
+    gated = (qc_ref[...] * long_ref[...].astype(F32).T).astype(BF16)
+    for co in range(2):
+        for y in range(4):
+            start = (2 * (y % 2) + co) * LANES
+            gated_ref[co, y] = gated[:, start : start + LANES]
+
+
+def partial_kernel(place_ref, gradient_ref, weight_ref, _, out_ref, total):
     xh, xl, yl = place_ref[0], place_ref[1], place_ref[3]
-    rows, features = gradient_ref.shape[3:]
-    width = out_ref.shape[4]
-    total = jnp.zeros((2 * rows, width), F32)
+    step = pl.program_id(0)
+    features, tokens = gradient_ref.shape[2:]
+    rows = tokens // 2
+    added = jnp.dot(
+        weight_ref[...].reshape(total.shape[0], features),
+        gradient_ref[(step // 2) ^ yl, (step % 2) ^ xl],
+        preferred_element_type=F32,
+    )
+
+    @pl.when(step == 0)
+    def _():
+        total[...] = added
+
+    @pl.when(step > 0)
+    def _():
+        total[...] += added
+
+    @pl.when(step == pl.num_programs(0) - 1)
+    def _():
+        for t in range(2):
+            value = total[:, t * rows : (t + 1) * rows].astype(BF16)
+            out_ref[t ^ xh] = value.reshape(out_ref.shape[1:])
+
+
+def long_gradient(parts_ref, qc_ref, long_ref, grad_ref, qg_ref):
     for e in range(2):
-        for f in range(2):
-            total += lax.dot_general(
-                gradient_ref[e ^ yl, f ^ xl].reshape(2 * rows, features),
-                weight_ref[0, :, e, f].reshape(width, features),
-                (((1,), (1,)), ((), ())),
-                preferred_element_type=F32,
-            )
-    for t in range(2):
-        out_ref[t ^ xh, 0, 0] = total[t * rows : (t + 1) * rows].astype(BF16)
-        out_ref[t, 0, 1] = gated_ref[t, pl.program_id(0) % 2]
-
-
-def long_gradient(parts_ref, qc_ref, long_ref, grad_ref, qg_ref):
-    parts = parts_ref[...].astype(F32).reshape(8, *qg_ref.shape[:1], LANES)
-    gated_grad = jnp.concatenate(
-        [parts[4 * r + e] + parts[4 * r + 2 + e] for e in range(2) for r in range(2)], axis=1
-    )
-    grad_ref[...] = (qc_ref[...] * gated_grad).T.astype(BF16)
-    qg_ref[...] = gated_grad * long_ref[...]
+        for r in range(2):
+            rows = slice((2 * e + r) * LANES, (2 * e + r + 1) * LANES)
+            gated_grad = parts_ref[4 * r + e].astype(F32) + parts_ref[4 * r + 2 + e].astype(F32)
+            grad_ref[rows] = (qc_ref[rows] * gated_grad).astype(BF16)
+            qg_ref[rows] = gated_grad * long_ref[rows].astype(F32)
 
 
 def mix_kernel(gated_ref, weight_ref, out_ref, total):
-    halves, _, _, rows, width = gated_ref.shape
-    features = weight_ref.shape[5]
+    halves, _, rows, width = gated_ref.shape
+    features = weight_ref.shape[4]
     step = pl.program_id(0)
 
     @pl.when(step == 0)
@@ -243,7 +260,7 @@
     for e in range(2):
         for f in range(2):
             total[2 * e + f] += jnp.dot(
-                gated, weight_ref[0, :, e, f].reshape(width, features), preferred_element_type=F32
+                gated, weight_ref[0, :, 2 * e + f].reshape(width, features), preferred_element_type=F32
             )
 
     @pl.when(step == pl.num_programs(0) - 1)
@@ -255,13 +272,20 @@
 
 
 def query_adjoint(qg_ref, after_ref, taps_ref, out_ref):
-    out_ref[...] = adjoint(qg_ref[...], after_ref[...], taps_ref[0]).astype(BF16)
-
-
-def key_value_adjoint(
-    back_ref, kc_ref, vc_ref, after_ref, next_ref, taps_ref, key_ref, value_ref
+    out_ref[...] = adjoint(qg_ref[...].T, after_ref[...], taps_ref[0]).astype(BF16)
+
+
+def key_value_adjoint(back_ref, kc_ref, vc_ref, taps_ref, key_ref, value_ref):
+    back = back_ref[...].astype(F32).T
+    after = jnp.zeros((2, back.shape[1]), F32)
+    key_ref[...] = adjoint(back * vc_ref[...], after, taps_ref[1]).astype(BF16)
+    value_ref[...] = adjoint(back * kc_ref[...], after, taps_ref[2]).astype(BF16)
+
+
+def key_value_rim(
+    tail_ref, kc_ref, vc_ref, after_ref, next_ref, taps_ref, _, __, key_ref, value_ref
 ):
-    back = back_ref[...].astype(F32).T
+    back = tail_ref[...].astype(F32)
     after = after_ref[...].astype(F32)
     key_ref[...] = adjoint(back * vc_ref[...], after * next_ref[1], taps_ref[1]).astype(BF16)
     value_ref[...] = adjoint(back * kc_ref[...], after * next_ref[0], taps_ref[2]).astype(BF16)
@@ -303,7 +327,7 @@
     rims = jnp.stack([x[rows - 2 :] for x in (queries, keys, values)])
     rims, out_weight = lax.optimization_barrier((rims, out_weight))
     before, turned = lax.optimization_barrier((shift(rims, 1), turn(out_weight)))
-    weight = lax.all_gather(turned, COLUMN, axis=0).reshape(4, 2, 2, 2, rows, features)
+    weight = lax.all_gather(turned, COLUMN, axis=0).reshape(4, 2, 4, rows, features)
     weight = pltpu.with_memory_space_constraint(weight, pltpu.HBM)
 
     steps, turns = transform_tables()
@@ -313,55 +337,66 @@
     channels = (chunk, rows)
     taps_block = (3, 3, chunk)
     plane = ((rows, width), F32, tokens, 1)
-    query_conv, key_conv, value_conv, product = run_blocks(
+    (product,) = run_blocks(
+        filter_product, 1,
+        [(keys, (rows, width), 1), (values, (rows, width), 1), (before, before.shape, 2), (short_taps, short_taps.shape, 2)],
+        [((width, rows), BF16, (width, rows), 0)], 2**20, limit=WHOLE_VMEM,
+    )
+    query_conv, key_conv, value_conv, query_turned = run_blocks(
         filter_inputs, kinds,
         [(queries, tokens, 1), (keys, tokens, 1), (values, tokens, 1),
-         (before, (3, 2, chunk), 2), (short_taps, taps_block, 2)],
-        [plane, plane, plane, ((width, rows), BF16, channels, 0)], 3 * 2**20, limit=WHOLE_VMEM,
+         (before, (3, 2, chunk), 2), (short_taps, taps_block, 2), (product, None, None)],
+        [plane, plane, plane, ((width, rows), F32, channels, 0)], 3 * 2**20, limit=WHOLE_VMEM,
     )
 
     product_owned = lax.all_to_all(product.reshape(BLOCKS, CHANNELS, LANES), SEQ, 0, 0, tiled=True)
     long_owned, product_spectrum = run_kernel(
-        forward_kernel, [SEQUENCES, SPECTRUM], [GRID, TURNED, SECTION], 2,
+        forward_kernel, [pltpu.HBM(SEQUENCES.shape, BF16), pltpu.HBM(SPECTRUM.shape, BF16)], [GRID, TURNED, SECTION], 2,
         product_owned, filter_spectrum, steps, turns,
     )
-    gradient = jnp.stack([jnp.stack([across(cotangent, dx, dl) for dx in range(2)]) for dl in range(2)])
+    turned = cotangent.T
+    gradient = jnp.stack(
+        [jnp.concatenate([across(turned, dx, dl) for dx in range(2)], axis=1) for dl in range(2)]
+    )
     gradient = jnp.stack([gradient, partner(gradient, "yl")])
 
     long_raw = lax.all_to_all(long_owned, SEQ, 0, 0, tiled=True).reshape(width, rows)
     wide, tall = (rows, width // 2), (width // 2, rows)
 
-    long_out, gated = run_blocks(
+    (gated,) = run_blocks(
         gate, 2,
         [(long_raw, tall, 0), (query_conv, wide, 1)],
-        [((rows, width), F32, wide, 1), ((2, 2, rows, chunk), BF16, (2, 2, rows, LANES), 3)], 2 * 2**20,
-    )
-
-    quarter = (1, 2, 2, 2, rows, features)
-    (outgoing,) = run_blocks(
+        [((2, 4, rows, chunk), BF16, (2, 4, rows, LANES), 3)], 2 * 2**20, pinned=True,
+    )
+
+    mixing = lax.all_to_all(gated.reshape(8, rows, chunk), PLANE, 0, 0, tiled=True)
+
+    (partial,) = run_blocks(
         partial_kernel, kinds,
-        [place, (gradient, gradient.shape, None), (weight, quarter, 0), (gated, gated.shape, None)],
-        [((2, 4, 2, rows, chunk), BF16, (2, 1, 2, rows, chunk), 1)], 6 * 2**20, 2**30,
-    )
-    arrived = lax.all_to_all(outgoing.reshape(8, 2, rows, chunk), PLANE, 0, 0, tiled=True)
+        [place, (gradient, gradient.shape, None),
+         (weight, (4, 2, 1, rows, features), 2), (mixing, None, None)],
+        [((2, 4, chunk, rows), BF16, (2, 4, chunk, rows), None)], 6 * 2**20, 2**30,
+        [pltpu.VMEM((width, 2 * rows), F32)],
+    )
+    arrived = lax.all_to_all(partial.reshape(8, chunk, rows), PLANE, 0, 0, tiled=True)
     long_grad, query_conv_grad = run_blocks(
         long_gradient, 2,
-        [(arrived, (8, 1, rows, LANES), 3), (query_conv, wide, 1), (long_out, wide, 1)],
-        [((width, rows), BF16, tall, 0), ((rows, width), F32, wide, 1)], 3 * 2**20,
+        [(arrived, (8, LANES, rows), 1), (query_turned, tall, 0), (long_raw, tall, 0)],
+        [((width, rows), BF16, tall, 0), ((width, rows), F32, tall, 0)], 3 * 2**20, pinned=True,
     )
     grad_owned = lax.all_to_all(long_grad.reshape(BLOCKS, CHANNELS, LANES), SEQ, 0, 0, tiled=True)
 
     back_owned, filter_grad = run_kernel(
         backward_kernel,
-        [SEQUENCES, jax.ShapeDtypeStruct((CHANNELS, LENGTH), F32)],
+        [pltpu.HBM(SEQUENCES.shape, BF16), pltpu.HBM((CHANNELS, LENGTH), F32)],
         [GRID, TURNED, SECTION], 3,
         grad_owned, filter_spectrum, product_spectrum, steps, turns,
     )
 
-    mixing = arrived.reshape(2, 4, 2, rows, chunk)
+    quarter = (1, 2, 4, rows, features)
     (share,) = run_blocks(
         mix_kernel, kinds,
-        [(mixing, ((2, 1, 1, rows, chunk), (0, 1)), 1), (weight, quarter, 0)],
+        [(mixing.reshape(2, 4, rows, chunk), (2, 1, rows, chunk), 1), (weight, quarter, 0)],
         [((2, 2, 2, rows, features), BF16, (2, 2, 2, rows, features), None)], 6 * 2**20, 2**30,
         [pltpu.VMEM((4, 2 * rows, features), F32)],
     )
@@ -372,7 +407,7 @@
     rim = (2, chunk)
     (query_grad,) = run_blocks(
         query_adjoint, kinds,
-        [(query_conv_grad, tokens, 1), (shift(query_conv_grad[:2], -1), rim, 1), (short_taps, taps_block, 2)],
+        [(query_conv_grad, channels, 0), (shift(query_conv_grad[:, :2].T, -1), rim, 1), (short_taps, taps_block, 2)],
         [((rows, width), BF16, tokens, 1)], 2**20,
     )
     following = shift(jnp.stack([key_conv[:2], value_conv[:2]]), -1)
@@ -380,11 +415,19 @@
     back_raw = lax.all_to_all(back_owned, SEQ, 0, 0, tiled=True).reshape(width, rows)
     head, query_grad = lax.optimization_barrier((back_raw[:, :2].T, query_grad))
     after = shift(head, -1)
+    grads = run_blocks(
+        key_value_adjoint, kinds,
+        [(back_raw, channels, 0), (key_conv, tokens, 1), (value_conv, tokens, 1), (short_taps, taps_block, 2)],
+        [((rows, width), BF16, tokens, 1)] * 2, 3 * 2**20,
+    )
+    tail = (RIM, width)
+    last = (tail, (rows // RIM - 1, 0))
     key_grad, value_grad = run_blocks(
-        key_value_adjoint, kinds,
-        [(back_raw, channels, 0), (key_conv, tokens, 1), (value_conv, tokens, 1),
-         (after, rim, 1), (following, (2, 2, chunk), 2), (short_taps, taps_block, 2)],
-        [((rows, width), BF16, tokens, 1)] * 2, 3 * 2**20,
+        key_value_rim, 1,
+        [(back_raw[:, rows - RIM :].T, tail, None), (key_conv, last, None), (value_conv, last, None),
+         (after, (2, width), None), (following, (2, 2, width), None), (short_taps, (3, 3, width), None),
+         (grads[0], None, None), (grads[1], None, None)],
+        [((rows, width), BF16, last, None)] * 2, 2**20, alias=((6, 0), (7, 1)),
     )
     return (mixed, query_grad, key_grad, value_grad, filter_grad)
 

time: 225 us -> 216 us (0.960)
  blocking collectives: 20.1 us -> 13.7 us
  local copies, waits for them, and re-layouts: 14.4 us -> 9.6 us
  waiting for transfers between devices: 84.1 us -> 80.1 us
  Pallas kernels: 22.9 us -> 26.6 us
  starting transfers between devices: 66.2 us -> 69 us
    ppermute x1, waiting for transfers between devices: 11.9 us -> 0.01 us  [partner(): return lax.ppermute(value, axis, [(0, 1), (1, 0)])]
    all_gather x1, waiting for transfers between devices: 9.76 us -> 0.01 us  [per_device(): lax.all_gather(turned, COLUMN, axis=0).reshape(4, 2, 4, rows, features)]
    all_to_all x1, waiting for transfers between devices: 13.8 us -> 23 us  [per_device(): lax.all_to_all(product.reshape(BLOCKS, CHANNELS, LANES), SEQ, 0, 0, tiled...]
    all_to_all x0 -> x1, waiting for transfers between devices: none -> 8.65 us  [per_device(): lax.all_to_all(gated.reshape(8, rows, chunk), PLANE, 0, 0, tiled=True)]
    all_to_all x1, blocking collectives: 20.1 us -> 13.7 us  [per_device(): lax.all_to_all(partial.reshape(8, chunk, rows), PLANE, 0, 0, tiled=True)]
    all_to_all x1, waiting for transfers between devices: 9.45 us -> 3.45 us  [per_device(): lax.all_to_all(long_owned, SEQ, 0, 0, tiled=True).reshape(width, rows)]
    ppermute x3, waiting for transfers between devices: 0.01 us -> 5.86 us  [across(): lax.ppermute(value, ('xh', 'xl'), [(i, i ^ 2 * dx + dl) for i in range(4)])]
    all_to_all x0 -> x1, starting transfers between devices: none -> 4.84 us  [per_device(): lax.all_to_all(gated.reshape(8, rows, chunk), PLANE, 0, 0, tiled=True)]
  transfers between devices with their start and end apart: 15 -> 16, of which waited for: 9 -> 10; matrix products, arithmetic and copies ran while one was open for 1% -> 1% of each run, Pallas kernels for 8% -> 10%
where the time goes in v4:
time: 216 us; the launch traced here: 215 us
  waiting for transfers between devices  80.1 us (37%)
  starting transfers between devices  69 us (32%)
  Pallas kernels  26.6 us (12%)
  between operations  14.4 us (7%)
  blocking collectives  13.7 us (6%)
  local copies, waits for them, and re-layouts  9.6 us (4%)
    all_to_all x1, waiting for transfers between devices, per_device(): lax.all_to_all(product.reshape(BLOCKS, CHANNELS, LANES), SEQ, 0, 0, tiled...  23 us
    pallas_call x9, Pallas kernels, run_blocks(): pl.pallas_call(kernel, grid=(steps,), in_specs=[spec(block, axis) for _,...  21.7 us
    all_to_all x1, starting transfers between devices, per_device(): lax.all_to_all(product.reshape(BLOCKS, CHANNELS, LANES), SEQ, 0, 0, tiled...  19.4 us
    all_to_all x1, waiting for transfers between devices, per_device(): lax.all_to_all(long_grad.reshape(BLOCKS, CHANNELS, LANES), SEQ, 0, 0, til...  18.4 us
    all_to_all x1, blocking collectives, per_device(): lax.all_to_all(partial.reshape(8, chunk, rows), PLANE, 0, 0, tiled=True)  13.7 us
    ppermute x4, waiting for transfers between devices, shift(): lax.ppermute(value, SEQ, [(i, i + steps) for i in range(first, last)])  11.3 us
    all_to_all x1, starting transfers between devices, per_device(): lax.all_to_all(long_grad.reshape(BLOCKS, CHANNELS, LANES), SEQ, 0, 0, til...  9.6 us
    all_to_all x1, waiting for transfers between devices, per_device(): lax.all_to_all(back_owned, SEQ, 0, 0, tiled=True).reshape(width, rows)  9.42 us
  transfers between devices with their start and end apart: 16, of which 10 were waited for; matrix products, arithmetic and copies ran while one was open for 1% of the time, Pallas kernels for 10%

profile of v4, /device:TPU:1, one launch (start us, length us, event | category | flops | bytes accessed | tf_op | source)
XLA Modules:
  0.0 214.8 jit_solution(12706619835169743858)
XLA Ops:
  7.2 0.8 slice_bitcast_fusion.5
  8.0 0.7 slice_bitcast_fusion.3
  8.8 6.0 %collective-permute-start.1 = (bf16[128,512]{1,0:T(8,128)(2,1)}, bf16[128,512]{1,0:T(8,128)(2,1)S(1)}, u32[]{:S(2)}, u32[]{:S(2)}) collective-permute-start(bf16[128,512]{1,0:T(8,128)(2,1)} %param.14), channel_id=1, source_target_pairs={{0,0},{1,16},{4,8},{5,24},{8,256},{9,272},{12,264},{13,280},{16,1}... | collective-permute-start | bytes 393224 | tf_op jit(solution)/shard_map/ppermute | solution.py:317
  14.8 1.9 collective-permute-start
  16.7 2.4 %collective-permute-done.before_ref = bf16[3,2,1024]{2,1,0:T(2,128)(2,1)S(1)} collective-permute-done((bf16[3,2,1024]{2,1,0:T(2,128)(2,1)S(1)}, bf16[3,2,1024]{2,1,0:T(2,128)(2,1)S(1)}, u32[]{:S(2)}, u32[]{:S(2)}) %collective-permute-start) | collective-permute-done | bytes 12320 | tf_op jit(solution)/shard_map/ppermute | solution.py:299
  19.1 0.7 copy-done.15
  19.8 2.2 %shard_map.128._ = bf16[1024,128]{1,0:T(8,128)(2,1)} custom-call(bf16[128,1024]{1,0:T(8,128)(2,1)} %k_ref.3, bf16[128,1024]{1,0:T(8,128)(2,1)} %v_ref.3, bf16[3,2,1024]{2,1,0:T(2,128)(2,1)} %copy-done.16, f32[3,3,1024]{2,1,0:T(4,128)} %taps_ref.9), custom_call_target="tpu_custom_call" | custom-call | flops 1000000 | bytes 1048576 | tf_op jit(solution)/shard_map/pallas_call | solution.py:156
  22.1 19.4 %all-to-all-start = ((bf16[64,16,128]{2,1,0:T(8,128)(2,1)}), bf16[64,16,128]{2,1,0:T(8,128)(2,1)S(1)}, u32[]{:S(2)}, u32[]{:S(2)}) async-start(bf16[64,16,128]{2,1,0:T(8,128)(2,1)} %bitcast.46), calls=%async_computation | async-start | bytes 524288 | tf_op jit(solution)/shard_map/all_to_all | solution.py:352
  41.5 1.0 copy-done.6
  42.5 1.0 copy-done.7
  43.5 0.8 copy-done.10
  44.4 0.5 shard_map.129.filter_spectrum
  44.9 23.0 %all-to-all-done.product_ref = bf16[64,16,128]{2,1,0:T(8,128)(2,1)S(1)} async-done(((bf16[64,16,128]{2,1,0:T(8,128)(2,1)}), bf16[64,16,128]{2,1,0:T(8,128)(2,1)S(1)}, u32[]{:S(2)}, u32[]{:S(2)}) %all-to-all-start) | async-done | bytes 262176 | tf_op jit(solution)/shard_map/all_to_all | solution.py:352
  67.9 1.0 copy-done.8
  68.9 1.8 shard_map.130
  70.7 4.2 %all-to-all-start.1 = ((bf16[64,16,128]{2,1,0:T(8,128)(2,1)}), bf16[64,16,128]{2,1,0:T(8,128)(2,1)S(1)}, u32[]{:S(2)}, u32[]{:S(2)}) async-start(bf16[64,16,128]{2,1,0:T(8,128)(2,1)} %get-tuple-element.28), calls=%async_computation.1 | async-start | bytes 524288 | tf_op jit(solution)/shard_map/all_to_all | solution.py:363
  75.0 4.9 %collective-permute-start.2 = (bf16[512,128]{1,0:T(8,128)(2,1)S(1)}, bf16[512,128]{1,0:T(8,128)(2,1)S(1)}, u32[]{:S(2)}, u32[]{:S(2)}) collective-permute-start(bf16[512,128]{1,0:T(8,128)(2,1)S(1)} %bitcast.48), channel_id=1, source_target_pairs={{0,256},{4,260},{256,0},{260,4},{1,257},{5,261},{257,1},{261,5},{2... | collective-permute-start | bytes 393224 | tf_op jit(solution)/shard_map/ppermute | solution.py:309
  79.9 1.9 collective-permute-start.3
  81.8 2.2 %collective-permute-start.4 = (bf16[512,128]{1,0:T(8,128)(2,1)S(1)}, bf16[512,128]{1,0:T(8,128)(2,1)S(1)}, u32[]{:S(2)}, u32[]{:S(2)}) collective-permute-start(bf16[512,128]{1,0:T(8,128)(2,1)S(1)} %bitcast.50), channel_id=1, source_target_pairs={{0,260},{4,256},{256,4},{260,0},{1,261},{5,257},{257,5},{261,1},{2... | collective-permute-start | bytes 393224 | tf_op jit(solution)/shard_map/ppermute | solution.py:309
  84.1 3.0 %collective-permute-done.3 = bf16[512,128]{1,0:T(8,128)(2,1)S(1)} collective-permute-done((bf16[512,128]{1,0:T(8,128)(2,1)S(1)}, bf16[512,128]{1,0:T(8,128)(2,1)S(1)}, u32[]{:S(2)}, u32[]{:S(2)}) %collective-permute-start.3) | collective-permute-done | bytes 131104 | tf_op jit(solution)/shard_map/ppermute | solution.py:309
  87.1 2.8 %collective-permute-done.4 = bf16[512,128]{1,0:T(8,128)(2,1)S(1)} collective-permute-done((bf16[512,128]{1,0:T(8,128)(2,1)S(1)}, bf16[512,128]{1,0:T(8,128)(2,1)S(1)}, u32[]{:S(2)}, u32[]{:S(2)}) %collective-permute-start.4) | collective-permute-done | bytes 131104 | tf_op jit(solution)/shard_map/ppermute | solution.py:309
  90.1 3.6 %collective-permute-start.5 = (bf16[2,512,256]{2,1,0:T(8,128)(2,1)S(1)}, bf16[2,512,256]{2,1,0:T(8,128)(2,1)S(1)}, u32[]{:S(2)}, u32[]{:S(2)}) collective-permute-start(bf16[2,512,256]{2,1,0:T(8,128)(2,1)S(1)} %get-tuple-element.46), channel_id=1, source_target_pairs={{0,1},{1,0},{2,3},{3,2},{4,5},{5,4},{6,7},{7,6},{8,9},{9,8},{10,11... | collective-permute-start | bytes 1572872 | tf_op jit(solution)/shard_map/ppermute | solution.py:303
  93.7 3.7 %shard_map.131 = (f32[128,1024]{1,0:T(8,128)}, f32[128,1024]{1,0:T(8,128)}, f32[128,1024]{1,0:T(8,128)}, f32[1024,128]{1,0:T(8,128)}) custom-call(bf16[128,1024]{1,0:T(8,128)(2,1)} %q_ref.1, bf16[128,1024]{1,0:T(8,128)(2,1)} %k_ref.3, bf16[128,1024]{1,0:T(8,128)(2,1)} %v_ref.3, bf16[3,2,1024]{2,1,0:T(2,128)(2,1)} %copy-done.16, f32[3,3,1024]{2,1,0:T(4,128)} %taps_ref.9, ...), custom_call_target="tpu_custom_call" | custom-call | flops 1000000 | bytes 3145728 | tf_op jit(solution)/shard_map/pallas_call | solution.py:156
  97.4 3.5 %all-to-all-done.1 = bf16[64,16,128]{2,1,0:T(8,128)(2,1)S(1)} async-done(((bf16[64,16,128]{2,1,0:T(8,128)(2,1)}), bf16[64,16,128]{2,1,0:T(8,128)(2,1)S(1)}, u32[]{:S(2)}, u32[]{:S(2)}) %all-to-all-start.1) | async-done | bytes 262176 | tf_op jit(solution)/shard_map/all_to_all | solution.py:363
  100.8 1.0 copy-done.5
  101.9 1.1 shard_map.132
  102.9 4.8 %all-to-all-start.2 = ((bf16[8,128,256]{2,1,0:T(8,128)(2,1)}), bf16[8,128,256]{2,1,0:T(8,128)(2,1)S(1)}, u32[]{:S(2)}, u32[]{:S(2)}) async-start(bf16[8,128,256]{2,1,0:T(8,128)(2,1)} %bitcast.47), calls=%async_computation.2 | async-start | bytes 1048576 | tf_op jit(solution)/shard_map/all_to_all | solution.py:372
  107.8 0.8 copy-done.13
  108.6 1.1 pad_maximum_fusion.gradient_ref
  109.8 8.6 %all-to-all-done.2._ = bf16[8,128,256]{2,1,0:T(8,128)(2,1)S(1)} async-done(((bf16[8,128,256]{2,1,0:T(8,128)(2,1)}), bf16[8,128,256]{2,1,0:T(8,128)(2,1)S(1)}, u32[]{:S(2)}, u32[]{:S(2)}) %all-to-all-start.2) | async-done | bytes 524320 | tf_op jit(solution)/shard_map/all_to_all | solution.py:372
  118.4 4.3 %shard_map.134 = bf16[2,4,256,128]{3,2,1,0:T(8,128)(2,1)S(1)} custom-call(s32[4]{0:T(128)S(1)} %pad_add_fusion.place_ref, bf16[2,2,512,256]{3,2,1,0:T(8,128)(2,1)S(1)} %pad_maximum_fusion.gradient_ref, bf16[4,2,4,128,512]{4,3,2,1,0:T(8,128)(2,1)} %bitcast.44, bf16[8,128,256]{2,1,0:T(8,128)(2,1)S(1)} %all-to-all-done.2._), custom_call_target="tpu_custom_call" | custom-call | flops 1073741824 | bytes 6291456 | tf_op jit(solution)/shard_map/pallas_call | solution.py:156
  122.7 13.7 %all_to_all.30.parts_ref = bf16[8,256,128]{2,1,0:T(8,128)(2,1)S(1)} all-to-all(bf16[8,256,128]{2,1,0:T(8,128)(2,1)S(1)} %bitcast.42), channel_id=1, replica_groups=mesh['xh'=2,'zy'=4,'zh'=2,'zb'=2,'co'=2,'xl'=2,'yh'=2,'yl'=2] {'xh','yh'..., dimensions={0} | all-to-all | bytes 1048576 | tf_op jit(solution)/shard_map/all_to_all | solution.py:381
  136.4 1.0 shard_map.135
  137.4 9.6 %all-to-all-start.4 = ((bf16[64,16,128]{2,1,0:T(8,128)(2,1)}), bf16[64,16,128]{2,1,0:T(8,128)(2,1)S(1)}, u32[]{:S(2)}, u32[]{:S(2)}) async-start(bf16[64,16,128]{2,1,0:T(8,128)(2,1)} %bitcast.53), calls=%async_computation.5 | async-start | bytes 524288 | tf_op jit(solution)/shard_map/all_to_all | solution.py:387
  147.1 5.2 %shard_map.133 = bf16[2,2,2,128,512]{4,3,2,1,0:T(8,128)(2,1)} custom-call(bf16[2,4,128,256]{3,2,1,0:T(8,128)(2,1)S(1)} %bitcast.36, bf16[4,2,4,128,512]{4,3,2,1,0:T(8,128)(2,1)} %bitcast.45), custom_call_target="tpu_custom_call" | custom-call | flops 1073741824 | bytes 6291456 | tf_op jit(solution)/shard_map/pallas_call | solution.py:156
  152.4 18.4 %all-to-all-done.4.grad_ref = bf16[64,16,128]{2,1,0:T(8,128)(2,1)S(1)} async-done(((bf16[64,16,128]{2,1,0:T(8,128)(2,1)}), bf16[64,16,128]{2,1,0:T(8,128)(2,1)S(1)}, u32[]{:S(2)}, u32[]{:S(2)}) %all-to-all-start.4) | async-done | bytes 262176 | tf_op jit(solution)/shard_map/all_to_all | solution.py:387
  170.8 1.0 copy-done.12
  171.8 2.5 %shard_map.136 = (bf16[64,16,128]{2,1,0:T(8,128)(2,1)}, f32[16,8192]{1,0:T(8,128)}) custom-call(bf16[64,16,128]{2,1,0:T(8,128)(2,1)S(1)} %all-to-all-done.4.grad_ref, bf16[1024,256]{1,0:T(8,128)(2,1)S(1)} %shard_map.129.filter_spectrum, bf16[1024,256]{1,0:T(8,128)(2,1)S(1)} %copy-done.12, bf16[256,640]{1,0:T(8,128)(2,1)S(1)} %copy-done.9, ...), custom_call_target="tpu_custom_call" | custom-call | flops 503316480 | bytes 4194304 | tf_op jit(solution)/shard_map/pallas_call | solution.py:135
  174.4 4.2 %all-to-all-start.5 = ((bf16[64,16,128]{2,1,0:T(8,128)(2,1)}), bf16[64,16,128]{2,1,0:T(8,128)(2,1)S(1)}, u32[]{:S(2)}, u32[]{:S(2)}) async-start(bf16[64,16,128]{2,1,0:T(8,128)(2,1)} %get-tuple-element.34), calls=%async_computation.6 | async-start | bytes 524288 | tf_op jit(solution)/shard_map/all_to_all | solution.py:415
  178.6 2.2 %collective-permute-start.8 = (f32[2,2,1024]{2,1,0:T(2,128)S(1)}, f32[2,2,1024]{2,1,0:T(2,128)S(1)}, u32[]{:S(2)}, u32[]{:S(2)}) collective-permute-start(f32[2,2,1024]{2,1,0:T(2,128)S(1)} %pad_maximum_fusion.2), channel_id=1, source_target_pairs={{8,0},{16,8},{24,16},{32,24},{40,32},{48,40},{56,48},{64,56},{72,6... | collective-permute-start | bytes 49160 | tf_op jit(solution)/shard_map/ppermute | solution.py:299
  181.1 1.9 collective-permute-start.6
  183.0 8.1 %collective-permute-done.6.after_ref = f32[2,1024]{1,0:T(2,128)S(1)} collective-permute-done((f32[2,1024]{1,0:T(2,128)S(1)}, f32[2,1024]{1,0:T(2,128)S(1)}, u32[]{:S(2)}, u32[]{:S(2)}) %collective-permute-start.6) | collective-permute-done | bytes 8224 | tf_op jit(solution)/shard_map/ppermute | solution.py:299
  191.1 1.6 shard_map.137
  192.8 9.4 %all-to-all-done.5 = bf16[64,16,128]{2,1,0:T(8,128)(2,1)S(1)} async-done(((bf16[64,16,128]{2,1,0:T(8,128)(2,1)}), bf16[64,16,128]{2,1,0:T(8,128)(2,1)S(1)}, u32[]{:S(2)}, u32[]{:S(2)}) %all-to-all-start.5) | async-done | bytes 262176 | tf_op jit(solution)/shard_map/all_to_all | solution.py:415
  202.3 1.9 collective-permute-start.7
  204.5 1.9 shard_map.138
  206.4 0.8 collective-permute-done.7.after_ref
  207.2 0.7 shard_map.139
  (50 shorter events, 1.1 us)
Async XLA Ops:
  7.2 67.7 %copy-start.14 = (bf16[128,512]{1,0:T(8,128)(2,1)S(1)}, bf16[128,512]{1,0:T(8,128)(2,1)}, u32[]{:S(2)}) copy-start(bf16[128,512]{1,0:T(8,128)(2,1)} %param.15) | copy-start | bytes 393220
  7.2 111.3 %all-gather.3.cloned.1.call-start = ((), (), s32[]{:S(2)}) async-start(), calls=%async_computation.8 | async-start | bytes 4325376 | tf_op jit(solution)/shard_map/all_gather | solution.py:330
  8.8 10.4 %collective-permute-start.1 = (bf16[128,512]{1,0:T(8,128)(2,1)}, bf16[128,512]{1,0:T(8,128)(2,1)S(1)}, u32[]{:S(2)}, u32[]{:S(2)}) collective-permute-start(bf16[128,512]{1,0:T(8,128)(2,1)} %param.14), channel_id=1, source_target_pairs={{0,0},{1,16},{4,8},{5,24},{8,256},{9,272},{12,264},{13,280},{16,1}... | collective-permute-start | bytes 393224 | tf_op jit(solution)/shard_map/ppermute | solution.py:317
  14.8 4.3 %collective-permute-start = (bf16[3,2,1024]{2,1,0:T(2,128)(2,1)S(1)}, bf16[3,2,1024]{2,1,0:T(2,128)(2,1)S(1)}, u32[]{:S(2)}, u32[]{:S(2)}) collective-permute-start(bf16[3,2,1024]{2,1,0:T(2,128)(2,1)S(1)} %pad_maximum_fusion.3), channel_id=1, source_target_pairs={{0,8},{8,16},{16,24},{24,32},{32,40},{40,48},{48,56},{56,64},{64,7... | collective-permute-start | bytes 36872 | tf_op jit(solution)/shard_map/ppermute | solution.py:299
  19.1 0.7 copy-start.16
  19.1 0.7 copy-start.15
  22.1 45.8 %all-to-all-start = ((bf16[64,16,128]{2,1,0:T(8,128)(2,1)}), bf16[64,16,128]{2,1,0:T(8,128)(2,1)S(1)}, u32[]{:S(2)}, u32[]{:S(2)}) async-start(bf16[64,16,128]{2,1,0:T(8,128)(2,1)} %bitcast.46), calls=%async_computation | async-start | bytes 524288 | tf_op jit(solution)/shard_map/all_to_all | solution.py:352
  41.5 1.0 copy-start.6
  42.5 1.0 copy-start.7
  43.5 0.8 copy-start.10
  67.9 1.0 copy-start.8
  70.7 30.2 %all-to-all-start.1 = ((bf16[64,16,128]{2,1,0:T(8,128)(2,1)}), bf16[64,16,128]{2,1,0:T(8,128)(2,1)S(1)}, u32[]{:S(2)}, u32[]{:S(2)}) async-start(bf16[64,16,128]{2,1,0:T(8,128)(2,1)} %get-tuple-element.28), calls=%async_computation.1 | async-start | bytes 524288 | tf_op jit(solution)/shard_map/all_to_all | solution.py:363
  75.0 9.0 %collective-permute-start.2 = (bf16[512,128]{1,0:T(8,128)(2,1)S(1)}, bf16[512,128]{1,0:T(8,128)(2,1)S(1)}, u32[]{:S(2)}, u32[]{:S(2)}) collective-permute-start(bf16[512,128]{1,0:T(8,128)(2,1)S(1)} %bitcast.48), channel_id=1, source_target_pairs={{0,256},{4,260},{256,0},{260,4},{1,257},{5,261},{257,1},{261,5},{2... | collective-permute-start | bytes 393224 | tf_op jit(solution)/shard_map/ppermute | solution.py:309
  79.9 7.2 %collective-permute-start.3 = (bf16[512,128]{1,0:T(8,128)(2,1)S(1)}, bf16[512,128]{1,0:T(8,128)(2,1)S(1)}, u32[]{:S(2)}, u32[]{:S(2)}) collective-permute-start(bf16[512,128]{1,0:T(8,128)(2,1)S(1)} %bitcast.49), channel_id=1, source_target_pairs={{0,4},{4,0},{256,260},{260,256},{1,5},{5,1},{257,261},{261,257},{2... | collective-permute-start | bytes 393224 | tf_op jit(solution)/shard_map/ppermute | solution.py:309
  81.8 8.1 %collective-permute-start.4 = (bf16[512,128]{1,0:T(8,128)(2,1)S(1)}, bf16[512,128]{1,0:T(8,128)(2,1)S(1)}, u32[]{:S(2)}, u32[]{:S(2)}) collective-permute-start(bf16[512,128]{1,0:T(8,128)(2,1)S(1)} %bitcast.50), channel_id=1, source_target_pairs={{0,260},{4,256},{256,4},{260,0},{1,261},{5,257},{257,5},{261,1},{2... | collective-permute-start | bytes 393224 | tf_op jit(solution)/shard_map/ppermute | solution.py:309
  90.1 17.8 %collective-permute-start.5 = (bf16[2,512,256]{2,1,0:T(8,128)(2,1)S(1)}, bf16[2,512,256]{2,1,0:T(8,128)(2,1)S(1)}, u32[]{:S(2)}, u32[]{:S(2)}) collective-permute-start(bf16[2,512,256]{2,1,0:T(8,128)(2,1)S(1)} %get-tuple-element.46), channel_id=1, source_target_pairs={{0,1},{1,0},{2,3},{3,2},{4,5},{5,4},{6,7},{7,6},{8,9},{9,8},{10,11... | collective-permute-start | bytes 1572872 | tf_op jit(solution)/shard_map/ppermute | solution.py:303
  100.8 1.0 copy-start.5
  102.9 15.5 %all-to-all-start.2 = ((bf16[8,128,256]{2,1,0:T(8,128)(2,1)}), bf16[8,128,256]{2,1,0:T(8,128)(2,1)S(1)}, u32[]{:S(2)}, u32[]{:S(2)}) async-start(bf16[8,128,256]{2,1,0:T(8,128)(2,1)} %bitcast.47), calls=%async_computation.2 | async-start | bytes 1048576 | tf_op jit(solution)/shard_map/all_to_all | solution.py:372
  107.8 0.8 copy-start.13
  109.8 26.6 %copy-start.4 = (f32[1024,128]{1,0:T(8,128)S(1)}, f32[1024,128]{1,0:T(8,128)}, u32[]{:S(2)}) copy-start(f32[1024,128]{1,0:T(8,128)} %get-tuple-element.31.qc_ref) | copy-start | bytes 1572868
  136.4 34.4 %copy-start.9 = (bf16[256,640]{1,0:T(8,128)(2,1)S(1)}, bf16[256,640]{1,0:T(8,128)(2,1)}, u32[]{:S(2)}) copy-start(bf16[256,640]{1,0:T(8,128)(2,1)} %constant.18.clone.steps) | copy-start | bytes 983044
  136.4 34.4 %copy-start.11 = (f32[64,256]{1,0:T(8,128)S(1)}, f32[64,256]{1,0:T(8,128)}, u32[]{:S(2)}) copy-start(f32[64,256]{1,0:T(8,128)} %constant.19.clone.turns) | copy-start | bytes 196612
  137.4 33.4 %all-to-all-start.4 = ((bf16[64,16,128]{2,1,0:T(8,128)(2,1)}), bf16[64,16,128]{2,1,0:T(8,128)(2,1)S(1)}, u32[]{:S(2)}, u32[]{:S(2)}) async-start(bf16[64,16,128]{2,1,0:T(8,128)(2,1)} %bitcast.53), calls=%async_computation.5 | async-start | bytes 524288 | tf_op jit(solution)/shard_map/all_to_all | solution.py:387
  147.0 60.9 %reduce-scatter.2.cloned.1.call-start = ((), (), s32[]{:S(2)}) async-start(), calls=%async_computation.7 | async-start | bytes 1179648 | tf_op jit(solution)/shard_map/reduce_scatter | solution.py:403
  147.1 31.5 %copy-start.1 = (f32[128,1024]{1,0:T(8,128)S(1)}, f32[128,1024]{1,0:T(8,128)}, u32[]{:S(2)}) copy-start(f32[128,1024]{1,0:T(8,128)} %get-tuple-element.38.vc_ref) | copy-start | bytes 1572868
  147.1 31.5 %copy-start = (f32[128,1024]{1,0:T(8,128)S(1)}, f32[128,1024]{1,0:T(8,128)}, u32[]{:S(2)}) copy-start(f32[128,1024]{1,0:T(8,128)} %get-tuple-element.37.kc_ref) | copy-start | bytes 1572868
  147.1 33.7 %copy-start.2 = (f32[1024,128]{1,0:T(8,128)S(1)}, f32[1024,128]{1,0:T(8,128)}, u32[]{:S(2)}) copy-start(f32[1024,128]{1,0:T(8,128)} %get-tuple-element.35.qg_ref) | copy-start | bytes 1572868
  147.1 44.0 %copy-start.3 = (f32[3,3,1024]{2,1,0:T(4,128)S(1)}, f32[3,3,1024]{2,1,0:T(4,128)}, u32[]{:S(2)}) copy-start(f32[3,3,1024]{2,1,0:T(4,128)} %taps_ref.9) | copy-start | bytes 110596
  170.8 1.0 copy-start.12
  174.4 27.8 %all-to-all-start.5 = ((bf16[64,16,128]{2,1,0:T(8,128)(2,1)}), bf16[64,16,128]{2,1,0:T(8,128)(2,1)S(1)}, u32[]{:S(2)}, u32[]{:S(2)}) async-start(bf16[64,16,128]{2,1,0:T(8,128)(2,1)} %get-tuple-element.34), calls=%async_computation.6 | async-start | bytes 524288 | tf_op jit(solution)/shard_map/all_to_all | solution.py:415
  178.6 27.8 %collective-permute-start.8 = (f32[2,2,1024]{2,1,0:T(2,128)S(1)}, f32[2,2,1024]{2,1,0:T(2,128)S(1)}, u32[]{:S(2)}, u32[]{:S(2)}) collective-permute-start(f32[2,2,1024]{2,1,0:T(2,128)S(1)} %pad_maximum_fusion.2), channel_id=1, source_target_pairs={{8,0},{16,8},{24,16},{32,24},{40,32},{48,40},{56,48},{64,56},{72,6... | collective-permute-start | bytes 49160 | tf_op jit(solution)/shard_map/ppermute | solution.py:299
  181.1 10.0 %collective-permute-start.6 = (f32[2,1024]{1,0:T(2,128)S(1)}, f32[2,1024]{1,0:T(2,128)S(1)}, u32[]{:S(2)}, u32[]{:S(2)}) collective-permute-start(f32[2,1024]{1,0:T(2,128)S(1)} %slice_bitcast_fusion), channel_id=1, source_target_pairs={{8,0},{16,8},{24,16},{32,24},{40,32},{48,40},{56,48},{64,56},{72,6... | collective-permute-start | bytes 24584 | tf_op jit(solution)/shard_map/ppermute | solution.py:299
  202.3 4.9 %collective-permute-start.7 = (bf16[2,1024]{1,0:T(2,128)(2,1)S(1)}, bf16[2,1024]{1,0:T(2,128)(2,1)S(1)}, u32[]{:S(2)}, u32[]{:S(2)}) collective-permute-start(bf16[2,1024]{1,0:T(2,128)(2,1)S(1)} %bitcast.54), channel_id=1, source_target_pairs={{8,0},{16,8},{24,16},{32,24},{40,32},{48,40},{56,48},{64,56},{72,6... | collective-permute-start | bytes 12296 | tf_op jit(solution)/shard_map/ppermute | solution.py:299
Sparse Core Ops, SparseCore 0:
  19.9 95.0 all-gather.2
  152.5 42.0 reduce-scatter.1

commit v5 on v4

--- a/solution.py
+++ b/solution.py
@@ -37,18 +37,27 @@
     first_table = np.concatenate([np.cos(first), -np.sin(first)], axis=0)
     cosine, sine = np.cos(second), np.sin(second)
     second_table = np.block([[cosine, -sine], [sine, cosine]])
-    steps = np.zeros((2 * LANES, 5 * LANES))
-    steps[:, : 2 * LANES] = second_table
-    steps[:, 2 * LANES : 4 * LANES] = second_table.T
+    steps = np.zeros((2 * LANES + BLOCKS, 5 * LANES))
+    steps[: 2 * LANES, : 2 * LANES] = second_table
+    steps[: 2 * LANES, 2 * LANES : 4 * LANES] = second_table.T
     steps[: 2 * BLOCKS, 4 * LANES : 4 * LANES + BLOCKS] = first_table
     steps[2 * BLOCKS : 3 * BLOCKS, 4 * LANES : 4 * LANES + 2 * BLOCKS] = first_table.T / LENGTH
     turns = np.concatenate([np.cos(twist), np.sin(twist)], axis=1)
-    return jnp.asarray(steps, BF16), jnp.asarray(turns, F32)
-
-
-def to_spectrum(grid_ref, turned_ref, steps, turns):
+    coarse = turns.astype(BF16).astype(np.float64)
+    steps[2 * LANES :, : 2 * LANES] = coarse
+    steps[2 * LANES :, 2 * LANES : 4 * LANES] = turns - coarse
+    return jnp.asarray(steps, BF16)
+
+
+def twist_of(steps):
+    parts = steps[2 * LANES :].astype(F32)
+    turns = parts[:, : 2 * LANES] + parts[:, 2 * LANES : 4 * LANES]
+    return turns[:, :LANES], turns[:, LANES:]
+
+
+def to_spectrum(grid_ref, turned_ref, steps):
     first = steps[: 2 * BLOCKS, 4 * LANES : 4 * LANES + BLOCKS]
-    cos_twist, sin_twist = turns[:, :LANES], turns[:, LANES:]
+    cos_twist, sin_twist = twist_of(steps)
     for c in range(CHANNELS):
         grid = grid_ref[pl.ds(c, BLOCKS, stride=CHANNELS), :].astype(BF16)
         section = jnp.dot(first, grid, preferred_element_type=F32)
@@ -56,14 +65,14 @@
         rows = slice(c * BLOCKS, (c + 1) * BLOCKS)
         turned_ref[rows, :LANES] = (real * cos_twist + imag * sin_twist).astype(BF16)
         turned_ref[rows, LANES:] = (imag * cos_twist - real * sin_twist).astype(BF16)
-    return jnp.dot(turned_ref[...], steps[:, : 2 * LANES], preferred_element_type=F32)
-
-
-def from_spectrum(spectrum, grid_ref, section_ref, steps, turns):
+    return jnp.dot(turned_ref[...], steps[: 2 * LANES, : 2 * LANES], preferred_element_type=F32)
+
+
+def from_spectrum(spectrum, grid_ref, section_ref, steps):
     first_back = steps[2 * BLOCKS : 3 * BLOCKS, 4 * LANES : 4 * LANES + 2 * BLOCKS]
-    cos_twist, sin_twist = turns[:, :LANES], turns[:, LANES:]
+    cos_twist, sin_twist = twist_of(steps)
     section_ref[...] = jnp.dot(
-        spectrum, steps[:, 2 * LANES : 4 * LANES], preferred_element_type=F32
+        spectrum, steps[: 2 * LANES, 2 * LANES : 4 * LANES], preferred_element_type=F32
     )
     for c in range(CHANNELS):
         rows = slice(c * BLOCKS, (c + 1) * BLOCKS)
@@ -76,44 +85,46 @@
         )
 
 
-def filter_kernel(filter_ref, steps, turns, spectrum_ref, grid, turned):
+def filter_kernel(filter_ref, steps, spectrum_ref, grid, turned):
     for b in range(BLOCKS):
         grid[b * CHANNELS : (b + 1) * CHANNELS, :] = filter_ref[:, b * LANES : (b + 1) * LANES]
-    spectrum_ref[...] = to_spectrum(grid, turned, steps, turns).astype(BF16)
+    spectrum_ref[...] = to_spectrum(grid, turned, steps).astype(BF16)
 
 
 def forward_kernel(
-    product_ref, filter_spectrum, steps, turns, long_ref, product_spectrum, grid, turned, section
+    product_ref, filter_spectrum, steps, long_ref, product_spectrum, grid, turned, section
 ):
     grid[...] = product_ref[...].astype(F32).reshape(BLOCKS * CHANNELS, LANES)
-    own = to_spectrum(grid, turned, steps, turns)
+    own = to_spectrum(grid, turned, steps)
     product_spectrum[...] = own.astype(BF16)
     own_re, own_im = own[:, :LANES], own[:, LANES:]
     other = filter_spectrum[...].astype(F32)
     other_re, other_im = other[:, :LANES], other[:, LANES:]
     turned[:, :LANES] = (own_re * other_re - own_im * other_im).astype(BF16)
     turned[:, LANES:] = (own_re * other_im + own_im * other_re).astype(BF16)
-    from_spectrum(turned[...], grid, section, steps, turns)
+    from_spectrum(turned[...], grid, section, steps)
     long_ref[...] = grid[...].reshape(BLOCKS, CHANNELS, LANES).astype(BF16)
 
 
-def backward_kernel(
-    grad_ref, filter_spectrum, product_spectrum, steps, turns,
-    back_ref, filter_grad_ref, grid, turned, section,
+def correlate(grad_ref, other, grid, turned, section, steps):
+    grid[...] = grad_ref[...].astype(F32).reshape(BLOCKS * CHANNELS, LANES)
+    own = to_spectrum(grid, turned, steps)
+    own_re, own_im = own[:, :LANES], own[:, LANES:]
+    other_re, other_im = other[:, :LANES].astype(F32), other[:, LANES:].astype(F32)
+    turned[:, :LANES] = (own_re * other_re + own_im * other_im).astype(BF16)
+    turned[:, LANES:] = (own_im * other_re - own_re * other_im).astype(BF16)
+    from_spectrum(turned[...], grid, section, steps)
+
+
+def backward_kernel(grad_ref, filter_spectrum, steps, back_ref, grid, turned, section):
+    correlate(grad_ref, filter_spectrum, grid, turned, section, steps)
+    back_ref[...] = grid[...].reshape(BLOCKS, CHANNELS, LANES).astype(BF16)
+
+
+def filter_grad_kernel(
+    grad_ref, product_spectrum, steps, _, filter_grad_ref, grid, turned, section
 ):
-    grid[...] = grad_ref[...].astype(F32).reshape(BLOCKS * CHANNELS, LANES)
-    own = to_spectrum(grid, turned, steps, turns)
-    own_re, own_im = own[:, :LANES], own[:, LANES:]
-
-    def correlate(other):
-        other_re, other_im = other[:, :LANES].astype(F32), other[:, LANES:].astype(F32)
-        turned[:, :LANES] = (own_re * other_re + own_im * other_im).astype(BF16)
-        turned[:, LANES:] = (own_im * other_re - own_re * other_im).astype(BF16)
-        from_spectrum(turned[...], grid, section, steps, turns)
-
-    correlate(filter_spectrum)
-    back_ref[...] = grid[...].reshape(BLOCKS, CHANNELS, LANES).astype(BF16)
-    correlate(product_spectrum)
+    correlate(grad_ref, product_spectrum, grid, turned, section, steps)
     for b in range(BLOCKS):
         filter_grad_ref[:, b * LANES : (b + 1) * LANES] = grid[
             b * CHANNELS : (b + 1) * CHANNELS, :
@@ -330,8 +341,8 @@
     weight = lax.all_gather(turned, COLUMN, axis=0).reshape(4, 2, 4, rows, features)
     weight = pltpu.with_memory_space_constraint(weight, pltpu.HBM)
 
-    steps, turns = transform_tables()
-    filter_spectrum = run_kernel(filter_kernel, SPECTRUM, [GRID, TURNED], 1, long_filter, steps, turns)
+    steps = transform_tables()
+    filter_spectrum = run_kernel(filter_kernel, SPECTRUM, [GRID, TURNED], 1, long_filter, steps)
 
     tokens = (rows, chunk)
     channels = (chunk, rows)
@@ -352,7 +363,7 @@
     product_owned = lax.all_to_all(product.reshape(BLOCKS, CHANNELS, LANES), SEQ, 0, 0, tiled=True)
     long_owned, product_spectrum = run_kernel(
         forward_kernel, [pltpu.HBM(SEQUENCES.shape, BF16), pltpu.HBM(SPECTRUM.shape, BF16)], [GRID, TURNED, SECTION], 2,
-        product_owned, filter_spectrum, steps, turns,
+        product_owned, filter_spectrum, steps,
     )
     turned = cotangent.T
     gradient = jnp.stack(
@@ -386,11 +397,13 @@
     )
     grad_owned = lax.all_to_all(long_grad.reshape(BLOCKS, CHANNELS, LANES), SEQ, 0, 0, tiled=True)
 
-    back_owned, filter_grad = run_kernel(
-        backward_kernel,
-        [pltpu.HBM(SEQUENCES.shape, BF16), pltpu.HBM((CHANNELS, LENGTH), F32)],
-        [GRID, TURNED, SECTION], 3,
-        grad_owned, filter_spectrum, product_spectrum, steps, turns,
+    back_owned = run_kernel(
+        backward_kernel, pltpu.HBM(SEQUENCES.shape, BF16), [GRID, TURNED, SECTION], 2,
+        grad_owned, filter_spectrum, steps,
+    )
+    filter_grad = run_kernel(
+        filter_grad_kernel, jax.ShapeDtypeStruct((CHANNELS, LENGTH), F32), [GRID, TURNED, SECTION], 2,
+        grad_owned, product_spectrum, steps, back_owned, unread=(3,),
     )
 
     quarter = (1, 2, 4, rows, features)
@@ -413,7 +426,7 @@
     following = shift(jnp.stack([key_conv[:2], value_conv[:2]]), -1)
 
     back_raw = lax.all_to_all(back_owned, SEQ, 0, 0, tiled=True).reshape(width, rows)
-    head, query_grad = lax.optimization_barrier((back_raw[:, :2].T, query_grad))
+    head, query_grad, filter_grad = lax.optimization_barrier((back_raw[:, :2].T, query_grad, filter_grad))
     after = shift(head, -1)
     grads = run_blocks(
         key_value_adjoint, kinds,

time: 216 us -> 214 us (level)
  waiting for transfers between devices: 80.1 us -> 77 us
    all_to_all x1, waiting for transfers between devices: 9.42 us -> 5.72 us  [per_device(): lax.all_to_all(back_owned, SEQ, 0, 0, tiled=True).reshape(width, rows)]
    pallas_call x3 -> x4, Pallas kernels: 4.87 us -> 6.07 us  [run_kernel(): pl.pallas_call(kernel, out_shape=out_shape, in_specs=in_specs, scratch_sh...]
    unnamed x37 -> x35, local copies, waits for them, and re-layouts: 7.76 us -> 7.91 us
  transfers between devices with their start and end apart: 16 -> 16, of which waited for: 10 -> 10; matrix products, arithmetic and copies ran while one was open for 1% -> 1% of each run, Pallas kernels for 10% -> 11%
where the time goes in v5:
time: 214 us; the launch traced here: 213 us
  waiting for transfers between devices  77 us (36%)
  starting transfers between devices  69 us (32%)
  Pallas kernels  27.8 us (13%)
  between operations  14.4 us (7%)
  blocking collectives  13.6 us (6%)
  local copies, waits for them, and re-layouts  9.76 us (5%)
    all_to_all x1, waiting for transfers between devices, per_device(): lax.all_to_all(product.reshape(BLOCKS, CHANNELS, LANES), SEQ, 0, 0, tiled...  23.8 us
    pallas_call x9, Pallas kernels, run_blocks(): pl.pallas_call(kernel, grid=(steps,), in_specs=[spec(block, axis) for _,...  21.7 us
    all_to_all x1, starting transfers between devices, per_device(): lax.all_to_all(product.reshape(BLOCKS, CHANNELS, LANES), SEQ, 0, 0, tiled...  19.4 us
    all_to_all x1, waiting for transfers between devices, per_device(): lax.all_to_all(long_grad.reshape(BLOCKS, CHANNELS, LANES), SEQ, 0, 0, til...  18.4 us
    all_to_all x1, blocking collectives, per_device(): lax.all_to_all(partial.reshape(8, chunk, rows), PLANE, 0, 0, tiled=True)  13.6 us
    ppermute x4, waiting for transfers between devices, shift(): lax.ppermute(value, SEQ, [(i, i + steps) for i in range(first, last)])  11.1 us
    all_to_all x1, starting transfers between devices, per_device(): lax.all_to_all(long_grad.reshape(BLOCKS, CHANNELS, LANES), SEQ, 0, 0, til...  9.61 us
    ppermute x3, starting transfers between devices, across(): lax.ppermute(value, ('xh', 'xl'), [(i, i ^ 2 * dx + dl) for i in range(4)])  9.01 us
  transfers between devices with their start and end apart: 16, of which 10 were waited for; matrix products, arithmetic and copies ran while one was open for 1% of the time, Pallas kernels for 11%

profile of v5, /device:TPU:1, one launch (start us, length us, event | category | flops | bytes accessed | tf_op | source)
XLA Modules:
  0.0 213.0 jit_solution(1819712006216284063)
XLA Ops:
  7.2 0.8 slice_bitcast_fusion.5
  8.0 0.7 slice_bitcast_fusion.3
  8.8 6.0 %collective-permute-start.1 = (bf16[128,512]{1,0:T(8,128)(2,1)}, bf16[128,512]{1,0:T(8,128)(2,1)S(1)}, u32[]{:S(2)}, u32[]{:S(2)}) collective-permute-start(bf16[128,512]{1,0:T(8,128)(2,1)} %param.13), channel_id=1, source_target_pairs={{0,0},{1,16},{4,8},{5,24},{8,256},{9,272},{12,264},{13,280},{16,1}... | collective-permute-start | bytes 393224 | tf_op jit(solution)/shard_map/ppermute | solution.py:328
  14.8 1.9 collective-permute-start
  16.7 2.4 %collective-permute-done.before_ref = bf16[3,2,1024]{2,1,0:T(2,128)(2,1)S(1)} collective-permute-done((bf16[3,2,1024]{2,1,0:T(2,128)(2,1)S(1)}, bf16[3,2,1024]{2,1,0:T(2,128)(2,1)S(1)}, u32[]{:S(2)}, u32[]{:S(2)}) %collective-permute-start) | collective-permute-done | bytes 12320 | tf_op jit(solution)/shard_map/ppermute | solution.py:310
  19.1 0.7 copy-done.14
  19.8 2.2 %shard_map.119._ = bf16[1024,128]{1,0:T(8,128)(2,1)} custom-call(bf16[128,1024]{1,0:T(8,128)(2,1)} %k_ref.3, bf16[128,1024]{1,0:T(8,128)(2,1)} %v_ref.3, bf16[3,2,1024]{2,1,0:T(2,128)(2,1)} %copy-done.15, f32[3,3,1024]{2,1,0:T(4,128)} %taps_ref.9), custom_call_target="tpu_custom_call" | custom-call | flops 1000000 | bytes 1048576 | tf_op jit(solution)/shard_map/pallas_call | solution.py:167
  22.1 19.4 %all-to-all-start = ((bf16[64,16,128]{2,1,0:T(8,128)(2,1)}), bf16[64,16,128]{2,1,0:T(8,128)(2,1)S(1)}, u32[]{:S(2)}, u32[]{:S(2)}) async-start(bf16[64,16,128]{2,1,0:T(8,128)(2,1)} %bitcast.46), calls=%async_computation | async-start | bytes 524288 | tf_op jit(solution)/shard_map/all_to_all | solution.py:363
  41.5 1.0 copy-done
  42.5 1.0 copy-done.10
  44.1 23.8 %all-to-all-done.product_ref = bf16[64,16,128]{2,1,0:T(8,128)(2,1)S(1)} async-done(((bf16[64,16,128]{2,1,0:T(8,128)(2,1)}), bf16[64,16,128]{2,1,0:T(8,128)(2,1)S(1)}, u32[]{:S(2)}, u32[]{:S(2)}) %all-to-all-start) | async-done | bytes 262176 | tf_op jit(solution)/shard_map/all_to_all | solution.py:363
  67.9 1.0 copy-done.1
  68.9 1.8 shard_map.121
  70.7 4.2 %all-to-all-start.1 = ((bf16[64,16,128]{2,1,0:T(8,128)(2,1)}), bf16[64,16,128]{2,1,0:T(8,128)(2,1)S(1)}, u32[]{:S(2)}, u32[]{:S(2)}) async-start(bf16[64,16,128]{2,1,0:T(8,128)(2,1)} %get-tuple-element.27), calls=%async_computation.1 | async-start | bytes 524288 | tf_op jit(solution)/shard_map/all_to_all | solution.py:374
  75.0 4.9 %collective-permute-start.2 = (bf16[512,128]{1,0:T(8,128)(2,1)S(1)}, bf16[512,128]{1,0:T(8,128)(2,1)S(1)}, u32[]{:S(2)}, u32[]{:S(2)}) collective-permute-start(bf16[512,128]{1,0:T(8,128)(2,1)S(1)} %bitcast.48), channel_id=1, source_target_pairs={{0,256},{4,260},{256,0},{260,4},{1,257},{5,261},{257,1},{261,5},{2... | collective-permute-start | bytes 393224 | tf_op jit(solution)/shard_map/ppermute | solution.py:320
  80.0 1.9 collective-permute-start.3
  81.9 2.2 %collective-permute-start.4 = (bf16[512,128]{1,0:T(8,128)(2,1)S(1)}, bf16[512,128]{1,0:T(8,128)(2,1)S(1)}, u32[]{:S(2)}, u32[]{:S(2)}) collective-permute-start(bf16[512,128]{1,0:T(8,128)(2,1)S(1)} %bitcast.50), channel_id=1, source_target_pairs={{0,260},{4,256},{256,4},{260,0},{1,261},{5,257},{257,5},{261,1},{2... | collective-permute-start | bytes 393224 | tf_op jit(solution)/shard_map/ppermute | solution.py:320
  84.1 3.1 %collective-permute-done.3 = bf16[512,128]{1,0:T(8,128)(2,1)S(1)} collective-permute-done((bf16[512,128]{1,0:T(8,128)(2,1)S(1)}, bf16[512,128]{1,0:T(8,128)(2,1)S(1)}, u32[]{:S(2)}, u32[]{:S(2)}) %collective-permute-start.3) | collective-permute-done | bytes 131104 | tf_op jit(solution)/shard_map/ppermute | solution.py:320
  87.2 2.8 %collective-permute-done.4 = bf16[512,128]{1,0:T(8,128)(2,1)S(1)} collective-permute-done((bf16[512,128]{1,0:T(8,128)(2,1)S(1)}, bf16[512,128]{1,0:T(8,128)(2,1)S(1)}, u32[]{:S(2)}, u32[]{:S(2)}) %collective-permute-start.4) | collective-permute-done | bytes 131104 | tf_op jit(solution)/shard_map/ppermute | solution.py:320
  90.1 3.7 %collective-permute-start.5 = (bf16[2,512,256]{2,1,0:T(8,128)(2,1)S(1)}, bf16[2,512,256]{2,1,0:T(8,128)(2,1)S(1)}, u32[]{:S(2)}, u32[]{:S(2)}) collective-permute-start(bf16[2,512,256]{2,1,0:T(8,128)(2,1)S(1)} %get-tuple-element.44), channel_id=1, source_target_pairs={{0,1},{1,0},{2,3},{3,2},{4,5},{5,4},{6,7},{7,6},{8,9},{9,8},{10,11... | collective-permute-start | bytes 1572872 | tf_op jit(solution)/shard_map/ppermute | solution.py:314
  93.8 3.7 %shard_map.122 = (f32[128,1024]{1,0:T(8,128)}, f32[128,1024]{1,0:T(8,128)}, f32[128,1024]{1,0:T(8,128)}, f32[1024,128]{1,0:T(8,128)}) custom-call(bf16[128,1024]{1,0:T(8,128)(2,1)} %q_ref.1, bf16[128,1024]{1,0:T(8,128)(2,1)} %k_ref.3, bf16[128,1024]{1,0:T(8,128)(2,1)} %v_ref.3, bf16[3,2,1024]{2,1,0:T(2,128)(2,1)} %copy-done.15, f32[3,3,1024]{2,1,0:T(4,128)} %taps_ref.9, ...), custom_call_target="tpu_custom_call" | custom-call | flops 1000000 | bytes 3145728 | tf_op jit(solution)/shard_map/pallas_call | solution.py:167
  97.5 3.4 %all-to-all-done.1 = bf16[64,16,128]{2,1,0:T(8,128)(2,1)S(1)} async-done(((bf16[64,16,128]{2,1,0:T(8,128)(2,1)}), bf16[64,16,128]{2,1,0:T(8,128)(2,1)S(1)}, u32[]{:S(2)}, u32[]{:S(2)}) %all-to-all-start.1) | async-done | bytes 262176 | tf_op jit(solution)/shard_map/all_to_all | solution.py:374
  100.9 1.0 copy-done.9
  101.9 1.0 shard_map.123
  103.0 4.9 %all-to-all-start.2 = ((bf16[8,128,256]{2,1,0:T(8,128)(2,1)}), bf16[8,128,256]{2,1,0:T(8,128)(2,1)S(1)}, u32[]{:S(2)}, u32[]{:S(2)}) async-start(bf16[8,128,256]{2,1,0:T(8,128)(2,1)} %bitcast.47), calls=%async_computation.2 | async-start | bytes 1048576 | tf_op jit(solution)/shard_map/all_to_all | solution.py:383
  107.9 0.8 copy-done.12
  108.7 1.1 pad_maximum_fusion.gradient_ref
  109.8 8.7 %all-to-all-done.2._ = bf16[8,128,256]{2,1,0:T(8,128)(2,1)S(1)} async-done(((bf16[8,128,256]{2,1,0:T(8,128)(2,1)}), bf16[8,128,256]{2,1,0:T(8,128)(2,1)S(1)}, u32[]{:S(2)}, u32[]{:S(2)}) %all-to-all-start.2) | async-done | bytes 524320 | tf_op jit(solution)/shard_map/all_to_all | solution.py:383
  118.5 4.3 %shard_map.125 = bf16[2,4,256,128]{3,2,1,0:T(8,128)(2,1)S(1)} custom-call(s32[4]{0:T(128)S(1)} %pad_add_fusion.place_ref, bf16[2,2,512,256]{3,2,1,0:T(8,128)(2,1)S(1)} %pad_maximum_fusion.gradient_ref, bf16[4,2,4,128,512]{4,3,2,1,0:T(8,128)(2,1)} %bitcast.44, bf16[8,128,256]{2,1,0:T(8,128)(2,1)S(1)} %all-to-all-done.2._), custom_call_target="tpu_custom_call" | custom-call | flops 1073741824 | bytes 6291456 | tf_op jit(solution)/shard_map/pallas_call | solution.py:167
  122.8 13.6 %all_to_all.30.parts_ref = bf16[8,256,128]{2,1,0:T(8,128)(2,1)S(1)} all-to-all(bf16[8,256,128]{2,1,0:T(8,128)(2,1)S(1)} %bitcast.42), channel_id=1, replica_groups=mesh['xh'=2,'zy'=4,'zh'=2,'zb'=2,'co'=2,'xl'=2,'yh'=2,'yl'=2] {'xh','yh'..., dimensions={0} | all-to-all | bytes 1048576 | tf_op jit(solution)/shard_map/all_to_all | solution.py:392
  136.4 1.0 shard_map.126
  137.4 9.6 %all-to-all-start.4 = ((bf16[64,16,128]{2,1,0:T(8,128)(2,1)}), bf16[64,16,128]{2,1,0:T(8,128)(2,1)S(1)}, u32[]{:S(2)}, u32[]{:S(2)}) async-start(bf16[64,16,128]{2,1,0:T(8,128)(2,1)} %bitcast.53), calls=%async_computation.5 | async-start | bytes 524288 | tf_op jit(solution)/shard_map/all_to_all | solution.py:398
  147.1 5.2 %shard_map.124 = bf16[2,2,2,128,512]{4,3,2,1,0:T(8,128)(2,1)} custom-call(bf16[2,4,128,256]{3,2,1,0:T(8,128)(2,1)S(1)} %bitcast.36, bf16[4,2,4,128,512]{4,3,2,1,0:T(8,128)(2,1)} %bitcast.45), custom_call_target="tpu_custom_call" | custom-call | flops 1073741824 | bytes 6291456 | tf_op jit(solution)/shard_map/pallas_call | solution.py:167
  152.4 18.4 %all-to-all-done.4.grad_ref = bf16[64,16,128]{2,1,0:T(8,128)(2,1)S(1)} async-done(((bf16[64,16,128]{2,1,0:T(8,128)(2,1)}), bf16[64,16,128]{2,1,0:T(8,128)(2,1)S(1)}, u32[]{:S(2)}, u32[]{:S(2)}) %all-to-all-start.4) | async-done | bytes 262176 | tf_op jit(solution)/shard_map/all_to_all | solution.py:398
  170.8 1.8 shard_map.127._
  172.6 4.2 %all-to-all-start.5 = ((bf16[64,16,128]{2,1,0:T(8,128)(2,1)}), bf16[64,16,128]{2,1,0:T(8,128)(2,1)S(1)}, u32[]{:S(2)}, u32[]{:S(2)}) async-start(bf16[64,16,128]{2,1,0:T(8,128)(2,1)} %shard_map.127._), calls=%async_computation.6 | async-start | bytes 524288 | tf_op jit(solution)/shard_map/all_to_all | solution.py:428
  177.1 2.2 %collective-permute-start.6 = (f32[2,1024]{1,0:T(2,128)S(1)}, f32[2,1024]{1,0:T(2,128)S(1)}, u32[]{:S(2)}, u32[]{:S(2)}) collective-permute-start(f32[2,1024]{1,0:T(2,128)S(1)} %slice_bitcast_fusion), channel_id=1, source_target_pairs={{8,0},{16,8},{24,16},{32,24},{40,32},{48,40},{56,48},{64,56},{72,6... | collective-permute-start | bytes 24584 | tf_op jit(solution)/shard_map/ppermute | solution.py:310
  179.3 1.9 collective-permute-start.8
  181.2 7.9 %collective-permute-done.6.after_ref = f32[2,1024]{1,0:T(2,128)S(1)} collective-permute-done((f32[2,1024]{1,0:T(2,128)S(1)}, f32[2,1024]{1,0:T(2,128)S(1)}, u32[]{:S(2)}, u32[]{:S(2)}) %collective-permute-start.6) | collective-permute-done | bytes 8224 | tf_op jit(solution)/shard_map/ppermute | solution.py:310
  189.1 1.6 shard_map.128
  190.7 0.9 copy-done.3
  191.7 1.0 copy-done.11
  192.7 1.9 shard_map.129
  194.7 5.7 %all-to-all-done.5 = bf16[64,16,128]{2,1,0:T(8,128)(2,1)S(1)} async-done(((bf16[64,16,128]{2,1,0:T(8,128)(2,1)}), bf16[64,16,128]{2,1,0:T(8,128)(2,1)S(1)}, u32[]{:S(2)}, u32[]{:S(2)}) %all-to-all-start.5) | async-done | bytes 262176 | tf_op jit(solution)/shard_map/all_to_all | solution.py:428
  200.5 1.9 collective-permute-start.7
  202.7 1.9 shard_map.130
  204.6 0.8 collective-permute-done.7.after_ref
  205.4 0.7 shard_map.131
  (49 shorter events, 1.7 us)
Async XLA Ops:
  7.2 67.8 %copy-start.13 = (bf16[128,512]{1,0:T(8,128)(2,1)S(1)}, bf16[128,512]{1,0:T(8,128)(2,1)}, u32[]{:S(2)}) copy-start(bf16[128,512]{1,0:T(8,128)(2,1)} %param.14) | copy-start | bytes 393220
  7.2 111.3 %all-gather.3.cloned.1.call-start = ((), (), s32[]{:S(2)}) async-start(), calls=%async_computation.8 | async-start | bytes 4325376 | tf_op jit(solution)/shard_map/all_gather | solution.py:341
  8.8 10.4 %collective-permute-start.1 = (bf16[128,512]{1,0:T(8,128)(2,1)}, bf16[128,512]{1,0:T(8,128)(2,1)S(1)}, u32[]{:S(2)}, u32[]{:S(2)}) collective-permute-start(bf16[128,512]{1,0:T(8,128)(2,1)} %param.13), channel_id=1, source_target_pairs={{0,0},{1,16},{4,8},{5,24},{8,256},{9,272},{12,264},{13,280},{16,1}... | collective-permute-start | bytes 393224 | tf_op jit(solution)/shard_map/ppermute | solution.py:328
  14.8 4.3 %collective-permute-start = (bf16[3,2,1024]{2,1,0:T(2,128)(2,1)S(1)}, bf16[3,2,1024]{2,1,0:T(2,128)(2,1)S(1)}, u32[]{:S(2)}, u32[]{:S(2)}) collective-permute-start(bf16[3,2,1024]{2,1,0:T(2,128)(2,1)S(1)} %pad_maximum_fusion.3), channel_id=1, source_target_pairs={{0,8},{8,16},{16,24},{24,32},{32,40},{40,48},{48,56},{56,64},{64,7... | collective-permute-start | bytes 36872 | tf_op jit(solution)/shard_map/ppermute | solution.py:310
  19.1 0.7 copy-start.15
  19.1 0.7 copy-start.14
  22.1 45.8 %all-to-all-start = ((bf16[64,16,128]{2,1,0:T(8,128)(2,1)}), bf16[64,16,128]{2,1,0:T(8,128)(2,1)S(1)}, u32[]{:S(2)}, u32[]{:S(2)}) async-start(bf16[64,16,128]{2,1,0:T(8,128)(2,1)} %bitcast.46), calls=%async_computation | async-start | bytes 524288 | tf_op jit(solution)/shard_map/all_to_all | solution.py:363
  41.5 1.0 copy-start
  42.5 1.0 copy-start.10
  67.9 1.0 copy-start.1
  70.7 30.2 %all-to-all-start.1 = ((bf16[64,16,128]{2,1,0:T(8,128)(2,1)}), bf16[64,16,128]{2,1,0:T(8,128)(2,1)S(1)}, u32[]{:S(2)}, u32[]{:S(2)}) async-start(bf16[64,16,128]{2,1,0:T(8,128)(2,1)} %get-tuple-element.27), calls=%async_computation.1 | async-start | bytes 524288 | tf_op jit(solution)/shard_map/all_to_all | solution.py:374
  75.0 9.0 %collective-permute-start.2 = (bf16[512,128]{1,0:T(8,128)(2,1)S(1)}, bf16[512,128]{1,0:T(8,128)(2,1)S(1)}, u32[]{:S(2)}, u32[]{:S(2)}) collective-permute-start(bf16[512,128]{1,0:T(8,128)(2,1)S(1)} %bitcast.48), channel_id=1, source_target_pairs={{0,256},{4,260},{256,0},{260,4},{1,257},{5,261},{257,1},{261,5},{2... | collective-permute-start | bytes 393224 | tf_op jit(solution)/shard_map/ppermute | solution.py:320
  80.0 7.2 %collective-permute-start.3 = (bf16[512,128]{1,0:T(8,128)(2,1)S(1)}, bf16[512,128]{1,0:T(8,128)(2,1)S(1)}, u32[]{:S(2)}, u32[]{:S(2)}) collective-permute-start(bf16[512,128]{1,0:T(8,128)(2,1)S(1)} %bitcast.49), channel_id=1, source_target_pairs={{0,4},{4,0},{256,260},{260,256},{1,5},{5,1},{257,261},{261,257},{2... | collective-permute-start | bytes 393224 | tf_op jit(solution)/shard_map/ppermute | solution.py:320
  81.9 8.1 %collective-permute-start.4 = (bf16[512,128]{1,0:T(8,128)(2,1)S(1)}, bf16[512,128]{1,0:T(8,128)(2,1)S(1)}, u32[]{:S(2)}, u32[]{:S(2)}) collective-permute-start(bf16[512,128]{1,0:T(8,128)(2,1)S(1)} %bitcast.50), channel_id=1, source_target_pairs={{0,260},{4,256},{256,4},{260,0},{1,261},{5,257},{257,5},{261,1},{2... | collective-permute-start | bytes 393224 | tf_op jit(solution)/shard_map/ppermute | solution.py:320
  90.1 17.8 %collective-permute-start.5 = (bf16[2,512,256]{2,1,0:T(8,128)(2,1)S(1)}, bf16[2,512,256]{2,1,0:T(8,128)(2,1)S(1)}, u32[]{:S(2)}, u32[]{:S(2)}) collective-permute-start(bf16[2,512,256]{2,1,0:T(8,128)(2,1)S(1)} %get-tuple-element.44), channel_id=1, source_target_pairs={{0,1},{1,0},{2,3},{3,2},{4,5},{5,4},{6,7},{7,6},{8,9},{9,8},{10,11... | collective-permute-start | bytes 1572872 | tf_op jit(solution)/shard_map/ppermute | solution.py:314
  100.9 1.0 copy-start.9
  103.0 15.5 %all-to-all-start.2 = ((bf16[8,128,256]{2,1,0:T(8,128)(2,1)}), bf16[8,128,256]{2,1,0:T(8,128)(2,1)S(1)}, u32[]{:S(2)}, u32[]{:S(2)}) async-start(bf16[8,128,256]{2,1,0:T(8,128)(2,1)} %bitcast.47), calls=%async_computation.2 | async-start | bytes 1048576 | tf_op jit(solution)/shard_map/all_to_all | solution.py:383
  107.9 0.8 copy-start.12
  109.8 26.6 %copy-start.8 = (f32[1024,128]{1,0:T(8,128)S(1)}, f32[1024,128]{1,0:T(8,128)}, u32[]{:S(2)}) copy-start(f32[1024,128]{1,0:T(8,128)} %get-tuple-element.30.qc_ref) | copy-start | bytes 1572868
  136.4 34.4 %copy-start.2 = (bf16[320,640]{1,0:T(8,128)(2,1)S(1)}, bf16[320,640]{1,0:T(8,128)(2,1)}, u32[]{:S(2)}) copy-start(bf16[320,640]{1,0:T(8,128)(2,1)} %constant.16.clone.steps) | copy-start | bytes 1228804
  137.4 33.4 %all-to-all-start.4 = ((bf16[64,16,128]{2,1,0:T(8,128)(2,1)}), bf16[64,16,128]{2,1,0:T(8,128)(2,1)S(1)}, u32[]{:S(2)}, u32[]{:S(2)}) async-start(bf16[64,16,128]{2,1,0:T(8,128)(2,1)} %bitcast.53), calls=%async_computation.5 | async-start | bytes 524288 | tf_op jit(solution)/shard_map/all_to_all | solution.py:398
  147.0 59.1 %reduce-scatter.2.cloned.1.call-start = ((), (), s32[]{:S(2)}) async-start(), calls=%async_computation.7 | async-start | bytes 1179648 | tf_op jit(solution)/shard_map/reduce_scatter | solution.py:416
  147.1 29.7 %copy-start.5 = (f32[128,1024]{1,0:T(8,128)S(1)}, f32[128,1024]{1,0:T(8,128)}, u32[]{:S(2)}) copy-start(f32[128,1024]{1,0:T(8,128)} %get-tuple-element.36.vc_ref) | copy-start | bytes 1572868
  147.1 29.7 %copy-start.4 = (f32[128,1024]{1,0:T(8,128)S(1)}, f32[128,1024]{1,0:T(8,128)}, u32[]{:S(2)}) copy-start(f32[128,1024]{1,0:T(8,128)} %get-tuple-element.35.kc_ref) | copy-start | bytes 1572868
  147.1 29.7 %copy-start.6 = (f32[1024,128]{1,0:T(8,128)S(1)}, f32[1024,128]{1,0:T(8,128)}, u32[]{:S(2)}) copy-start(f32[1024,128]{1,0:T(8,128)} %get-tuple-element.32.qg_ref) | copy-start | bytes 1572868
  147.1 42.0 %copy-start.7 = (f32[3,3,1024]{2,1,0:T(4,128)S(1)}, f32[3,3,1024]{2,1,0:T(4,128)}, u32[]{:S(2)}) copy-start(f32[3,3,1024]{2,1,0:T(4,128)} %taps_ref.9) | copy-start | bytes 110596
  172.6 27.8 %all-to-all-start.5 = ((bf16[64,16,128]{2,1,0:T(8,128)(2,1)}), bf16[64,16,128]{2,1,0:T(8,128)(2,1)S(1)}, u32[]{:S(2)}, u32[]{:S(2)}) async-start(bf16[64,16,128]{2,1,0:T(8,128)(2,1)} %shard_map.127._), calls=%async_computation.6 | async-start | bytes 524288 | tf_op jit(solution)/shard_map/all_to_all | solution.py:428
  177.1 12.1 %collective-permute-start.6 = (f32[2,1024]{1,0:T(2,128)S(1)}, f32[2,1024]{1,0:T(2,128)S(1)}, u32[]{:S(2)}, u32[]{:S(2)}) collective-permute-start(f32[2,1024]{1,0:T(2,128)S(1)} %slice_bitcast_fusion), channel_id=1, source_target_pairs={{8,0},{16,8},{24,16},{32,24},{40,32},{48,40},{56,48},{64,56},{72,6... | collective-permute-start | bytes 24584 | tf_op jit(solution)/shard_map/ppermute | solution.py:310
  179.3 25.3 %collective-permute-start.8 = (f32[2,2,1024]{2,1,0:T(2,128)S(1)}, f32[2,2,1024]{2,1,0:T(2,128)S(1)}, u32[]{:S(2)}, u32[]{:S(2)}) collective-permute-start(f32[2,2,1024]{2,1,0:T(2,128)S(1)} %pad_maximum_fusion.2), channel_id=1, source_target_pairs={{8,0},{16,8},{24,16},{32,24},{40,32},{48,40},{56,48},{64,56},{72,6... | collective-permute-start | bytes 49160 | tf_op jit(solution)/shard_map/ppermute | solution.py:310
  190.7 1.0 copy-start.3
  191.7 1.0 copy-start.11
  200.5 4.9 %collective-permute-start.7 = (bf16[2,1024]{1,0:T(2,128)(2,1)S(1)}, bf16[2,1024]{1,0:T(2,128)(2,1)S(1)}, u32[]{:S(2)}, u32[]{:S(2)}) collective-permute-start(bf16[2,1024]{1,0:T(2,128)(2,1)S(1)} %bitcast.54), channel_id=1, source_target_pairs={{8,0},{16,8},{24,16},{32,24},{40,32},{48,40},{56,48},{64,56},{72,6... | collective-permute-start | bytes 12296 | tf_op jit(solution)/shard_map/ppermute | solution.py:310
Sparse Core Ops, SparseCore 0:
  19.9 95.1 all-gather.2
  152.5 42.2 reduce-scatter.1

commit v6 on v5

--- a/solution.py
+++ b/solution.py
@@ -22,6 +22,7 @@
 BLOCKS = 64
 LANES = 128
 LENGTH = BLOCKS * LANES
+ROWS = BLOCKS * CHANNELS
 
 RIM = 16
 VMEM_LIMIT = 20 * 2**20
@@ -94,7 +95,7 @@
 def forward_kernel(
     product_ref, filter_spectrum, steps, long_ref, product_spectrum, grid, turned, section
 ):
-    grid[...] = product_ref[...].astype(F32).reshape(BLOCKS * CHANNELS, LANES)
+    grid[:ROWS] = product_ref[...].astype(F32).reshape(ROWS, LANES)
     own = to_spectrum(grid, turned, steps)
     product_spectrum[...] = own.astype(BF16)
     own_re, own_im = own[:, :LANES], own[:, LANES:]
@@ -103,11 +104,11 @@
     turned[:, :LANES] = (own_re * other_re - own_im * other_im).astype(BF16)
     turned[:, LANES:] = (own_re * other_im + own_im * other_re).astype(BF16)
     from_spectrum(turned[...], grid, section, steps)
-    long_ref[...] = grid[...].reshape(BLOCKS, CHANNELS, LANES).astype(BF16)
+    long_ref[...] = grid[:ROWS].reshape(BLOCKS, CHANNELS, LANES).astype(BF16)
 
 
 def correlate(grad_ref, other, grid, turned, section, steps):
-    grid[...] = grad_ref[...].astype(F32).reshape(BLOCKS * CHANNELS, LANES)
+    grid[:ROWS] = grad_ref[...].astype(F32).reshape(ROWS, LANES)
     own = to_spectrum(grid, turned, steps)
     own_re, own_im = own[:, :LANES], own[:, LANES:]
     other_re, other_im = other[:, :LANES].astype(F32), other[:, LANES:].astype(F32)
@@ -118,7 +119,7 @@
 
 def backward_kernel(grad_ref, filter_spectrum, steps, back_ref, grid, turned, section):
     correlate(grad_ref, filter_spectrum, grid, turned, section, steps)
-    back_ref[...] = grid[...].reshape(BLOCKS, CHANNELS, LANES).astype(BF16)
+    back_ref[...] = grid[:ROWS].reshape(BLOCKS, CHANNELS, LANES).astype(BF16)
 
 
 def filter_grad_kernel(
@@ -133,7 +134,7 @@
 
 SPECTRUM = jax.ShapeDtypeStruct((CHANNELS * BLOCKS, 2 * LANES), BF16)
 SEQUENCES = jax.ShapeDtypeStruct((BLOCKS, CHANNELS, LANES), BF16)
-GRID = pltpu.VMEM((BLOCKS * CHANNELS, LANES), F32)
+GRID = pltpu.VMEM((ROWS + CHANNELS, LANES), F32)
 TURNED = pltpu.VMEM((CHANNELS * BLOCKS, 2 * LANES), BF16)
 SECTION = pltpu.VMEM((CHANNELS * BLOCKS, 2 * LANES), F32)
 

time: 214 us -> 214 us (level)
  no operation moved by 1% of the time
where the time goes in v6:
time: 214 us; the launch traced here: 213 us
  waiting for transfers between devices  77 us (36%)
  starting transfers between devices  69 us (32%)
  Pallas kernels  27.8 us (13%)
  between operations  14.4 us (7%)
  blocking collectives  13.7 us (6%)
  local copies, waits for them, and re-layouts  9.76 us (5%)
    all_to_all x1, waiting for transfers between devices, per_device(): lax.all_to_all(product.reshape(BLOCKS, CHANNELS, LANES), SEQ, 0, 0, tiled...  23.8 us
    pallas_call x9, Pallas kernels, run_blocks(): pl.pallas_call(kernel, grid=(steps,), in_specs=[spec(block, axis) for _,...  21.7 us
    all_to_all x1, starting transfers between devices, per_device(): lax.all_to_all(product.reshape(BLOCKS, CHANNELS, LANES), SEQ, 0, 0, tiled...  19.4 us
    all_to_all x1, waiting for transfers between devices, per_device(): lax.all_to_all(long_grad.reshape(BLOCKS, CHANNELS, LANES), SEQ, 0, 0, til...  18.4 us
    all_to_all x1, blocking collectives, per_device(): lax.all_to_all(partial.reshape(8, chunk, rows), PLANE, 0, 0, tiled=True)  13.7 us
    ppermute x4, waiting for transfers between devices, shift(): lax.ppermute(value, SEQ, [(i, i + steps) for i in range(first, last)])  11.1 us
    all_to_all x1, starting transfers between devices, per_device(): lax.all_to_all(long_grad.reshape(BLOCKS, CHANNELS, LANES), SEQ, 0, 0, til...  9.56 us
    ppermute x3, starting transfers between devices, across(): lax.ppermute(value, ('xh', 'xl'), [(i, i ^ 2 * dx + dl) for i in range(4)])  9.01 us
  transfers between devices with their start and end apart: 16, of which 10 were waited for; matrix products, arithmetic and copies ran while one was open for 1% of the time, Pallas kernels for 11%

profile of v6, /device:TPU:1, one launch (start us, length us, event | category | flops | bytes accessed | tf_op | source)
XLA Modules:
  0.0 213.0 jit_solution(11986599984916099493)
XLA Ops:
  7.2 0.8 slice_bitcast_fusion.5
  8.0 0.7 slice_bitcast_fusion.3
  8.8 6.0 %collective-permute-start.1 = (bf16[128,512]{1,0:T(8,128)(2,1)}, bf16[128,512]{1,0:T(8,128)(2,1)S(1)}, u32[]{:S(2)}, u32[]{:S(2)}) collective-permute-start(bf16[128,512]{1,0:T(8,128)(2,1)} %param.13), channel_id=1, source_target_pairs={{0,0},{1,16},{4,8},{5,24},{8,256},{9,272},{12,264},{13,280},{16,1}... | collective-permute-start | bytes 393224 | tf_op jit(solution)/shard_map/ppermute | solution.py:329
  14.8 1.9 collective-permute-start
  16.7 2.4 %collective-permute-done.before_ref = bf16[3,2,1024]{2,1,0:T(2,128)(2,1)S(1)} collective-permute-done((bf16[3,2,1024]{2,1,0:T(2,128)(2,1)S(1)}, bf16[3,2,1024]{2,1,0:T(2,128)(2,1)S(1)}, u32[]{:S(2)}, u32[]{:S(2)}) %collective-permute-start) | collective-permute-done | bytes 12320 | tf_op jit(solution)/shard_map/ppermute | solution.py:311
  19.1 0.7 copy-done.14
  19.8 2.2 %shard_map.119._ = bf16[1024,128]{1,0:T(8,128)(2,1)} custom-call(bf16[128,1024]{1,0:T(8,128)(2,1)} %k_ref.3, bf16[128,1024]{1,0:T(8,128)(2,1)} %v_ref.3, bf16[3,2,1024]{2,1,0:T(2,128)(2,1)} %copy-done.15, f32[3,3,1024]{2,1,0:T(4,128)} %taps_ref.9), custom_call_target="tpu_custom_call" | custom-call | flops 1000000 | bytes 1048576 | tf_op jit(solution)/shard_map/pallas_call | solution.py:168
  22.1 19.4 %all-to-all-start = ((bf16[64,16,128]{2,1,0:T(8,128)(2,1)}), bf16[64,16,128]{2,1,0:T(8,128)(2,1)S(1)}, u32[]{:S(2)}, u32[]{:S(2)}) async-start(bf16[64,16,128]{2,1,0:T(8,128)(2,1)} %bitcast.46), calls=%async_computation | async-start | bytes 524288 | tf_op jit(solution)/shard_map/all_to_all | solution.py:364
  41.5 1.0 copy-done
  42.5 1.0 copy-done.10
  44.1 23.8 %all-to-all-done.product_ref = bf16[64,16,128]{2,1,0:T(8,128)(2,1)S(1)} async-done(((bf16[64,16,128]{2,1,0:T(8,128)(2,1)}), bf16[64,16,128]{2,1,0:T(8,128)(2,1)S(1)}, u32[]{:S(2)}, u32[]{:S(2)}) %all-to-all-start) | async-done | bytes 262176 | tf_op jit(solution)/shard_map/all_to_all | solution.py:364
  67.9 1.0 copy-done.1
  68.9 1.8 shard_map.121
  70.7 4.2 %all-to-all-start.1 = ((bf16[64,16,128]{2,1,0:T(8,128)(2,1)}), bf16[64,16,128]{2,1,0:T(8,128)(2,1)S(1)}, u32[]{:S(2)}, u32[]{:S(2)}) async-start(bf16[64,16,128]{2,1,0:T(8,128)(2,1)} %get-tuple-element.27), calls=%async_computation.1 | async-start | bytes 524288 | tf_op jit(solution)/shard_map/all_to_all | solution.py:375
  75.1 4.9 %collective-permute-start.2 = (bf16[512,128]{1,0:T(8,128)(2,1)S(1)}, bf16[512,128]{1,0:T(8,128)(2,1)S(1)}, u32[]{:S(2)}, u32[]{:S(2)}) collective-permute-start(bf16[512,128]{1,0:T(8,128)(2,1)S(1)} %bitcast.48), channel_id=1, source_target_pairs={{0,256},{4,260},{256,0},{260,4},{1,257},{5,261},{257,1},{261,5},{2... | collective-permute-start | bytes 393224 | tf_op jit(solution)/shard_map/ppermute | solution.py:321
  80.0 1.9 collective-permute-start.3
  81.9 2.2 %collective-permute-start.4 = (bf16[512,128]{1,0:T(8,128)(2,1)S(1)}, bf16[512,128]{1,0:T(8,128)(2,1)S(1)}, u32[]{:S(2)}, u32[]{:S(2)}) collective-permute-start(bf16[512,128]{1,0:T(8,128)(2,1)S(1)} %bitcast.50), channel_id=1, source_target_pairs={{0,260},{4,256},{256,4},{260,0},{1,261},{5,257},{257,5},{261,1},{2... | collective-permute-start | bytes 393224 | tf_op jit(solution)/shard_map/ppermute | solution.py:321
  84.1 3.0 %collective-permute-done.3 = bf16[512,128]{1,0:T(8,128)(2,1)S(1)} collective-permute-done((bf16[512,128]{1,0:T(8,128)(2,1)S(1)}, bf16[512,128]{1,0:T(8,128)(2,1)S(1)}, u32[]{:S(2)}, u32[]{:S(2)}) %collective-permute-start.3) | collective-permute-done | bytes 131104 | tf_op jit(solution)/shard_map/ppermute | solution.py:321
  87.1 2.9 %collective-permute-done.4 = bf16[512,128]{1,0:T(8,128)(2,1)S(1)} collective-permute-done((bf16[512,128]{1,0:T(8,128)(2,1)S(1)}, bf16[512,128]{1,0:T(8,128)(2,1)S(1)}, u32[]{:S(2)}, u32[]{:S(2)}) %collective-permute-start.4) | collective-permute-done | bytes 131104 | tf_op jit(solution)/shard_map/ppermute | solution.py:321
  90.1 3.6 %collective-permute-start.5 = (bf16[2,512,256]{2,1,0:T(8,128)(2,1)S(1)}, bf16[2,512,256]{2,1,0:T(8,128)(2,1)S(1)}, u32[]{:S(2)}, u32[]{:S(2)}) collective-permute-start(bf16[2,512,256]{2,1,0:T(8,128)(2,1)S(1)} %get-tuple-element.44), channel_id=1, source_target_pairs={{0,1},{1,0},{2,3},{3,2},{4,5},{5,4},{6,7},{7,6},{8,9},{9,8},{10,11... | collective-permute-start | bytes 1572872 | tf_op jit(solution)/shard_map/ppermute | solution.py:315
  93.8 3.7 %shard_map.122 = (f32[128,1024]{1,0:T(8,128)}, f32[128,1024]{1,0:T(8,128)}, f32[128,1024]{1,0:T(8,128)}, f32[1024,128]{1,0:T(8,128)}) custom-call(bf16[128,1024]{1,0:T(8,128)(2,1)} %q_ref.1, bf16[128,1024]{1,0:T(8,128)(2,1)} %k_ref.3, bf16[128,1024]{1,0:T(8,128)(2,1)} %v_ref.3, bf16[3,2,1024]{2,1,0:T(2,128)(2,1)} %copy-done.15, f32[3,3,1024]{2,1,0:T(4,128)} %taps_ref.9, ...), custom_call_target="tpu_custom_call" | custom-call | flops 1000000 | bytes 3145728 | tf_op jit(solution)/shard_map/pallas_call | solution.py:168
  97.5 3.4 %all-to-all-done.1 = bf16[64,16,128]{2,1,0:T(8,128)(2,1)S(1)} async-done(((bf16[64,16,128]{2,1,0:T(8,128)(2,1)}), bf16[64,16,128]{2,1,0:T(8,128)(2,1)S(1)}, u32[]{:S(2)}, u32[]{:S(2)}) %all-to-all-start.1) | async-done | bytes 262176 | tf_op jit(solution)/shard_map/all_to_all | solution.py:375
  100.9 1.0 copy-done.9
  101.9 1.0 shard_map.123
  103.0 4.9 %all-to-all-start.2 = ((bf16[8,128,256]{2,1,0:T(8,128)(2,1)}), bf16[8,128,256]{2,1,0:T(8,128)(2,1)S(1)}, u32[]{:S(2)}, u32[]{:S(2)}) async-start(bf16[8,128,256]{2,1,0:T(8,128)(2,1)} %bitcast.47), calls=%async_computation.2 | async-start | bytes 1048576 | tf_op jit(solution)/shard_map/all_to_all | solution.py:384
  107.9 0.8 copy-done.12
  108.7 1.1 pad_maximum_fusion.gradient_ref
  109.9 8.7 %all-to-all-done.2._ = bf16[8,128,256]{2,1,0:T(8,128)(2,1)S(1)} async-done(((bf16[8,128,256]{2,1,0:T(8,128)(2,1)}), bf16[8,128,256]{2,1,0:T(8,128)(2,1)S(1)}, u32[]{:S(2)}, u32[]{:S(2)}) %all-to-all-start.2) | async-done | bytes 524320 | tf_op jit(solution)/shard_map/all_to_all | solution.py:384
  118.5 4.3 %shard_map.125 = bf16[2,4,256,128]{3,2,1,0:T(8,128)(2,1)S(1)} custom-call(s32[4]{0:T(128)S(1)} %pad_add_fusion.place_ref, bf16[2,2,512,256]{3,2,1,0:T(8,128)(2,1)S(1)} %pad_maximum_fusion.gradient_ref, bf16[4,2,4,128,512]{4,3,2,1,0:T(8,128)(2,1)} %bitcast.44, bf16[8,128,256]{2,1,0:T(8,128)(2,1)S(1)} %all-to-all-done.2._), custom_call_target="tpu_custom_call" | custom-call | flops 1073741824 | bytes 6291456 | tf_op jit(solution)/shard_map/pallas_call | solution.py:168
  122.8 13.7 %all_to_all.30.parts_ref = bf16[8,256,128]{2,1,0:T(8,128)(2,1)S(1)} all-to-all(bf16[8,256,128]{2,1,0:T(8,128)(2,1)S(1)} %bitcast.42), channel_id=1, replica_groups=mesh['xh'=2,'zy'=4,'zh'=2,'zb'=2,'co'=2,'xl'=2,'yh'=2,'yl'=2] {'xh','yh'..., dimensions={0} | all-to-all | bytes 1048576 | tf_op jit(solution)/shard_map/all_to_all | solution.py:393
  136.5 1.0 shard_map.126
  137.4 9.6 %all-to-all-start.4 = ((bf16[64,16,128]{2,1,0:T(8,128)(2,1)}), bf16[64,16,128]{2,1,0:T(8,128)(2,1)S(1)}, u32[]{:S(2)}, u32[]{:S(2)}) async-start(bf16[64,16,128]{2,1,0:T(8,128)(2,1)} %bitcast.53), calls=%async_computation.5 | async-start | bytes 524288 | tf_op jit(solution)/shard_map/all_to_all | solution.py:399
  147.1 5.2 %shard_map.124 = bf16[2,2,2,128,512]{4,3,2,1,0:T(8,128)(2,1)} custom-call(bf16[2,4,128,256]{3,2,1,0:T(8,128)(2,1)S(1)} %bitcast.36, bf16[4,2,4,128,512]{4,3,2,1,0:T(8,128)(2,1)} %bitcast.45), custom_call_target="tpu_custom_call" | custom-call | flops 1073741824 | bytes 6291456 | tf_op jit(solution)/shard_map/pallas_call | solution.py:168
  152.4 18.4 %all-to-all-done.4.grad_ref = bf16[64,16,128]{2,1,0:T(8,128)(2,1)S(1)} async-done(((bf16[64,16,128]{2,1,0:T(8,128)(2,1)}), bf16[64,16,128]{2,1,0:T(8,128)(2,1)S(1)}, u32[]{:S(2)}, u32[]{:S(2)}) %all-to-all-start.4) | async-done | bytes 262176 | tf_op jit(solution)/shard_map/all_to_all | solution.py:399
  170.8 1.8 shard_map.127._
  172.6 4.2 %all-to-all-start.5 = ((bf16[64,16,128]{2,1,0:T(8,128)(2,1)}), bf16[64,16,128]{2,1,0:T(8,128)(2,1)S(1)}, u32[]{:S(2)}, u32[]{:S(2)}) async-start(bf16[64,16,128]{2,1,0:T(8,128)(2,1)} %shard_map.127._), calls=%async_computation.6 | async-start | bytes 524288 | tf_op jit(solution)/shard_map/all_to_all | solution.py:429
  177.1 2.2 %collective-permute-start.6 = (f32[2,1024]{1,0:T(2,128)S(1)}, f32[2,1024]{1,0:T(2,128)S(1)}, u32[]{:S(2)}, u32[]{:S(2)}) collective-permute-start(f32[2,1024]{1,0:T(2,128)S(1)} %slice_bitcast_fusion), channel_id=1, source_target_pairs={{8,0},{16,8},{24,16},{32,24},{40,32},{48,40},{56,48},{64,56},{72,6... | collective-permute-start | bytes 24584 | tf_op jit(solution)/shard_map/ppermute | solution.py:311
  179.3 1.9 collective-permute-start.8
  181.2 7.9 %collective-permute-done.6.after_ref = f32[2,1024]{1,0:T(2,128)S(1)} collective-permute-done((f32[2,1024]{1,0:T(2,128)S(1)}, f32[2,1024]{1,0:T(2,128)S(1)}, u32[]{:S(2)}, u32[]{:S(2)}) %collective-permute-start.6) | collective-permute-done | bytes 8224 | tf_op jit(solution)/shard_map/ppermute | solution.py:311
  189.1 1.6 shard_map.128
  190.8 0.9 copy-done.3
  191.7 1.0 copy-done.11
  192.8 1.9 shard_map.129
  194.7 5.7 %all-to-all-done.5 = bf16[64,16,128]{2,1,0:T(8,128)(2,1)S(1)} async-done(((bf16[64,16,128]{2,1,0:T(8,128)(2,1)}), bf16[64,16,128]{2,1,0:T(8,128)(2,1)S(1)}, u32[]{:S(2)}, u32[]{:S(2)}) %all-to-all-start.5) | async-done | bytes 262176 | tf_op jit(solution)/shard_map/all_to_all | solution.py:429
  200.5 1.9 collective-permute-start.7
  202.7 1.9 shard_map.130
  204.6 0.8 collective-permute-done.7.after_ref
  205.4 0.7 shard_map.131
  (49 shorter events, 1.7 us)
Async XLA Ops:
  7.2 67.8 %copy-start.13 = (bf16[128,512]{1,0:T(8,128)(2,1)S(1)}, bf16[128,512]{1,0:T(8,128)(2,1)}, u32[]{:S(2)}) copy-start(bf16[128,512]{1,0:T(8,128)(2,1)} %param.14) | copy-start | bytes 393220
  7.2 111.4 %all-gather.3.cloned.1.call-start = ((), (), s32[]{:S(2)}) async-start(), calls=%async_computation.8 | async-start | bytes 4325376 | tf_op jit(solution)/shard_map/all_gather | solution.py:342
  8.8 10.4 %collective-permute-start.1 = (bf16[128,512]{1,0:T(8,128)(2,1)}, bf16[128,512]{1,0:T(8,128)(2,1)S(1)}, u32[]{:S(2)}, u32[]{:S(2)}) collective-permute-start(bf16[128,512]{1,0:T(8,128)(2,1)} %param.13), channel_id=1, source_target_pairs={{0,0},{1,16},{4,8},{5,24},{8,256},{9,272},{12,264},{13,280},{16,1}... | collective-permute-start | bytes 393224 | tf_op jit(solution)/shard_map/ppermute | solution.py:329
  14.8 4.3 %collective-permute-start = (bf16[3,2,1024]{2,1,0:T(2,128)(2,1)S(1)}, bf16[3,2,1024]{2,1,0:T(2,128)(2,1)S(1)}, u32[]{:S(2)}, u32[]{:S(2)}) collective-permute-start(bf16[3,2,1024]{2,1,0:T(2,128)(2,1)S(1)} %pad_maximum_fusion.3), channel_id=1, source_target_pairs={{0,8},{8,16},{16,24},{24,32},{32,40},{40,48},{48,56},{56,64},{64,7... | collective-permute-start | bytes 36872 | tf_op jit(solution)/shard_map/ppermute | solution.py:311
  19.1 0.7 copy-start.15
  19.1 0.7 copy-start.14
  22.1 45.8 %all-to-all-start = ((bf16[64,16,128]{2,1,0:T(8,128)(2,1)}), bf16[64,16,128]{2,1,0:T(8,128)(2,1)S(1)}, u32[]{:S(2)}, u32[]{:S(2)}) async-start(bf16[64,16,128]{2,1,0:T(8,128)(2,1)} %bitcast.46), calls=%async_computation | async-start | bytes 524288 | tf_op jit(solution)/shard_map/all_to_all | solution.py:364
  41.5 1.0 copy-start
  42.5 1.0 copy-start.10
  67.9 1.0 copy-start.1
  70.7 30.2 %all-to-all-start.1 = ((bf16[64,16,128]{2,1,0:T(8,128)(2,1)}), bf16[64,16,128]{2,1,0:T(8,128)(2,1)S(1)}, u32[]{:S(2)}, u32[]{:S(2)}) async-start(bf16[64,16,128]{2,1,0:T(8,128)(2,1)} %get-tuple-element.27), calls=%async_computation.1 | async-start | bytes 524288 | tf_op jit(solution)/shard_map/all_to_all | solution.py:375
  75.1 9.0 %collective-permute-start.2 = (bf16[512,128]{1,0:T(8,128)(2,1)S(1)}, bf16[512,128]{1,0:T(8,128)(2,1)S(1)}, u32[]{:S(2)}, u32[]{:S(2)}) collective-permute-start(bf16[512,128]{1,0:T(8,128)(2,1)S(1)} %bitcast.48), channel_id=1, source_target_pairs={{0,256},{4,260},{256,0},{260,4},{1,257},{5,261},{257,1},{261,5},{2... | collective-permute-start | bytes 393224 | tf_op jit(solution)/shard_map/ppermute | solution.py:321
  80.0 7.2 %collective-permute-start.3 = (bf16[512,128]{1,0:T(8,128)(2,1)S(1)}, bf16[512,128]{1,0:T(8,128)(2,1)S(1)}, u32[]{:S(2)}, u32[]{:S(2)}) collective-permute-start(bf16[512,128]{1,0:T(8,128)(2,1)S(1)} %bitcast.49), channel_id=1, source_target_pairs={{0,4},{4,0},{256,260},{260,256},{1,5},{5,1},{257,261},{261,257},{2... | collective-permute-start | bytes 393224 | tf_op jit(solution)/shard_map/ppermute | solution.py:321
  81.9 8.1 %collective-permute-start.4 = (bf16[512,128]{1,0:T(8,128)(2,1)S(1)}, bf16[512,128]{1,0:T(8,128)(2,1)S(1)}, u32[]{:S(2)}, u32[]{:S(2)}) collective-permute-start(bf16[512,128]{1,0:T(8,128)(2,1)S(1)} %bitcast.50), channel_id=1, source_target_pairs={{0,260},{4,256},{256,4},{260,0},{1,261},{5,257},{257,5},{261,1},{2... | collective-permute-start | bytes 393224 | tf_op jit(solution)/shard_map/ppermute | solution.py:321
  90.1 17.8 %collective-permute-start.5 = (bf16[2,512,256]{2,1,0:T(8,128)(2,1)S(1)}, bf16[2,512,256]{2,1,0:T(8,128)(2,1)S(1)}, u32[]{:S(2)}, u32[]{:S(2)}) collective-permute-start(bf16[2,512,256]{2,1,0:T(8,128)(2,1)S(1)} %get-tuple-element.44), channel_id=1, source_target_pairs={{0,1},{1,0},{2,3},{3,2},{4,5},{5,4},{6,7},{7,6},{8,9},{9,8},{10,11... | collective-permute-start | bytes 1572872 | tf_op jit(solution)/shard_map/ppermute | solution.py:315
  100.9 1.0 copy-start.9
  103.0 15.6 %all-to-all-start.2 = ((bf16[8,128,256]{2,1,0:T(8,128)(2,1)}), bf16[8,128,256]{2,1,0:T(8,128)(2,1)S(1)}, u32[]{:S(2)}, u32[]{:S(2)}) async-start(bf16[8,128,256]{2,1,0:T(8,128)(2,1)} %bitcast.47), calls=%async_computation.2 | async-start | bytes 1048576 | tf_op jit(solution)/shard_map/all_to_all | solution.py:384
  107.9 0.8 copy-start.12
  109.8 26.6 %copy-start.8 = (f32[1024,128]{1,0:T(8,128)S(1)}, f32[1024,128]{1,0:T(8,128)}, u32[]{:S(2)}) copy-start(f32[1024,128]{1,0:T(8,128)} %get-tuple-element.30.qc_ref) | copy-start | bytes 1572868
  136.5 34.3 %copy-start.2 = (bf16[320,640]{1,0:T(8,128)(2,1)S(1)}, bf16[320,640]{1,0:T(8,128)(2,1)}, u32[]{:S(2)}) copy-start(bf16[320,640]{1,0:T(8,128)(2,1)} %constant.16.clone.steps) | copy-start | bytes 1228804
  137.4 33.3 %all-to-all-start.4 = ((bf16[64,16,128]{2,1,0:T(8,128)(2,1)}), bf16[64,16,128]{2,1,0:T(8,128)(2,1)S(1)}, u32[]{:S(2)}, u32[]{:S(2)}) async-start(bf16[64,16,128]{2,1,0:T(8,128)(2,1)} %bitcast.53), calls=%async_computation.5 | async-start | bytes 524288 | tf_op jit(solution)/shard_map/all_to_all | solution.py:399
  147.0 59.1 %reduce-scatter.2.cloned.1.call-start = ((), (), s32[]{:S(2)}) async-start(), calls=%async_computation.7 | async-start | bytes 1179648 | tf_op jit(solution)/shard_map/reduce_scatter | solution.py:417
  147.1 29.7 %copy-start.5 = (f32[128,1024]{1,0:T(8,128)S(1)}, f32[128,1024]{1,0:T(8,128)}, u32[]{:S(2)}) copy-start(f32[128,1024]{1,0:T(8,128)} %get-tuple-element.36.vc_ref) | copy-start | bytes 1572868
  147.1 29.7 %copy-start.4 = (f32[128,1024]{1,0:T(8,128)S(1)}, f32[128,1024]{1,0:T(8,128)}, u32[]{:S(2)}) copy-start(f32[128,1024]{1,0:T(8,128)} %get-tuple-element.35.kc_ref) | copy-start | bytes 1572868
  147.1 29.7 %copy-start.6 = (f32[1024,128]{1,0:T(8,128)S(1)}, f32[1024,128]{1,0:T(8,128)}, u32[]{:S(2)}) copy-start(f32[1024,128]{1,0:T(8,128)} %get-tuple-element.32.qg_ref) | copy-start | bytes 1572868
  147.1 42.0 %copy-start.7 = (f32[3,3,1024]{2,1,0:T(4,128)S(1)}, f32[3,3,1024]{2,1,0:T(4,128)}, u32[]{:S(2)}) copy-start(f32[3,3,1024]{2,1,0:T(4,128)} %taps_ref.9) | copy-start | bytes 110596
  172.6 27.8 %all-to-all-start.5 = ((bf16[64,16,128]{2,1,0:T(8,128)(2,1)}), bf16[64,16,128]{2,1,0:T(8,128)(2,1)S(1)}, u32[]{:S(2)}, u32[]{:S(2)}) async-start(bf16[64,16,128]{2,1,0:T(8,128)(2,1)} %shard_map.127._), calls=%async_computation.6 | async-start | bytes 524288 | tf_op jit(solution)/shard_map/all_to_all | solution.py:429
  177.1 12.1 %collective-permute-start.6 = (f32[2,1024]{1,0:T(2,128)S(1)}, f32[2,1024]{1,0:T(2,128)S(1)}, u32[]{:S(2)}, u32[]{:S(2)}) collective-permute-start(f32[2,1024]{1,0:T(2,128)S(1)} %slice_bitcast_fusion), channel_id=1, source_target_pairs={{8,0},{16,8},{24,16},{32,24},{40,32},{48,40},{56,48},{64,56},{72,6... | collective-permute-start | bytes 24584 | tf_op jit(solution)/shard_map/ppermute | solution.py:311
  179.3 25.3 %collective-permute-start.8 = (f32[2,2,1024]{2,1,0:T(2,128)S(1)}, f32[2,2,1024]{2,1,0:T(2,128)S(1)}, u32[]{:S(2)}, u32[]{:S(2)}) collective-permute-start(f32[2,2,1024]{2,1,0:T(2,128)S(1)} %pad_maximum_fusion.2), channel_id=1, source_target_pairs={{8,0},{16,8},{24,16},{32,24},{40,32},{48,40},{56,48},{64,56},{72,6... | collective-permute-start | bytes 49160 | tf_op jit(solution)/shard_map/ppermute | solution.py:311
  190.8 0.9 copy-start.3
  191.7 1.0 copy-start.11
  200.5 4.9 %collective-permute-start.7 = (bf16[2,1024]{1,0:T(2,128)(2,1)S(1)}, bf16[2,1024]{1,0:T(2,128)(2,1)S(1)}, u32[]{:S(2)}, u32[]{:S(2)}) collective-permute-start(bf16[2,1024]{1,0:T(2,128)(2,1)S(1)} %bitcast.54), channel_id=1, source_target_pairs={{8,0},{16,8},{24,16},{32,24},{40,32},{48,40},{56,48},{64,56},{72,6... | collective-permute-start | bytes 12296 | tf_op jit(solution)/shard_map/ppermute | solution.py:311
Sparse Core Ops, SparseCore 0:
  19.9 95.1 all-gather.2
  152.5 42.1 reduce-scatter.1

commit v7 on v6

--- a/solution.py
+++ b/solution.py
@@ -86,7 +86,8 @@
         )
 
 
-def filter_kernel(filter_ref, steps, spectrum_ref, grid, turned):
+def filter_kernel(filter_ref, steps, spectrum_ref, kept_ref, grid, turned):
+    kept_ref[...] = steps[...]
     for b in range(BLOCKS):
         grid[b * CHANNELS : (b + 1) * CHANNELS, :] = filter_ref[:, b * LANES : (b + 1) * LANES]
     spectrum_ref[...] = to_spectrum(grid, turned, steps).astype(BF16)
@@ -107,18 +108,24 @@
     long_ref[...] = grid[:ROWS].reshape(BLOCKS, CHANNELS, LANES).astype(BF16)
 
 
-def correlate(grad_ref, other, grid, turned, section, steps):
+def correlate(grad_ref, other, grid, turned, section, steps, fetch=None):
     grid[:ROWS] = grad_ref[...].astype(F32).reshape(ROWS, LANES)
     own = to_spectrum(grid, turned, steps)
     own_re, own_im = own[:, :LANES], own[:, LANES:]
+    if fetch is not None:
+        fetch.wait()
     other_re, other_im = other[:, :LANES].astype(F32), other[:, LANES:].astype(F32)
     turned[:, :LANES] = (own_re * other_re + own_im * other_im).astype(BF16)
     turned[:, LANES:] = (own_im * other_re - own_re * other_im).astype(BF16)
     from_spectrum(turned[...], grid, section, steps)
 
 
-def backward_kernel(grad_ref, filter_spectrum, steps, back_ref, grid, turned, section):
-    correlate(grad_ref, filter_spectrum, grid, turned, section, steps)
+def backward_kernel(
+    grad_ref, spectrum_ref, steps, back_ref, grid, turned, section, filter_spectrum, fetched
+):
+    fetch = pltpu.make_async_copy(spectrum_ref, filter_spectrum, fetched)
+    fetch.start()
+    correlate(grad_ref, filter_spectrum, grid, turned, section, steps, fetch)
     back_ref[...] = grid[:ROWS].reshape(BLOCKS, CHANNELS, LANES).astype(BF16)
 
 
@@ -224,30 +231,21 @@
             gated_ref[co, y] = gated[:, start : start + LANES]
 
 
-def partial_kernel(place_ref, gradient_ref, weight_ref, _, out_ref, total):
+def partial_kernel(place_ref, gradient_ref, weight_ref, _, out_ref):
     xh, xl, yl = place_ref[0], place_ref[1], place_ref[3]
-    step = pl.program_id(0)
-    features, tokens = gradient_ref.shape[2:]
+    kinds, features, tokens = weight_ref.shape[2], *gradient_ref.shape[2:]
     rows = tokens // 2
-    added = jnp.dot(
-        weight_ref[...].reshape(total.shape[0], features),
-        gradient_ref[(step // 2) ^ yl, (step % 2) ^ xl],
-        preferred_element_type=F32,
-    )
-
-    @pl.when(step == 0)
-    def _():
-        total[...] = added
-
-    @pl.when(step > 0)
-    def _():
-        total[...] += added
-
-    @pl.when(step == pl.num_programs(0) - 1)
-    def _():
+    for zy in range(weight_ref.shape[0]):
+        total = jnp.zeros((out_ref.shape[2], tokens), F32)
+        for k in range(kinds):
+            total += jnp.dot(
+                weight_ref[zy, :, k].reshape(-1, features),
+                gradient_ref[(k // 2) ^ yl, (k % 2) ^ xl],
+                preferred_element_type=F32,
+            )
+        total = total.astype(BF16)
         for t in range(2):
-            value = total[:, t * rows : (t + 1) * rows].astype(BF16)
-            out_ref[t ^ xh] = value.reshape(out_ref.shape[1:])
+            out_ref[t ^ xh, zy] = total[:, t * rows : (t + 1) * rows]
 
 
 def long_gradient(parts_ref, qc_ref, long_ref, grad_ref, qg_ref):
@@ -340,10 +338,12 @@
     rims, out_weight = lax.optimization_barrier((rims, out_weight))
     before, turned = lax.optimization_barrier((shift(rims, 1), turn(out_weight)))
     weight = lax.all_gather(turned, COLUMN, axis=0).reshape(4, 2, 4, rows, features)
-    weight = pltpu.with_memory_space_constraint(weight, pltpu.HBM)
 
     steps = transform_tables()
-    filter_spectrum = run_kernel(filter_kernel, SPECTRUM, [GRID, TURNED], 1, long_filter, steps)
+    kept = jax.ShapeDtypeStruct(steps.shape, BF16)
+    filter_spectrum, kept = run_kernel(
+        filter_kernel, [SPECTRUM, kept], [GRID, TURNED], 1, long_filter, steps
+    )
 
     tokens = (rows, chunk)
     channels = (chunk, rows)
@@ -358,13 +358,13 @@
         filter_inputs, kinds,
         [(queries, tokens, 1), (keys, tokens, 1), (values, tokens, 1),
          (before, (3, 2, chunk), 2), (short_taps, taps_block, 2), (product, None, None)],
-        [plane, plane, plane, ((width, rows), F32, channels, 0)], 3 * 2**20, limit=WHOLE_VMEM,
+        [plane, plane, plane, ((width, rows), F32, channels, 0)], 3 * 2**20,
     )
 
     product_owned = lax.all_to_all(product.reshape(BLOCKS, CHANNELS, LANES), SEQ, 0, 0, tiled=True)
     long_owned, product_spectrum = run_kernel(
         forward_kernel, [pltpu.HBM(SEQUENCES.shape, BF16), pltpu.HBM(SPECTRUM.shape, BF16)], [GRID, TURNED, SECTION], 2,
-        product_owned, filter_spectrum, steps,
+        product_owned, filter_spectrum, kept,
     )
     turned = cotangent.T
     gradient = jnp.stack(
@@ -383,13 +383,14 @@
 
     mixing = lax.all_to_all(gated.reshape(8, rows, chunk), PLANE, 0, 0, tiled=True)
 
-    (partial,) = run_blocks(
-        partial_kernel, kinds,
-        [place, (gradient, gradient.shape, None),
-         (weight, (4, 2, 1, rows, features), 2), (mixing, None, None)],
-        [((2, 4, chunk, rows), BF16, (2, 4, chunk, rows), None)], 6 * 2**20, 2**30,
-        [pltpu.VMEM((width, 2 * rows), F32)],
-    )
+    memory = (pltpu.SMEM, pltpu.VMEM, pltpu.VMEM, pl.ANY)
+    partial = pl.pallas_call(
+        partial_kernel,
+        in_specs=[pl.BlockSpec(memory_space=space) for space in memory],
+        out_shape=jax.ShapeDtypeStruct((2, 4, chunk, rows), BF16),
+        compiler_params=pltpu.CompilerParams(vmem_limit_bytes=VMEM_LIMIT),
+        cost_estimate=pl.CostEstimate(flops=2**30, bytes_accessed=6 * 2**20, transcendentals=0),
+    )(place[0], gradient, weight, mixing)
     arrived = lax.all_to_all(partial.reshape(8, chunk, rows), PLANE, 0, 0, tiled=True)
     long_grad, query_conv_grad = run_blocks(
         long_gradient, 2,
@@ -399,8 +400,9 @@
     grad_owned = lax.all_to_all(long_grad.reshape(BLOCKS, CHANNELS, LANES), SEQ, 0, 0, tiled=True)
 
     back_owned = run_kernel(
-        backward_kernel, pltpu.HBM(SEQUENCES.shape, BF16), [GRID, TURNED, SECTION], 2,
-        grad_owned, filter_spectrum, steps,
+        backward_kernel, pltpu.HBM(SEQUENCES.shape, BF16),
+        [GRID, TURNED, SECTION, TURNED, pltpu.SemaphoreType.DMA], 2,
+        grad_owned, pltpu.with_memory_space_constraint(filter_spectrum, pltpu.HBM), steps, unread=(1,),
     )
     filter_grad = run_kernel(
         filter_grad_kernel, jax.ShapeDtypeStruct((CHANNELS, LENGTH), F32), [GRID, TURNED, SECTION], 2,

time: 214 us -> 214 us (level)
  Pallas kernels: 27.8 us -> 21.5 us
  local copies, waits for them, and re-layouts: 9.76 us -> 11.9 us
    pallas_call x9 -> x8, Pallas kernels: 21.7 us -> 12.8 us  [run_blocks(): pl.pallas_call(kernel, grid=(steps,), in_specs=[spec(block, axis) for _,...]
    unnamed x35 -> x39, local copies, waits for them, and re-layouts: 7.91 us -> 8.43 us
  transfers between devices with their start and end apart: 16 -> 16, of which waited for: 10 -> 10; matrix products, arithmetic and copies ran while one was open for 1% -> 2% of each run, Pallas kernels for 11% -> 9%
where the time goes in v7:
time: 214 us; the launch traced here: 213 us
  waiting for transfers between devices  78.6 us (37%)
  starting transfers between devices  68.6 us (32%)
  Pallas kernels  21.5 us (10%)
  blocking collectives  15.3 us (7%)
  between operations  14.4 us (7%)
  local copies, waits for them, and re-layouts  11.9 us (6%)
  other arithmetic  2.53 us (1%)
    all_to_all x1, waiting for transfers between devices, per_device(): lax.all_to_all(product.reshape(BLOCKS, CHANNELS, LANES), SEQ, 0, 0, tiled...  23.7 us
    all_to_all x1, starting transfers between devices, per_device(): lax.all_to_all(product.reshape(BLOCKS, CHANNELS, LANES), SEQ, 0, 0, tiled...  19.5 us
    all_to_all x1, waiting for transfers between devices, per_device(): lax.all_to_all(long_grad.reshape(BLOCKS, CHANNELS, LANES), SEQ, 0, 0, til...  18.4 us
    all_to_all x1, blocking collectives, per_device(): lax.all_to_all(partial.reshape(8, chunk, rows), PLANE, 0, 0, tiled=True)  15.3 us
    pallas_call x8, Pallas kernels, run_blocks(): pl.pallas_call(kernel, grid=(steps,), in_specs=[spec(block, axis) for _,...  12.8 us
    all_to_all x1, starting transfers between devices, per_device(): lax.all_to_all(long_grad.reshape(BLOCKS, CHANNELS, LANES), SEQ, 0, 0, til...  9.7 us
    ppermute x4, waiting for transfers between devices, shift(): lax.ppermute(value, SEQ, [(i, i + steps) for i in range(first, last)])  9.6 us
    all_to_all x1, waiting for transfers between devices, per_device(): lax.all_to_all(gated.reshape(8, rows, chunk), PLANE, 0, 0, tiled=True)  9.3 us
  transfers between devices with their start and end apart: 16, of which 10 were waited for; matrix products, arithmetic and copies ran while one was open for 2% of the time, Pallas kernels for 9%

profile of v7, /device:TPU:1, one launch (start us, length us, event | category | flops | bytes accessed | tf_op | source)
XLA Modules:
  0.0 212.9 jit_solution(3751898935646038160)
XLA Ops:
  7.3 0.8 slice_bitcast_fusion.5
  8.1 0.7 slice_bitcast_fusion.3
  8.8 6.0 %collective-permute-start.1 = (bf16[128,512]{1,0:T(8,128)(2,1)}, bf16[128,512]{1,0:T(8,128)(2,1)S(1)}, u32[]{:S(2)}, u32[]{:S(2)}) collective-permute-start(bf16[128,512]{1,0:T(8,128)(2,1)} %param.13), channel_id=1, source_target_pairs={{0,0},{1,16},{4,8},{5,24},{8,256},{9,272},{12,264},{13,280},{16,1}... | collective-permute-start | bytes 393224 | tf_op jit(solution)/shard_map/ppermute | solution.py:327
  14.9 1.9 collective-permute-start
  16.8 2.4 %collective-permute-done.before_ref = bf16[3,2,1024]{2,1,0:T(2,128)(2,1)S(1)} collective-permute-done((bf16[3,2,1024]{2,1,0:T(2,128)(2,1)S(1)}, bf16[3,2,1024]{2,1,0:T(2,128)(2,1)S(1)}, u32[]{:S(2)}, u32[]{:S(2)}) %collective-permute-start) | collective-permute-done | bytes 12320 | tf_op jit(solution)/shard_map/ppermute | solution.py:309
  19.9 2.2 %shard_map.119._ = bf16[1024,128]{1,0:T(8,128)(2,1)} custom-call(bf16[128,1024]{1,0:T(8,128)(2,1)} %k_ref.3, bf16[128,1024]{1,0:T(8,128)(2,1)} %v_ref.3, bf16[3,2,1024]{2,1,0:T(2,128)(2,1)} %copy-done.14, f32[3,3,1024]{2,1,0:T(4,128)} %taps_ref.9), custom_call_target="tpu_custom_call" | custom-call | flops 1000000 | bytes 1048576 | tf_op jit(solution)/shard_map/pallas_call | solution.py:175
  22.2 19.5 %all-to-all-start = ((bf16[64,16,128]{2,1,0:T(8,128)(2,1)}), bf16[64,16,128]{2,1,0:T(8,128)(2,1)S(1)}, u32[]{:S(2)}, u32[]{:S(2)}) async-start(bf16[64,16,128]{2,1,0:T(8,128)(2,1)} %bitcast.44), calls=%async_computation | async-start | bytes 524288 | tf_op jit(solution)/shard_map/all_to_all | solution.py:364
  41.7 1.0 copy-done.2
  42.7 1.0 copy-done.10
  44.4 23.7 %all-to-all-done.product_ref = bf16[64,16,128]{2,1,0:T(8,128)(2,1)S(1)} async-done(((bf16[64,16,128]{2,1,0:T(8,128)(2,1)}), bf16[64,16,128]{2,1,0:T(8,128)(2,1)S(1)}, u32[]{:S(2)}, u32[]{:S(2)}) %all-to-all-start) | async-done | bytes 262176 | tf_op jit(solution)/shard_map/all_to_all | solution.py:364
  68.1 1.8 shard_map.121
  69.9 4.3 %all-to-all-start.1 = ((bf16[64,16,128]{2,1,0:T(8,128)(2,1)}), bf16[64,16,128]{2,1,0:T(8,128)(2,1)S(1)}, u32[]{:S(2)}, u32[]{:S(2)}) async-start(bf16[64,16,128]{2,1,0:T(8,128)(2,1)} %get-tuple-element.31), calls=%async_computation.1 | async-start | bytes 524288 | tf_op jit(solution)/shard_map/all_to_all | solution.py:375
  74.3 4.9 %collective-permute-start.2 = (bf16[512,128]{1,0:T(8,128)(2,1)S(1)}, bf16[512,128]{1,0:T(8,128)(2,1)S(1)}, u32[]{:S(2)}, u32[]{:S(2)}) collective-permute-start(bf16[512,128]{1,0:T(8,128)(2,1)S(1)} %bitcast.48), channel_id=1, source_target_pairs={{0,256},{4,260},{256,0},{260,4},{1,257},{5,261},{257,1},{261,5},{2... | collective-permute-start | bytes 393224 | tf_op jit(solution)/shard_map/ppermute | solution.py:319
  79.2 1.9 collective-permute-start.3
  81.1 2.2 %collective-permute-start.4 = (bf16[512,128]{1,0:T(8,128)(2,1)S(1)}, bf16[512,128]{1,0:T(8,128)(2,1)S(1)}, u32[]{:S(2)}, u32[]{:S(2)}) collective-permute-start(bf16[512,128]{1,0:T(8,128)(2,1)S(1)} %bitcast.50), channel_id=1, source_target_pairs={{0,260},{4,256},{256,4},{260,0},{1,261},{5,257},{257,5},{261,1},{2... | collective-permute-start | bytes 393224 | tf_op jit(solution)/shard_map/ppermute | solution.py:319
  83.4 3.1 %collective-permute-done.3 = bf16[512,128]{1,0:T(8,128)(2,1)S(1)} collective-permute-done((bf16[512,128]{1,0:T(8,128)(2,1)S(1)}, bf16[512,128]{1,0:T(8,128)(2,1)S(1)}, u32[]{:S(2)}, u32[]{:S(2)}) %collective-permute-start.3) | collective-permute-done | bytes 131104 | tf_op jit(solution)/shard_map/ppermute | solution.py:319
  86.5 2.6 %collective-permute-done.4 = bf16[512,128]{1,0:T(8,128)(2,1)S(1)} collective-permute-done((bf16[512,128]{1,0:T(8,128)(2,1)S(1)}, bf16[512,128]{1,0:T(8,128)(2,1)S(1)}, u32[]{:S(2)}, u32[]{:S(2)}) %collective-permute-start.4) | collective-permute-done | bytes 131104 | tf_op jit(solution)/shard_map/ppermute | solution.py:319
  89.1 1.1 fusion
  90.2 3.6 %collective-permute-start.5 = (bf16[2,512,256]{2,1,0:T(8,128)(2,1)}, bf16[2,512,256]{2,1,0:T(8,128)(2,1)}, u32[]{:S(2)}, u32[]{:S(2)}) collective-permute-start(bf16[2,512,256]{2,1,0:T(8,128)(2,1)} %get-tuple-element.48), channel_id=1, source_target_pairs={{0,1},{1,0},{2,3},{3,2},{4,5},{5,4},{6,7},{7,6},{8,9},{9,8},{10,11... | collective-permute-start | bytes 1572872 | tf_op jit(solution)/shard_map/ppermute | solution.py:313
  93.8 1.2 shard_map.122
  95.0 5.2 %all-to-all-done.1 = bf16[64,16,128]{2,1,0:T(8,128)(2,1)S(1)} async-done(((bf16[64,16,128]{2,1,0:T(8,128)(2,1)}), bf16[64,16,128]{2,1,0:T(8,128)(2,1)S(1)}, u32[]{:S(2)}, u32[]{:S(2)}) %all-to-all-start.1) | async-done | bytes 262176 | tf_op jit(solution)/shard_map/all_to_all | solution.py:375
  100.2 1.1 shard_map.123
  101.3 4.2 %all-to-all-start.2 = ((bf16[8,128,256]{2,1,0:T(8,128)(2,1)}), bf16[8,128,256]{2,1,0:T(8,128)(2,1)S(1)}, u32[]{:S(2)}, u32[]{:S(2)}) async-start(bf16[8,128,256]{2,1,0:T(8,128)(2,1)} %bitcast.47), calls=%async_computation.2 | async-start | bytes 1048576 | tf_op jit(solution)/shard_map/all_to_all | solution.py:384
  105.5 1.3 pad_maximum_fusion.gradient_ref
  106.8 9.3 %all-to-all-done.2._ = bf16[8,128,256]{2,1,0:T(8,128)(2,1)S(1)} async-done(((bf16[8,128,256]{2,1,0:T(8,128)(2,1)}), bf16[8,128,256]{2,1,0:T(8,128)(2,1)S(1)}, u32[]{:S(2)}, u32[]{:S(2)}) %all-to-all-start.2) | async-done | bytes 524320 | tf_op jit(solution)/shard_map/all_to_all | solution.py:384
  116.1 2.2 %copy-done = bf16[4096,512]{1,0:T(8,128)(2,1)S(1)} copy-done((bf16[4096,512]{1,0:T(8,128)(2,1)S(1)}, bf16[4096,512]{1,0:T(8,128)(2,1)}, u32[]{:S(2)}) %copy-start) | copy-done | bytes 4194328
  118.3 1.8 shard_map.125
  120.1 15.3 %all_to_all.30.parts_ref = bf16[8,256,128]{2,1,0:T(8,128)(2,1)S(1)} all-to-all(bf16[8,256,128]{2,1,0:T(8,128)(2,1)S(1)} %bitcast.45), channel_id=1, replica_groups=mesh['xh'=2,'zy'=4,'zh'=2,'zb'=2,'co'=2,'xl'=2,'yh'=2,'yl'=2] {'xh','yh'..., dimensions={0} | all-to-all | bytes 1048576 | tf_op jit(solution)/shard_map/all_to_all | solution.py:394
  135.5 1.0 shard_map.126
  136.5 9.7 %all-to-all-start.4 = ((bf16[64,16,128]{2,1,0:T(8,128)(2,1)}), bf16[64,16,128]{2,1,0:T(8,128)(2,1)S(1)}, u32[]{:S(2)}, u32[]{:S(2)}) async-start(bf16[64,16,128]{2,1,0:T(8,128)(2,1)} %bitcast.52), calls=%async_computation.5 | async-start | bytes 524288 | tf_op jit(solution)/shard_map/all_to_all | solution.py:400
  146.2 2.2 %copy-done.1 = bf16[4096,512]{1,0:T(8,128)(2,1)S(1)} copy-done((bf16[4096,512]{1,0:T(8,128)(2,1)S(1)}, bf16[4096,512]{1,0:T(8,128)(2,1)}, u32[]{:S(2)}) %copy-start.1) | copy-done | bytes 4194328
  148.4 3.1 %shard_map.124 = bf16[2,2,2,128,512]{4,3,2,1,0:T(8,128)(2,1)} custom-call(bf16[2,4,128,256]{3,2,1,0:T(8,128)(2,1)S(1)} %bitcast.38, bf16[4,2,4,128,512]{4,3,2,1,0:T(8,128)(2,1)S(1)} %bitcast.37), custom_call_target="tpu_custom_call" | custom-call | flops 1073741824 | bytes 6291456 | tf_op jit(solution)/shard_map/pallas_call | solution.py:175
  151.5 18.4 %all-to-all-done.4.grad_ref = bf16[64,16,128]{2,1,0:T(8,128)(2,1)S(1)} async-done(((bf16[64,16,128]{2,1,0:T(8,128)(2,1)}), bf16[64,16,128]{2,1,0:T(8,128)(2,1)S(1)}, u32[]{:S(2)}, u32[]{:S(2)}) %all-to-all-start.4) | async-done | bytes 262176 | tf_op jit(solution)/shard_map/all_to_all | solution.py:400
  169.9 2.6 %shard_map.127._ = bf16[64,16,128]{2,1,0:T(8,128)(2,1)} custom-call(bf16[64,16,128]{2,1,0:T(8,128)(2,1)S(1)} %all-to-all-done.4.grad_ref, bf16[1024,256]{1,0:T(8,128)(2,1)} %copy-done.12, bf16[320,640]{1,0:T(8,128)(2,1)S(1)} %copy-done.3), custom_call_target="tpu_custom_call" | custom-call | flops 335544320 | bytes 4194304 | tf_op jit(solution)/shard_map/pallas_call | solution.py:154
  172.5 4.2 %all-to-all-start.5 = ((bf16[64,16,128]{2,1,0:T(8,128)(2,1)}), bf16[64,16,128]{2,1,0:T(8,128)(2,1)S(1)}, u32[]{:S(2)}, u32[]{:S(2)}) async-start(bf16[64,16,128]{2,1,0:T(8,128)(2,1)} %shard_map.127._), calls=%async_computation.6 | async-start | bytes 524288 | tf_op jit(solution)/shard_map/all_to_all | solution.py:431
  176.8 1.0 copy.21
  177.8 0.8 slice_bitcast_fusion
  178.5 2.2 %collective-permute-start.6 = (f32[2,1024]{1,0:T(2,128)S(1)}, f32[2,1024]{1,0:T(2,128)S(1)}, u32[]{:S(2)}, u32[]{:S(2)}) collective-permute-start(f32[2,1024]{1,0:T(2,128)S(1)} %slice_bitcast_fusion), channel_id=1, source_target_pairs={{8,0},{16,8},{24,16},{32,24},{40,32},{48,40},{56,48},{64,56},{72,6... | collective-permute-start | bytes 24584 | tf_op jit(solution)/shard_map/ppermute | solution.py:309
  180.8 1.9 collective-permute-start.8
  182.7 6.4 %collective-permute-done.6.after_ref = f32[2,1024]{1,0:T(2,128)S(1)} collective-permute-done((f32[2,1024]{1,0:T(2,128)S(1)}, f32[2,1024]{1,0:T(2,128)S(1)}, u32[]{:S(2)}, u32[]{:S(2)}) %collective-permute-start.6) | collective-permute-done | bytes 8224 | tf_op jit(solution)/shard_map/ppermute | solution.py:309
  189.1 1.6 shard_map.128
  190.7 0.9 copy-done.5
  191.7 1.9 shard_map.129
  193.6 6.7 %all-to-all-done.5 = bf16[64,16,128]{2,1,0:T(8,128)(2,1)S(1)} async-done(((bf16[64,16,128]{2,1,0:T(8,128)(2,1)}), bf16[64,16,128]{2,1,0:T(8,128)(2,1)S(1)}, u32[]{:S(2)}, u32[]{:S(2)}) %all-to-all-start.5) | async-done | bytes 262176 | tf_op jit(solution)/shard_map/all_to_all | solution.py:431
  200.4 1.9 collective-permute-start.7
  202.6 1.9 shard_map.130
  204.6 0.8 collective-permute-done.7.after_ref
  205.4 0.7 shard_map.131
  (53 shorter events, 2.1 us)
Async XLA Ops:
  7.2 86.6 %copy-start.13 = (bf16[128,1024]{1,0:T(8,128)(2,1)S(1)}, bf16[128,1024]{1,0:T(8,128)(2,1)}, u32[]{:S(2)}) copy-start(bf16[128,1024]{1,0:T(8,128)(2,1)} %q_ref.1) | copy-start | bytes 786436
  7.2 86.6 %copy-start.9 = (bf16[128,1024]{1,0:T(8,128)(2,1)S(1)}, bf16[128,1024]{1,0:T(8,128)(2,1)}, u32[]{:S(2)}) copy-start(bf16[128,1024]{1,0:T(8,128)(2,1)} %v_ref.3) | copy-start | bytes 786436
  7.2 86.6 %copy-start.8 = (bf16[128,1024]{1,0:T(8,128)(2,1)S(1)}, bf16[128,1024]{1,0:T(8,128)(2,1)}, u32[]{:S(2)}) copy-start(bf16[128,1024]{1,0:T(8,128)(2,1)} %k_ref.3) | copy-start | bytes 786436
  7.2 86.6 %copy-start.7 = (f32[3,3,1024]{2,1,0:T(4,128)S(1)}, f32[3,3,1024]{2,1,0:T(4,128)}, u32[]{:S(2)}) copy-start(f32[3,3,1024]{2,1,0:T(4,128)} %taps_ref.9) | copy-start | bytes 110596
  7.2 66.9 %copy-start.16 = (bf16[128,512]{1,0:T(8,128)(2,1)S(1)}, bf16[128,512]{1,0:T(8,128)(2,1)}, u32[]{:S(2)}) copy-start(bf16[128,512]{1,0:T(8,128)(2,1)} %param.14) | copy-start | bytes 393220
  7.2 108.9 %all-gather.3.cloned.1.call-start = ((), (), s32[]{:S(2)}) async-start(), calls=%async_computation.8 | async-start | bytes 4325376 | tf_op jit(solution)/shard_map/all_gather | solution.py:340
  8.8 10.4 %collective-permute-start.1 = (bf16[128,512]{1,0:T(8,128)(2,1)}, bf16[128,512]{1,0:T(8,128)(2,1)S(1)}, u32[]{:S(2)}, u32[]{:S(2)}) collective-permute-start(bf16[128,512]{1,0:T(8,128)(2,1)} %param.13), channel_id=1, source_target_pairs={{0,0},{1,16},{4,8},{5,24},{8,256},{9,272},{12,264},{13,280},{16,1}... | collective-permute-start | bytes 393224 | tf_op jit(solution)/shard_map/ppermute | solution.py:327
  14.9 4.3 %collective-permute-start = (bf16[3,2,1024]{2,1,0:T(2,128)(2,1)S(1)}, bf16[3,2,1024]{2,1,0:T(2,128)(2,1)S(1)}, u32[]{:S(2)}, u32[]{:S(2)}) collective-permute-start(bf16[3,2,1024]{2,1,0:T(2,128)(2,1)S(1)} %pad_maximum_fusion.3), channel_id=1, source_target_pairs={{0,8},{8,16},{16,24},{24,32},{32,40},{40,48},{48,56},{56,64},{64,7... | collective-permute-start | bytes 36872 | tf_op jit(solution)/shard_map/ppermute | solution.py:309
  19.2 0.7 copy-start.14
  19.2 0.7 copy-start.17
  22.2 71.7 %copy-start.4 = (bf16[1024,128]{1,0:T(8,128)(2,1)S(1)}, bf16[1024,128]{1,0:T(8,128)(2,1)}, u32[]{:S(2)}) copy-start(bf16[1024,128]{1,0:T(8,128)(2,1)} %shard_map.119._) | copy-start | bytes 786436
  22.2 71.7 %copy-start.15 = (bf16[3,2,1024]{2,1,0:T(2,128)(2,1)S(1)}, bf16[3,2,1024]{2,1,0:T(2,128)(2,1)}, u32[]{:S(2)}) copy-start(bf16[3,2,1024]{2,1,0:T(2,128)(2,1)} %copy-done.14) | copy-start | bytes 36868
  22.2 45.9 %all-to-all-start = ((bf16[64,16,128]{2,1,0:T(8,128)(2,1)}), bf16[64,16,128]{2,1,0:T(8,128)(2,1)S(1)}, u32[]{:S(2)}, u32[]{:S(2)}) async-start(bf16[64,16,128]{2,1,0:T(8,128)(2,1)} %bitcast.44), calls=%async_computation | async-start | bytes 524288 | tf_op jit(solution)/shard_map/all_to_all | solution.py:364
  41.7 1.0 copy-start.2
  42.7 1.0 copy-start.10
  44.4 45.8 %copy-start.12 = (bf16[1024,256]{1,0:T(8,128)(2,1)}, bf16[1024,256]{1,0:T(8,128)(2,1)S(1)}, u32[]{:S(2)}) copy-start(bf16[1024,256]{1,0:T(8,128)(2,1)S(1)} %get-tuple-element.29.filter_spectrum.spectrum_ref) | copy-start | bytes 1572868
  69.9 30.4 %all-to-all-start.1 = ((bf16[64,16,128]{2,1,0:T(8,128)(2,1)}), bf16[64,16,128]{2,1,0:T(8,128)(2,1)S(1)}, u32[]{:S(2)}, u32[]{:S(2)}) async-start(bf16[64,16,128]{2,1,0:T(8,128)(2,1)} %get-tuple-element.31), calls=%async_computation.1 | async-start | bytes 524288 | tf_op jit(solution)/shard_map/all_to_all | solution.py:375
  74.3 9.0 %collective-permute-start.2 = (bf16[512,128]{1,0:T(8,128)(2,1)S(1)}, bf16[512,128]{1,0:T(8,128)(2,1)S(1)}, u32[]{:S(2)}, u32[]{:S(2)}) collective-permute-start(bf16[512,128]{1,0:T(8,128)(2,1)S(1)} %bitcast.48), channel_id=1, source_target_pairs={{0,256},{4,260},{256,0},{260,4},{1,257},{5,261},{257,1},{261,5},{2... | collective-permute-start | bytes 393224 | tf_op jit(solution)/shard_map/ppermute | solution.py:319
  79.2 7.3 %collective-permute-start.3 = (bf16[512,128]{1,0:T(8,128)(2,1)S(1)}, bf16[512,128]{1,0:T(8,128)(2,1)S(1)}, u32[]{:S(2)}, u32[]{:S(2)}) collective-permute-start(bf16[512,128]{1,0:T(8,128)(2,1)S(1)} %bitcast.49), channel_id=1, source_target_pairs={{0,4},{4,0},{256,260},{260,256},{1,5},{5,1},{257,261},{261,257},{2... | collective-permute-start | bytes 393224 | tf_op jit(solution)/shard_map/ppermute | solution.py:319
  81.1 8.0 %collective-permute-start.4 = (bf16[512,128]{1,0:T(8,128)(2,1)S(1)}, bf16[512,128]{1,0:T(8,128)(2,1)S(1)}, u32[]{:S(2)}, u32[]{:S(2)}) collective-permute-start(bf16[512,128]{1,0:T(8,128)(2,1)S(1)} %bitcast.50), channel_id=1, source_target_pairs={{0,260},{4,256},{256,4},{260,0},{1,261},{5,257},{257,5},{261,1},{2... | collective-permute-start | bytes 393224 | tf_op jit(solution)/shard_map/ppermute | solution.py:319
  90.2 15.4 %collective-permute-start.5 = (bf16[2,512,256]{2,1,0:T(8,128)(2,1)}, bf16[2,512,256]{2,1,0:T(8,128)(2,1)}, u32[]{:S(2)}, u32[]{:S(2)}) collective-permute-start(bf16[2,512,256]{2,1,0:T(8,128)(2,1)} %get-tuple-element.48), channel_id=1, source_target_pairs={{0,1},{1,0},{2,3},{3,2},{4,5},{5,4},{6,7},{7,6},{8,9},{9,8},{10,11... | collective-permute-start | bytes 1572872 | tf_op jit(solution)/shard_map/ppermute | solution.py:313
  101.3 14.8 %all-to-all-start.2 = ((bf16[8,128,256]{2,1,0:T(8,128)(2,1)}), bf16[8,128,256]{2,1,0:T(8,128)(2,1)S(1)}, u32[]{:S(2)}, u32[]{:S(2)}) async-start(bf16[8,128,256]{2,1,0:T(8,128)(2,1)} %bitcast.47), calls=%async_computation.2 | async-start | bytes 1048576 | tf_op jit(solution)/shard_map/all_to_all | solution.py:384
  116.1 2.2 %copy-start = (bf16[4096,512]{1,0:T(8,128)(2,1)S(1)}, bf16[4096,512]{1,0:T(8,128)(2,1)}, u32[]{:S(2)}) copy-start(bf16[4096,512]{1,0:T(8,128)(2,1)} %all-gather.3.cloned.1.call-done) | copy-start | bytes 12582916
  135.5 34.5 %copy-start.3 = (bf16[320,640]{1,0:T(8,128)(2,1)S(1)}, bf16[320,640]{1,0:T(8,128)(2,1)}, u32[]{:S(2)}) copy-start(bf16[320,640]{1,0:T(8,128)(2,1)} %constant.16.clone.steps) | copy-start | bytes 1228804
  136.5 33.5 %all-to-all-start.4 = ((bf16[64,16,128]{2,1,0:T(8,128)(2,1)}), bf16[64,16,128]{2,1,0:T(8,128)(2,1)S(1)}, u32[]{:S(2)}, u32[]{:S(2)}) async-start(bf16[64,16,128]{2,1,0:T(8,128)(2,1)} %bitcast.52), calls=%async_computation.5 | async-start | bytes 524288 | tf_op jit(solution)/shard_map/all_to_all | solution.py:400
  146.2 59.9 %reduce-scatter.2.cloned.1.call-start = ((), (), s32[]{:S(2)}) async-start(), calls=%async_computation.7 | async-start | bytes 1179648 | tf_op jit(solution)/shard_map/reduce_scatter | solution.py:419
  146.2 2.2 %copy-start.1 = (bf16[4096,512]{1,0:T(8,128)(2,1)S(1)}, bf16[4096,512]{1,0:T(8,128)(2,1)}, u32[]{:S(2)}) copy-start(bf16[4096,512]{1,0:T(8,128)(2,1)} %all-gather.3.cloned.1.call-done) | copy-start | bytes 12582916
  148.4 28.3 %copy-start.6 = (f32[1024,128]{1,0:T(8,128)S(1)}, f32[1024,128]{1,0:T(8,128)}, u32[]{:S(2)}) copy-start(f32[1024,128]{1,0:T(8,128)} %get-tuple-element.36.qg_ref) | copy-start | bytes 1572868
  148.4 42.3 %copy-start.11 = (bf16[1024,256]{1,0:T(8,128)(2,1)S(1)}, bf16[1024,256]{1,0:T(8,128)(2,1)}, u32[]{:S(2)}) copy-start(bf16[1024,256]{1,0:T(8,128)(2,1)} %get-tuple-element.37.product_spectrum) | copy-start | bytes 1572868
  172.5 27.8 %all-to-all-start.5 = ((bf16[64,16,128]{2,1,0:T(8,128)(2,1)}), bf16[64,16,128]{2,1,0:T(8,128)(2,1)S(1)}, u32[]{:S(2)}, u32[]{:S(2)}) async-start(bf16[64,16,128]{2,1,0:T(8,128)(2,1)} %shard_map.127._), calls=%async_computation.6 | async-start | bytes 524288 | tf_op jit(solution)/shard_map/all_to_all | solution.py:431
  178.5 10.5 %collective-permute-start.6 = (f32[2,1024]{1,0:T(2,128)S(1)}, f32[2,1024]{1,0:T(2,128)S(1)}, u32[]{:S(2)}, u32[]{:S(2)}) collective-permute-start(f32[2,1024]{1,0:T(2,128)S(1)} %slice_bitcast_fusion), channel_id=1, source_target_pairs={{8,0},{16,8},{24,16},{32,24},{40,32},{48,40},{56,48},{64,56},{72,6... | collective-permute-start | bytes 24584 | tf_op jit(solution)/shard_map/ppermute | solution.py:309
  180.8 23.8 %collective-permute-start.8 = (f32[2,2,1024]{2,1,0:T(2,128)S(1)}, f32[2,2,1024]{2,1,0:T(2,128)S(1)}, u32[]{:S(2)}, u32[]{:S(2)}) collective-permute-start(f32[2,2,1024]{2,1,0:T(2,128)S(1)} %pad_maximum_fusion.2), channel_id=1, source_target_pairs={{8,0},{16,8},{24,16},{32,24},{40,32},{48,40},{56,48},{64,56},{72,6... | collective-permute-start | bytes 49160 | tf_op jit(solution)/shard_map/ppermute | solution.py:309
  190.7 1.0 copy-start.5
  200.4 4.9 %collective-permute-start.7 = (bf16[2,1024]{1,0:T(2,128)(2,1)S(1)}, bf16[2,1024]{1,0:T(2,128)(2,1)S(1)}, u32[]{:S(2)}, u32[]{:S(2)}) collective-permute-start(bf16[2,1024]{1,0:T(2,128)(2,1)S(1)} %bitcast.53), channel_id=1, source_target_pairs={{8,0},{16,8},{24,16},{32,24},{40,32},{48,40},{56,48},{64,56},{72,6... | collective-permute-start | bytes 12296 | tf_op jit(solution)/shard_map/ppermute | solution.py:309
Sparse Core Ops, SparseCore 0:
  20.0 94.4 all-gather.2
  151.7 41.9 reduce-scatter.1

commit v8 on v6

--- a/solution.py
+++ b/solution.py
@@ -358,7 +358,7 @@
         filter_inputs, kinds,
         [(queries, tokens, 1), (keys, tokens, 1), (values, tokens, 1),
          (before, (3, 2, chunk), 2), (short_taps, taps_block, 2), (product, None, None)],
-        [plane, plane, plane, ((width, rows), F32, channels, 0)], 3 * 2**20, limit=WHOLE_VMEM,
+        [plane, plane, plane, ((width, rows), F32, channels, 0)], 3 * 2**20,
     )
 
     product_owned = lax.all_to_all(product.reshape(BLOCKS, CHANNELS, LANES), SEQ, 0, 0, tiled=True)

time: 214 us -> 214 us (level)
  Pallas kernels: 27.8 us -> 25.3 us
    pallas_call x9, Pallas kernels: 21.7 us -> 19.2 us  [run_blocks(): pl.pallas_call(kernel, grid=(steps,), in_specs=[spec(block, axis) for _,...]
    unnamed x35 -> x43, local copies, waits for them, and re-layouts: 7.91 us -> 7.92 us
  transfers between devices with their start and end apart: 16 -> 16, of which waited for: 10 -> 10; matrix products, arithmetic and copies ran while one was open for 1% -> 2% of each run, Pallas kernels for 11% -> 9%
where the time goes in v8:
time: 214 us; the launch traced here: 213 us
  waiting for transfers between devices  77.9 us (36%)
  starting transfers between devices  69.4 us (32%)
  Pallas kernels  25.3 us (12%)
  between operations  14.4 us (7%)
  blocking collectives  13.8 us (6%)
  local copies, waits for them, and re-layouts  9.81 us (5%)
  other arithmetic  2.54 us (1%)
    all_to_all x1, waiting for transfers between devices, per_device(): lax.all_to_all(product.reshape(BLOCKS, CHANNELS, LANES), SEQ, 0, 0, tiled...  23.7 us
    all_to_all x1, starting transfers between devices, per_device(): lax.all_to_all(product.reshape(BLOCKS, CHANNELS, LANES), SEQ, 0, 0, tiled...  19.5 us
    pallas_call x9, Pallas kernels, run_blocks(): pl.pallas_call(kernel, grid=(steps,), in_specs=[spec(block, axis) for _,...  19.2 us
    all_to_all x1, waiting for transfers between devices, per_device(): lax.all_to_all(long_grad.reshape(BLOCKS, CHANNELS, LANES), SEQ, 0, 0, til...  18.5 us
    all_to_all x1, blocking collectives, per_device(): lax.all_to_all(partial.reshape(8, chunk, rows), PLANE, 0, 0, tiled=True)  13.8 us
    ppermute x4, waiting for transfers between devices, shift(): lax.ppermute(value, SEQ, [(i, i + steps) for i in range(first, last)])  11.1 us
    all_to_all x1, starting transfers between devices, per_device(): lax.all_to_all(long_grad.reshape(BLOCKS, CHANNELS, LANES), SEQ, 0, 0, til...  9.41 us
    all_to_all x1, waiting for transfers between devices, per_device(): lax.all_to_all(gated.reshape(8, rows, chunk), PLANE, 0, 0, tiled=True)  9.26 us
  transfers between devices with their start and end apart: 16, of which 10 were waited for; matrix products, arithmetic and copies ran while one was open for 2% of the time, Pallas kernels for 9%

profile of v8, /device:TPU:1, one launch (start us, length us, event | category | flops | bytes accessed | tf_op | source)
XLA Modules:
  0.0 213.1 jit_solution(1508524269638967923)
XLA Ops:
  7.3 0.8 slice_bitcast_fusion.5
  8.1 0.7 slice_bitcast_fusion.3
  8.8 6.0 %collective-permute-start.1 = (bf16[128,512]{1,0:T(8,128)(2,1)}, bf16[128,512]{1,0:T(8,128)(2,1)S(1)}, u32[]{:S(2)}, u32[]{:S(2)}) collective-permute-start(bf16[128,512]{1,0:T(8,128)(2,1)} %param.13), channel_id=1, source_target_pairs={{0,0},{1,16},{4,8},{5,24},{8,256},{9,272},{12,264},{13,280},{16,1}... | collective-permute-start | bytes 393224 | tf_op jit(solution)/shard_map/ppermute | solution.py:329
  14.9 1.9 collective-permute-start
  16.8 2.4 %collective-permute-done.before_ref = bf16[3,2,1024]{2,1,0:T(2,128)(2,1)S(1)} collective-permute-done((bf16[3,2,1024]{2,1,0:T(2,128)(2,1)S(1)}, bf16[3,2,1024]{2,1,0:T(2,128)(2,1)S(1)}, u32[]{:S(2)}, u32[]{:S(2)}) %collective-permute-start) | collective-permute-done | bytes 12320 | tf_op jit(solution)/shard_map/ppermute | solution.py:311
  19.9 2.2 %shard_map.119._ = bf16[1024,128]{1,0:T(8,128)(2,1)} custom-call(bf16[128,1024]{1,0:T(8,128)(2,1)} %k_ref.3, bf16[128,1024]{1,0:T(8,128)(2,1)} %v_ref.3, bf16[3,2,1024]{2,1,0:T(2,128)(2,1)} %copy-done.16, f32[3,3,1024]{2,1,0:T(4,128)} %taps_ref.9), custom_call_target="tpu_custom_call" | custom-call | flops 1000000 | bytes 1048576 | tf_op jit(solution)/shard_map/pallas_call | solution.py:168
  22.2 19.5 %all-to-all-start = ((bf16[64,16,128]{2,1,0:T(8,128)(2,1)}), bf16[64,16,128]{2,1,0:T(8,128)(2,1)S(1)}, u32[]{:S(2)}, u32[]{:S(2)}) async-start(bf16[64,16,128]{2,1,0:T(8,128)(2,1)} %bitcast.42), calls=%async_computation | async-start | bytes 524288 | tf_op jit(solution)/shard_map/all_to_all | solution.py:364
  41.7 1.0 copy-done
  42.7 1.0 copy-done.13
  44.3 23.7 %all-to-all-done.product_ref = bf16[64,16,128]{2,1,0:T(8,128)(2,1)S(1)} async-done(((bf16[64,16,128]{2,1,0:T(8,128)(2,1)}), bf16[64,16,128]{2,1,0:T(8,128)(2,1)S(1)}, u32[]{:S(2)}, u32[]{:S(2)}) %all-to-all-start) | async-done | bytes 262176 | tf_op jit(solution)/shard_map/all_to_all | solution.py:364
  68.1 1.0 copy-done.1
  69.1 1.8 shard_map.121
  70.9 4.3 %all-to-all-start.1 = ((bf16[64,16,128]{2,1,0:T(8,128)(2,1)}), bf16[64,16,128]{2,1,0:T(8,128)(2,1)S(1)}, u32[]{:S(2)}, u32[]{:S(2)}) async-start(bf16[64,16,128]{2,1,0:T(8,128)(2,1)} %get-tuple-element.27), calls=%async_computation.1 | async-start | bytes 524288 | tf_op jit(solution)/shard_map/all_to_all | solution.py:375
  75.3 4.9 %collective-permute-start.2 = (bf16[512,128]{1,0:T(8,128)(2,1)S(1)}, bf16[512,128]{1,0:T(8,128)(2,1)S(1)}, u32[]{:S(2)}, u32[]{:S(2)}) collective-permute-start(bf16[512,128]{1,0:T(8,128)(2,1)S(1)} %bitcast.48), channel_id=1, source_target_pairs={{0,256},{4,260},{256,0},{260,4},{1,257},{5,261},{257,1},{261,5},{2... | collective-permute-start | bytes 393224 | tf_op jit(solution)/shard_map/ppermute | solution.py:321
  80.2 1.9 collective-permute-start.3
  82.1 2.2 %collective-permute-start.4 = (bf16[512,128]{1,0:T(8,128)(2,1)S(1)}, bf16[512,128]{1,0:T(8,128)(2,1)S(1)}, u32[]{:S(2)}, u32[]{:S(2)}) collective-permute-start(bf16[512,128]{1,0:T(8,128)(2,1)S(1)} %bitcast.50), channel_id=1, source_target_pairs={{0,260},{4,256},{256,4},{260,0},{1,261},{5,257},{257,5},{261,1},{2... | collective-permute-start | bytes 393224 | tf_op jit(solution)/shard_map/ppermute | solution.py:321
  84.4 3.2 %collective-permute-done.3 = bf16[512,128]{1,0:T(8,128)(2,1)S(1)} collective-permute-done((bf16[512,128]{1,0:T(8,128)(2,1)S(1)}, bf16[512,128]{1,0:T(8,128)(2,1)S(1)}, u32[]{:S(2)}, u32[]{:S(2)}) %collective-permute-start.3) | collective-permute-done | bytes 131104 | tf_op jit(solution)/shard_map/ppermute | solution.py:321
  87.6 2.4 %collective-permute-done.4 = bf16[512,128]{1,0:T(8,128)(2,1)S(1)} collective-permute-done((bf16[512,128]{1,0:T(8,128)(2,1)S(1)}, bf16[512,128]{1,0:T(8,128)(2,1)S(1)}, u32[]{:S(2)}, u32[]{:S(2)}) %collective-permute-start.4) | collective-permute-done | bytes 131104 | tf_op jit(solution)/shard_map/ppermute | solution.py:321
  90.0 1.1 fusion
  91.1 4.0 %collective-permute-start.5 = (bf16[2,512,256]{2,1,0:T(8,128)(2,1)}, bf16[2,512,256]{2,1,0:T(8,128)(2,1)}, u32[]{:S(2)}, u32[]{:S(2)}) collective-permute-start(bf16[2,512,256]{2,1,0:T(8,128)(2,1)} %get-tuple-element.44), channel_id=1, source_target_pairs={{0,1},{1,0},{2,3},{3,2},{4,5},{5,4},{6,7},{7,6},{8,9},{9,8},{10,11... | collective-permute-start | bytes 1572872 | tf_op jit(solution)/shard_map/ppermute | solution.py:315
  95.1 1.2 shard_map.122
  96.3 0.8 copy-done.11
  97.1 3.9 %all-to-all-done.1 = bf16[64,16,128]{2,1,0:T(8,128)(2,1)S(1)} async-done(((bf16[64,16,128]{2,1,0:T(8,128)(2,1)}), bf16[64,16,128]{2,1,0:T(8,128)(2,1)S(1)}, u32[]{:S(2)}, u32[]{:S(2)}) %all-to-all-start.1) | async-done | bytes 262176 | tf_op jit(solution)/shard_map/all_to_all | solution.py:375
  101.0 1.0 copy-done.12
  102.1 1.0 shard_map.123
  103.1 4.9 %all-to-all-start.2 = ((bf16[8,128,256]{2,1,0:T(8,128)(2,1)}), bf16[8,128,256]{2,1,0:T(8,128)(2,1)S(1)}, u32[]{:S(2)}, u32[]{:S(2)}) async-start(bf16[8,128,256]{2,1,0:T(8,128)(2,1)} %bitcast.47), calls=%async_computation.2 | async-start | bytes 1048576 | tf_op jit(solution)/shard_map/all_to_all | solution.py:384
  108.1 1.3 pad_maximum_fusion.gradient_ref
  109.4 9.3 %all-to-all-done.2._ = bf16[8,128,256]{2,1,0:T(8,128)(2,1)S(1)} async-done(((bf16[8,128,256]{2,1,0:T(8,128)(2,1)}), bf16[8,128,256]{2,1,0:T(8,128)(2,1)S(1)}, u32[]{:S(2)}, u32[]{:S(2)}) %all-to-all-start.2) | async-done | bytes 524320 | tf_op jit(solution)/shard_map/all_to_all | solution.py:384
  118.7 4.3 %shard_map.125 = bf16[2,4,256,128]{3,2,1,0:T(8,128)(2,1)S(1)} custom-call(s32[4]{0:T(128)S(1)} %pad_add_fusion.place_ref, bf16[2,2,512,256]{3,2,1,0:T(8,128)(2,1)S(1)} %pad_maximum_fusion.gradient_ref, bf16[4,2,4,128,512]{4,3,2,1,0:T(8,128)(2,1)} %bitcast.45, bf16[8,128,256]{2,1,0:T(8,128)(2,1)S(1)} %all-to-all-done.2._), custom_call_target="tpu_custom_call" | custom-call | flops 1073741824 | bytes 6291456 | tf_op jit(solution)/shard_map/pallas_call | solution.py:168
  123.0 13.8 %all_to_all.30.parts_ref = bf16[8,256,128]{2,1,0:T(8,128)(2,1)S(1)} all-to-all(bf16[8,256,128]{2,1,0:T(8,128)(2,1)S(1)} %bitcast.43), channel_id=1, replica_groups=mesh['xh'=2,'zy'=4,'zh'=2,'zb'=2,'co'=2,'xl'=2,'yh'=2,'yl'=2] {'xh','yh'..., dimensions={0} | all-to-all | bytes 1048576 | tf_op jit(solution)/shard_map/all_to_all | solution.py:393
  136.8 1.0 shard_map.126
  137.8 9.4 %all-to-all-start.4 = ((bf16[64,16,128]{2,1,0:T(8,128)(2,1)}), bf16[64,16,128]{2,1,0:T(8,128)(2,1)S(1)}, u32[]{:S(2)}, u32[]{:S(2)}) async-start(bf16[64,16,128]{2,1,0:T(8,128)(2,1)} %bitcast.52), calls=%async_computation.5 | async-start | bytes 524288 | tf_op jit(solution)/shard_map/all_to_all | solution.py:399
  147.2 5.2 %shard_map.124 = bf16[2,2,2,128,512]{4,3,2,1,0:T(8,128)(2,1)} custom-call(bf16[2,4,128,256]{3,2,1,0:T(8,128)(2,1)S(1)} %bitcast.36, bf16[4,2,4,128,512]{4,3,2,1,0:T(8,128)(2,1)} %bitcast.46), custom_call_target="tpu_custom_call" | custom-call | flops 1073741824 | bytes 6291456 | tf_op jit(solution)/shard_map/pallas_call | solution.py:168
  152.5 18.5 %all-to-all-done.4.grad_ref = bf16[64,16,128]{2,1,0:T(8,128)(2,1)S(1)} async-done(((bf16[64,16,128]{2,1,0:T(8,128)(2,1)}), bf16[64,16,128]{2,1,0:T(8,128)(2,1)S(1)}, u32[]{:S(2)}, u32[]{:S(2)}) %all-to-all-start.4) | async-done | bytes 262176 | tf_op jit(solution)/shard_map/all_to_all | solution.py:399
  170.9 1.8 shard_map.127._
  172.8 4.2 %all-to-all-start.5 = ((bf16[64,16,128]{2,1,0:T(8,128)(2,1)}), bf16[64,16,128]{2,1,0:T(8,128)(2,1)S(1)}, u32[]{:S(2)}, u32[]{:S(2)}) async-start(bf16[64,16,128]{2,1,0:T(8,128)(2,1)} %shard_map.127._), calls=%async_computation.6 | async-start | bytes 524288 | tf_op jit(solution)/shard_map/all_to_all | solution.py:429
  177.2 2.2 %collective-permute-start.6 = (f32[2,1024]{1,0:T(2,128)S(1)}, f32[2,1024]{1,0:T(2,128)S(1)}, u32[]{:S(2)}, u32[]{:S(2)}) collective-permute-start(f32[2,1024]{1,0:T(2,128)S(1)} %slice_bitcast_fusion), channel_id=1, source_target_pairs={{8,0},{16,8},{24,16},{32,24},{40,32},{48,40},{56,48},{64,56},{72,6... | collective-permute-start | bytes 24584 | tf_op jit(solution)/shard_map/ppermute | solution.py:311
  179.4 1.9 collective-permute-start.8
  181.4 7.9 %collective-permute-done.6.after_ref = f32[2,1024]{1,0:T(2,128)S(1)} collective-permute-done((f32[2,1024]{1,0:T(2,128)S(1)}, f32[2,1024]{1,0:T(2,128)S(1)}, u32[]{:S(2)}, u32[]{:S(2)}) %collective-permute-start.6) | collective-permute-done | bytes 8224 | tf_op jit(solution)/shard_map/ppermute | solution.py:311
  189.3 1.6 shard_map.128
  190.9 0.9 copy-done.4
  191.9 1.0 copy-done.14
  192.9 1.9 shard_map.129
  194.8 5.7 %all-to-all-done.5 = bf16[64,16,128]{2,1,0:T(8,128)(2,1)S(1)} async-done(((bf16[64,16,128]{2,1,0:T(8,128)(2,1)}), bf16[64,16,128]{2,1,0:T(8,128)(2,1)S(1)}, u32[]{:S(2)}, u32[]{:S(2)}) %all-to-all-start.5) | async-done | bytes 262176 | tf_op jit(solution)/shard_map/all_to_all | solution.py:429
  200.7 1.9 collective-permute-start.7
  202.9 1.9 shard_map.130
  204.8 0.8 collective-permute-done.7.after_ref
  205.6 0.7 shard_map.131
  (57 shorter events, 2.3 us)
Async XLA Ops:
  7.2 87.9 %copy-start.15 = (bf16[128,1024]{1,0:T(8,128)(2,1)S(1)}, bf16[128,1024]{1,0:T(8,128)(2,1)}, u32[]{:S(2)}) copy-start(bf16[128,1024]{1,0:T(8,128)(2,1)} %q_ref.1) | copy-start | bytes 786436
  7.2 87.9 %copy-start.8 = (bf16[128,1024]{1,0:T(8,128)(2,1)S(1)}, bf16[128,1024]{1,0:T(8,128)(2,1)}, u32[]{:S(2)}) copy-start(bf16[128,1024]{1,0:T(8,128)(2,1)} %v_ref.3) | copy-start | bytes 786436
  7.2 87.9 %copy-start.7 = (bf16[128,1024]{1,0:T(8,128)(2,1)S(1)}, bf16[128,1024]{1,0:T(8,128)(2,1)}, u32[]{:S(2)}) copy-start(bf16[128,1024]{1,0:T(8,128)(2,1)} %k_ref.3) | copy-start | bytes 786436
  7.2 87.9 %copy-start.6 = (f32[3,3,1024]{2,1,0:T(4,128)S(1)}, f32[3,3,1024]{2,1,0:T(4,128)}, u32[]{:S(2)}) copy-start(f32[3,3,1024]{2,1,0:T(4,128)} %taps_ref.9) | copy-start | bytes 110596
  7.2 67.9 %copy-start.18 = (bf16[128,512]{1,0:T(8,128)(2,1)S(1)}, bf16[128,512]{1,0:T(8,128)(2,1)}, u32[]{:S(2)}) copy-start(bf16[128,512]{1,0:T(8,128)(2,1)} %param.14) | copy-start | bytes 393220
  7.2 111.5 %all-gather.3.cloned.1.call-start = ((), (), s32[]{:S(2)}) async-start(), calls=%async_computation.8 | async-start | bytes 4325376 | tf_op jit(solution)/shard_map/all_gather | solution.py:342
  8.8 10.4 %collective-permute-start.1 = (bf16[128,512]{1,0:T(8,128)(2,1)}, bf16[128,512]{1,0:T(8,128)(2,1)S(1)}, u32[]{:S(2)}, u32[]{:S(2)}) collective-permute-start(bf16[128,512]{1,0:T(8,128)(2,1)} %param.13), channel_id=1, source_target_pairs={{0,0},{1,16},{4,8},{5,24},{8,256},{9,272},{12,264},{13,280},{16,1}... | collective-permute-start | bytes 393224 | tf_op jit(solution)/shard_map/ppermute | solution.py:329
  14.9 4.3 %collective-permute-start = (bf16[3,2,1024]{2,1,0:T(2,128)(2,1)S(1)}, bf16[3,2,1024]{2,1,0:T(2,128)(2,1)S(1)}, u32[]{:S(2)}, u32[]{:S(2)}) collective-permute-start(bf16[3,2,1024]{2,1,0:T(2,128)(2,1)S(1)} %pad_maximum_fusion.3), channel_id=1, source_target_pairs={{0,8},{8,16},{16,24},{24,32},{32,40},{40,48},{48,56},{56,64},{64,7... | collective-permute-start | bytes 36872 | tf_op jit(solution)/shard_map/ppermute | solution.py:311
  19.2 0.7 copy-start.16
  19.2 0.7 copy-start.19
  22.2 72.9 %copy-start.3 = (bf16[1024,128]{1,0:T(8,128)(2,1)S(1)}, bf16[1024,128]{1,0:T(8,128)(2,1)}, u32[]{:S(2)}) copy-start(bf16[1024,128]{1,0:T(8,128)(2,1)} %shard_map.119._) | copy-start | bytes 786436
  22.2 72.9 %copy-start.17 = (bf16[3,2,1024]{2,1,0:T(2,128)(2,1)S(1)}, bf16[3,2,1024]{2,1,0:T(2,128)(2,1)}, u32[]{:S(2)}) copy-start(bf16[3,2,1024]{2,1,0:T(2,128)(2,1)} %copy-done.16) | copy-start | bytes 36868
  22.2 45.9 %all-to-all-start = ((bf16[64,16,128]{2,1,0:T(8,128)(2,1)}), bf16[64,16,128]{2,1,0:T(8,128)(2,1)S(1)}, u32[]{:S(2)}, u32[]{:S(2)}) async-start(bf16[64,16,128]{2,1,0:T(8,128)(2,1)} %bitcast.42), calls=%async_computation | async-start | bytes 524288 | tf_op jit(solution)/shard_map/all_to_all | solution.py:364
  41.7 1.0 copy-start
  42.7 1.0 copy-start.13
  68.1 1.0 copy-start.1
  70.9 30.2 %all-to-all-start.1 = ((bf16[64,16,128]{2,1,0:T(8,128)(2,1)}), bf16[64,16,128]{2,1,0:T(8,128)(2,1)S(1)}, u32[]{:S(2)}, u32[]{:S(2)}) async-start(bf16[64,16,128]{2,1,0:T(8,128)(2,1)} %get-tuple-element.27), calls=%async_computation.1 | async-start | bytes 524288 | tf_op jit(solution)/shard_map/all_to_all | solution.py:375
  75.3 9.0 %collective-permute-start.2 = (bf16[512,128]{1,0:T(8,128)(2,1)S(1)}, bf16[512,128]{1,0:T(8,128)(2,1)S(1)}, u32[]{:S(2)}, u32[]{:S(2)}) collective-permute-start(bf16[512,128]{1,0:T(8,128)(2,1)S(1)} %bitcast.48), channel_id=1, source_target_pairs={{0,256},{4,260},{256,0},{260,4},{1,257},{5,261},{257,1},{261,5},{2... | collective-permute-start | bytes 393224 | tf_op jit(solution)/shard_map/ppermute | solution.py:321
  80.2 7.4 %collective-permute-start.3 = (bf16[512,128]{1,0:T(8,128)(2,1)S(1)}, bf16[512,128]{1,0:T(8,128)(2,1)S(1)}, u32[]{:S(2)}, u32[]{:S(2)}) collective-permute-start(bf16[512,128]{1,0:T(8,128)(2,1)S(1)} %bitcast.49), channel_id=1, source_target_pairs={{0,4},{4,0},{256,260},{260,256},{1,5},{5,1},{257,261},{261,257},{2... | collective-permute-start | bytes 393224 | tf_op jit(solution)/shard_map/ppermute | solution.py:321
  82.1 7.9 %collective-permute-start.4 = (bf16[512,128]{1,0:T(8,128)(2,1)S(1)}, bf16[512,128]{1,0:T(8,128)(2,1)S(1)}, u32[]{:S(2)}, u32[]{:S(2)}) collective-permute-start(bf16[512,128]{1,0:T(8,128)(2,1)S(1)} %bitcast.50), channel_id=1, source_target_pairs={{0,260},{4,256},{256,4},{260,0},{1,261},{5,257},{257,5},{261,1},{2... | collective-permute-start | bytes 393224 | tf_op jit(solution)/shard_map/ppermute | solution.py:321
  91.1 17.0 %collective-permute-start.5 = (bf16[2,512,256]{2,1,0:T(8,128)(2,1)}, bf16[2,512,256]{2,1,0:T(8,128)(2,1)}, u32[]{:S(2)}, u32[]{:S(2)}) collective-permute-start(bf16[2,512,256]{2,1,0:T(8,128)(2,1)} %get-tuple-element.44), channel_id=1, source_target_pairs={{0,1},{1,0},{2,3},{3,2},{4,5},{5,4},{6,7},{7,6},{8,9},{9,8},{10,11... | collective-permute-start | bytes 1572872 | tf_op jit(solution)/shard_map/ppermute | solution.py:315
  96.3 0.8 copy-start.11
  97.1 11.0 %copy-start.9 = (f32[1024,128]{1,0:T(8,128)}, f32[1024,128]{1,0:T(8,128)S(1)}, u32[]{:S(2)}) copy-start(f32[1024,128]{1,0:T(8,128)S(1)} %get-tuple-element.30.qc_ref) | copy-start | bytes 1572868
  101.0 1.0 copy-start.12
  103.1 15.6 %all-to-all-start.2 = ((bf16[8,128,256]{2,1,0:T(8,128)(2,1)}), bf16[8,128,256]{2,1,0:T(8,128)(2,1)S(1)}, u32[]{:S(2)}, u32[]{:S(2)}) async-start(bf16[8,128,256]{2,1,0:T(8,128)(2,1)} %bitcast.47), calls=%async_computation.2 | async-start | bytes 1048576 | tf_op jit(solution)/shard_map/all_to_all | solution.py:384
  118.7 18.1 %copy-start.10 = (f32[1024,128]{1,0:T(8,128)S(1)}, f32[1024,128]{1,0:T(8,128)}, u32[]{:S(2)}) copy-start(f32[1024,128]{1,0:T(8,128)} %copy-done.9) | copy-start | bytes 1572868
  136.8 34.2 %copy-start.2 = (bf16[320,640]{1,0:T(8,128)(2,1)S(1)}, bf16[320,640]{1,0:T(8,128)(2,1)}, u32[]{:S(2)}) copy-start(bf16[320,640]{1,0:T(8,128)(2,1)} %constant.16.clone.steps) | copy-start | bytes 1228804
  137.8 33.2 %all-to-all-start.4 = ((bf16[64,16,128]{2,1,0:T(8,128)(2,1)}), bf16[64,16,128]{2,1,0:T(8,128)(2,1)S(1)}, u32[]{:S(2)}, u32[]{:S(2)}) async-start(bf16[64,16,128]{2,1,0:T(8,128)(2,1)} %bitcast.52), calls=%async_computation.5 | async-start | bytes 524288 | tf_op jit(solution)/shard_map/all_to_all | solution.py:399
  147.2 59.1 %reduce-scatter.2.cloned.1.call-start = ((), (), s32[]{:S(2)}) async-start(), calls=%async_computation.7 | async-start | bytes 1179648 | tf_op jit(solution)/shard_map/reduce_scatter | solution.py:417
  147.2 29.7 %copy-start.5 = (f32[1024,128]{1,0:T(8,128)S(1)}, f32[1024,128]{1,0:T(8,128)}, u32[]{:S(2)}) copy-start(f32[1024,128]{1,0:T(8,128)} %get-tuple-element.32.qg_ref) | copy-start | bytes 1572868
  172.8 27.8 %all-to-all-start.5 = ((bf16[64,16,128]{2,1,0:T(8,128)(2,1)}), bf16[64,16,128]{2,1,0:T(8,128)(2,1)S(1)}, u32[]{:S(2)}, u32[]{:S(2)}) async-start(bf16[64,16,128]{2,1,0:T(8,128)(2,1)} %shard_map.127._), calls=%async_computation.6 | async-start | bytes 524288 | tf_op jit(solution)/shard_map/all_to_all | solution.py:429
  177.2 12.1 %collective-permute-start.6 = (f32[2,1024]{1,0:T(2,128)S(1)}, f32[2,1024]{1,0:T(2,128)S(1)}, u32[]{:S(2)}, u32[]{:S(2)}) collective-permute-start(f32[2,1024]{1,0:T(2,128)S(1)} %slice_bitcast_fusion), channel_id=1, source_target_pairs={{8,0},{16,8},{24,16},{32,24},{40,32},{48,40},{56,48},{64,56},{72,6... | collective-permute-start | bytes 24584 | tf_op jit(solution)/shard_map/ppermute | solution.py:311
  179.4 25.4 %collective-permute-start.8 = (f32[2,2,1024]{2,1,0:T(2,128)S(1)}, f32[2,2,1024]{2,1,0:T(2,128)S(1)}, u32[]{:S(2)}, u32[]{:S(2)}) collective-permute-start(f32[2,2,1024]{2,1,0:T(2,128)S(1)} %pad_maximum_fusion.2), channel_id=1, source_target_pairs={{8,0},{16,8},{24,16},{32,24},{40,32},{48,40},{56,48},{64,56},{72,6... | collective-permute-start | bytes 49160 | tf_op jit(solution)/shard_map/ppermute | solution.py:311
  190.9 0.9 copy-start.4
  191.9 1.0 copy-start.14
  200.7 4.9 %collective-permute-start.7 = (bf16[2,1024]{1,0:T(2,128)(2,1)S(1)}, bf16[2,1024]{1,0:T(2,128)(2,1)S(1)}, u32[]{:S(2)}, u32[]{:S(2)}) collective-permute-start(bf16[2,1024]{1,0:T(2,128)(2,1)S(1)} %bitcast.53), channel_id=1, source_target_pairs={{8,0},{16,8},{24,16},{32,24},{40,32},{48,40},{56,48},{64,56},{72,6... | collective-permute-start | bytes 12296 | tf_op jit(solution)/shard_map/ppermute | solution.py:311
Sparse Core Ops, SparseCore 0:
  20.0 94.9 all-gather.2
  152.6 42.2 reduce-scatter.1
